TPU v7x, 512 devices: a whole 4x4x16 slice. The times are simulated.
512 devices in a mesh: grp: 2 (over core), ctx: 32 (over x_lo, z), kvh: 8 (over y, x_hi).
Axes of the slice: x: 4 (x_hi: 2, x_lo: 2; x = x_hi * 2 + x_lo), y: 4, z: 16, core: 2. Of those that a mesh axis runs over, the one named last changes fastest.
Arguments:
- slab_query: bfloat16 [2, 256, 8, 12, 128], P('grp', 'ctx', 'kvh'), may hold values from -32 to 32
- kv_cache: bfloat16 [2, 2, 65536, 8, 128], P('grp', None, 'ctx', 'kvh'), may hold values from -32 to 32
- kept_list: int32 [2, 8, 384], P(None, 'kvh'), may hold values from 0 to 511, as said below
- decode_place: int32 [2, 8, 384], P(None, 'kvh'), may hold values from 0 to 31, as said below
- step_query: bfloat16 [2, 2, 8, 12, 128], P('grp', None, 'kvh'), may hold values from -32 to 32
- step_cache: bfloat16 [2, 2, 2, 8, 128], P('grp', None, None, 'kvh'), may hold values from -16 to 16
Outputs:
- slab_out: bfloat16 [2, 256, 8, 12, 128], P('grp', 'ctx', 'kvh')
- heavy_score: float32 [2, 8, 65536], P('grp', 'kvh', 'ctx')
- paged_cache: bfloat16 [2, 8, 2, 384, 128, 128], P('grp', 'kvh', None, 'ctx')
- step_out: bfloat16 [2, 2, 8, 12, 128], P('grp', None, 'kvh')
Inputs may be any that keep to these rules, and one draw needn't show every extreme that they name: `kept_list`: for each sequence and KV head, 384 different block numbers in increasing order; the last 16 blocks of the sequence are always among them. `decode_place`: entry i is the index along ctx of the decode device of block kept_list[., ., i]; in each aligned run of 32 entries (r * 32 to r * 32 + 31) every decode device appears exactly once; the kept blocks of one head that lie on one prefill device go to different decode devices.
All inputs are finite; a program needn't handle non-finite values.
Results may differ from a plain program's by a relative error of at most 0.0075.
Values may be sent and summed in bfloat16 or wider, within the bound.
No kernel may reach another device: no remote copies, remote signals or barrier semaphores. Data moves between devices by JAX's collectives and lax.ppermute only.
A program may use at most 64 MiB of HBM per device.

v0:
```python
import math

import jax
import jax.numpy as jnp
from jax import lax
from jax.sharding import PartitionSpec as P

BLK = 128


def from_partner(array, axis, apart):
    return lax.ppermute(array, axis, [(i, i ^ 1 << apart) for i in range(lax.axis_size(axis))])


def merged(array, axis, combine):
    everything = jax.tree.map(lambda part: lax.all_gather(part, axis), array)
    initial = jax.tree.map(lambda part: part[0], everything)

    def hop(k, so_far):
        return combine(so_far, jax.tree.map(lambda part: part[k], everything))

    return lax.fori_loop(1, lax.axis_size(axis), hop, initial)


def join_parts(first_part, second_part):
    row_top = jnp.maximum(first_part[0], second_part[0])
    left_scale = jnp.exp(first_part[0] - row_top)
    right_scale = jnp.exp(second_part[0] - row_top)
    return (row_top, first_part[1] * left_scale + second_part[1] * right_scale)


def join_steps(first_part, second_part):
    row_top = jnp.maximum(first_part[0], second_part[0])
    left_scale = jnp.exp(first_part[0] - row_top)
    right_scale = jnp.exp(second_part[0] - row_top)
    row_mass = first_part[1] * left_scale + second_part[1] * right_scale
    accumulated = first_part[2] * left_scale[..., None] + second_part[2] * right_scale[..., None]
    return (row_top, row_mass, accumulated)


def slot_lanes(block_list, place_map, ctx_pos, ctx_count, per_dev):
    heads_dev = block_list.shape[0]
    slot_count = block_list.shape[1] // ctx_count
    lane_ids = jnp.arange(ctx_count, dtype=jnp.int32)
    here_mask = place_map.reshape(heads_dev, slot_count, ctx_count) == ctx_pos
    column_ids = jnp.sum(jnp.where(here_mask, lane_ids, 0), axis=2)
    entry_index = jnp.arange(slot_count, dtype=jnp.int32)[None, :] * ctx_count + column_ids
    return jnp.take_along_axis(block_list, entry_index, axis=1) // per_dev


def slab_stats(row_sets, pos_sets, key_set, key_pos, score_scale):

    def one_block(inputs):
        scores = (
            jnp.einsum("rd,kd->rk", inputs[0], key_set, preferred_element_type=jnp.float32)
            * score_scale
        )
        seen_mask = key_pos[None, :] <= inputs[1][:, None]
        row_top = jnp.max(jnp.where(seen_mask, scores, -jnp.inf), axis=1)
        row_mass = jnp.sum(jnp.where(seen_mask, jnp.exp(scores - row_top[:, None]), 0.0), axis=1)
        return (row_top, row_mass)

    row_top, row_mass = lax.map(one_block, (row_sets, pos_sets))
    return (row_top.reshape(-1), row_mass.reshape(-1))


def slab_final(row_sets, pos_sets, peak_sets, total_sets, key_set, value_set, key_pos, score_scale):

    def one_block(column, inputs):
        row_set, pos_set, row_peak, row_total = inputs
        scores = (
            jnp.einsum("rd,kd->rk", row_set, key_set, preferred_element_type=jnp.float32)
            * score_scale
        )
        seen_mask = key_pos[None, :] <= pos_set[:, None]
        weight = jnp.where(seen_mask, jnp.exp(scores - row_peak[:, None]) / row_total[:, None], 0.0)
        term_rows = jnp.dot(
            weight.astype(jnp.bfloat16), value_set, preferred_element_type=jnp.float32
        )
        return (column + jnp.sum(weight, axis=0), term_rows)

    return lax.scan(
        one_block,
        jnp.zeros((key_set.shape[0],), jnp.float32),
        (row_sets, pos_sets, peak_sets, total_sets),
    )


def cache_partial(query_rows, key_rows, value_rows, score_scale):
    scores = (
        jnp.einsum("rd,kd->rk", query_rows, key_rows, preferred_element_type=jnp.float32)
        * score_scale
    )
    row_top = jnp.max(scores, axis=1)
    weight = jnp.exp(scores - row_top[:, None])
    accumulated = jnp.dot(weight, value_rows.astype(jnp.float32), precision=lax.Precision.HIGHEST)
    return (row_top, jnp.sum(weight, axis=1), accumulated)


def fresh_partial(query_rows, new_keys, new_values, visible, score_scale):
    scores = (
        jnp.einsum("rd,kd->rk", query_rows, new_keys, preferred_element_type=jnp.float32)
        * score_scale
    )
    row_top = jnp.max(jnp.where(visible, scores, -jnp.inf), axis=1)
    weight = jnp.where(visible, jnp.exp(scores - row_top[:, None]), 0.0)
    accumulated = jnp.dot(weight, new_values.astype(jnp.float32), precision=lax.Precision.HIGHEST)
    return (row_top, jnp.sum(weight, axis=1), accumulated)


def local(slab_query, kv_cache, kept_list, decode_place, step_query, step_cache):
    ctx_count = lax.axis_size("ctx")
    ctx_pos = lax.axis_index("ctx")
    group_index = lax.axis_index("grp")
    span_rows = slab_query.shape[1]
    heads_dev = slab_query.shape[2]
    group_q = slab_query.shape[3]
    head_dim = slab_query.shape[4]
    ctx_len = kv_cache.shape[2]
    step_count = step_query.shape[1]
    slab_rows = span_rows * ctx_count
    total_len = ctx_len * ctx_count
    per_dev = ctx_len // BLK
    keep_count = kept_list.shape[2]
    slot_count = keep_count // ctx_count
    score_scale = 1.0 / math.sqrt(head_dim)
    lane_ids = jnp.arange(ctx_count, dtype=jnp.int32)
    own_list = lax.dynamic_index_in_dim(kept_list, group_index, 0, keepdims=False)
    own_place = lax.dynamic_index_in_dim(decode_place, group_index, 0, keepdims=False)
    local_first = ctx_pos * per_dev
    mine_mask = own_list // per_dev == ctx_pos
    hit_mask = mine_mask[:, None, :] & (own_place[:, None, :] == lane_ids[None, :, None])
    pick_index = jnp.sum(jnp.where(hit_mask, own_list[:, None, :] - local_first, 0), axis=2)
    sent_mask = jnp.any(hit_mask, axis=2)
    cache_blocks = kv_cache[0].reshape(2, per_dev, BLK, heads_dev, head_dim)
    outgoing = jnp.stack([jnp.take(cache_blocks[:, :, :, 0], pick_index[0], axis=1)], axis=0)
    outgoing = jnp.where(sent_mask[:, None, :, None, None], outgoing, jnp.zeros((), jnp.bfloat16))
    arrived = lax.all_to_all(outgoing, "ctx", split_axis=2, concat_axis=2, tiled=True)
    arrived = from_partner(arrived, "grp", 0)
    other_list = lax.dynamic_index_in_dim(kept_list, 1 - group_index, 0, keepdims=False)
    other_place = lax.dynamic_index_in_dim(decode_place, 1 - group_index, 0, keepdims=False)
    source = slot_lanes(other_list, other_place, ctx_pos, ctx_count, per_dev)
    paged = jnp.stack([jnp.take(arrived[0], source[0], axis=1)], axis=0)
    row_step = jnp.arange(step_count * group_q, dtype=jnp.int32) // group_q
    visible = jnp.arange(step_count, dtype=jnp.int32)[None, :] <= row_step[:, None]
    head_index = 0
    query_rows = step_query[0, :, head_index].reshape(step_count * group_q, head_dim)
    key_rows = paged[head_index, 0].reshape(slot_count * BLK, head_dim)
    value_rows = paged[head_index, 1].reshape(slot_count * BLK, head_dim)
    cache_parts = [cache_partial(query_rows, key_rows, value_rows, score_scale)]
    fresh_parts = [
        fresh_partial(
            query_rows,
            step_cache[0, 0, :, head_index],
            step_cache[0, 1, :, head_index],
            visible,
            score_scale,
        )
    ]
    step_top = jnp.stack([item[0] for item in cache_parts], axis=0)
    step_mass = jnp.stack([item[1] for item in cache_parts], axis=0)
    step_accum = jnp.stack([item[2] for item in cache_parts], axis=0)
    fresh_state = (
        jnp.stack([item[0] for item in fresh_parts], axis=0),
        jnp.stack([item[1] for item in fresh_parts], axis=0),
        jnp.stack([item[2] for item in fresh_parts], axis=0),
    )
    gathered = lax.all_gather(slab_query, "ctx", axis=1, tiled=True)
    rows_all = slab_rows * group_q
    row_block = math.gcd(rows_all, 512)
    count_blocks = rows_all // row_block
    row_pos = (total_len - slab_rows + jnp.arange(rows_all, dtype=jnp.int32) // group_q).reshape(
        count_blocks, row_block
    )
    key_pos = ctx_pos * ctx_len + jnp.arange(ctx_len, dtype=jnp.int32)
    row_sets = [gathered[0, :, 0].reshape(count_blocks, row_block, head_dim)]
    key_sets = [kv_cache[0, 0, :, 0]]
    value_sets = [kv_cache[0, 1, :, 0]]
    stat_pairs = [slab_stats(row_sets[0], row_pos, key_sets[0], key_pos, score_scale)]
    local_top = jnp.stack([item[0] for item in stat_pairs], axis=0)
    local_mass = jnp.stack([item[1] for item in stat_pairs], axis=0)
    row_peak, row_total = merged((local_top, local_mass), "ctx", join_parts)
    step_state = merged((step_top, step_mass, step_accum), "ctx", join_steps)
    head_index = 0
    column, terms = slab_final(
        row_sets[head_index],
        row_pos,
        row_peak[head_index].reshape(count_blocks, row_block),
        row_total[head_index].reshape(count_blocks, row_block),
        key_sets[head_index],
        value_sets[head_index],
        key_pos,
        score_scale,
    )
    column_parts = [column * (total_len / (group_q * slab_rows))]
    term_parts = [terms.reshape(slab_rows, group_q, head_dim)]
    slab_terms = jnp.stack(term_parts, axis=1)
    slab_out = lax.psum_scatter(slab_terms, "ctx", scatter_dimension=0, tiled=True).astype(
        jnp.bfloat16
    )[None]
    heavy = jnp.stack(column_parts, axis=0)[None]
    final_state = join_steps(step_state, fresh_state)
    step_rows = (final_state[2] / final_state[1][..., None]).astype(jnp.bfloat16)
    step_out = jnp.moveaxis(step_rows.reshape(heads_dev, step_count, group_q, head_dim), 0, 1)[None]
    return (slab_out, heavy, paged[None], step_out)


def solution(mesh):
    return jax.shard_map(
        local,
        mesh=mesh,
        in_specs=(
            P("grp", "ctx", "kvh", None, None),
            P("grp", None, "ctx", "kvh", None),
            P(None, "kvh", None),
            P(None, "kvh", None),
            P("grp", None, "kvh", None, None),
            P("grp", None, None, "kvh", None),
        ),
        out_specs=(
            P("grp", "ctx", "kvh", None, None),
            P("grp", "kvh", "ctx"),
            P("grp", "kvh", None, "ctx", None, None),
            P("grp", None, "kvh", None, None),
        ),
        check_vma=False,
    )
```

profile of v0, /device:TPU:24, one launch (start us, length us, event | category | flops | bytes accessed | tf_op | source)
XLA Modules:
  0.0 625.2 jit_solution(1634445004184950240)
XLA Ops:
  7.2 0.7 compare_reduce_fusion
  7.9 0.7 dynamic-slice_reduce_fusion.1
  8.9 3.4 gather_fusion.1
  12.3 3.3 fusion.32
  15.6 16.7 %all-to-all-start = ((bf16[1,2,32,128,128]{4,3,1,0,2:T(8,128)(2,1)}), bf16[1,2,32,128,128]{4,3,1,0,2:T(8,128)(2,1)}, u32[]{:S(2)}, u32[]{:S(2)}) async-start(bf16[1,2,32,128,128]{4,3,1,0,2:T(8,128)(2,1)} %fusion.32), calls=%async_computation.1 | async-start | bytes 4194304 | tf_op jit(solution)/shard_map/all_to_all | solution.py:138
  32.4 0.9 slice_bitcast_fusion
  33.3 151.0 %all_gather.18 = bf16[1,256,1,12,128]{4,1,3,2,0:T(8,128)(2,1)S(1)} all-gather(bf16[1,8,1,12,128]{4,1,3,2,0:T(8,128)(2,1)S(1)} %copy-done.1), channel_id=1, replica_groups=mesh['grp'=2,'ctx'=32,'kvh'=8] {'ctx'}, dimensions={1}, use_global_device_ids=true | all-gather | bytes 811008 | tf_op jit(solution)/shard_map/all_gather | solution.py:168
  184.3 0.5 copy.40
  184.9 1.1 reshape_squeeze.18
  185.9 19.6 %while.64 = (s32[]{:T(128)}, f32[6,512]{1,0:T(8,128)S(1)}, f32[6,512]{1,0:T(8,128)S(1)}, s32[6,512]{1,0:T(8,128)S(1)}, bf16[6,512,128]{2,1,0:T(8,128)(2,1)}, /*i...) while((s32[]{:T(128)}, f32[6,512]{1,0:T(8,128)S(1)}, f32[6,512]{1,0:T(8,128)S(1)}, ...), condition=%wide.region_3.4_spmd.clone, body=%wide.region_0.3_spmd.clone.sunk | while | flops 277873664 | bytes 9091193 | solution.py:63
  185.9 2.0 fusion.87
  187.9 1.1 fusion.88
  189.2 2.0 fusion.87
  191.2 1.1 fusion.88
  192.5 2.0 fusion.87
  194.4 1.1 fusion.88
  195.7 2.0 fusion.87
  197.7 1.1 fusion.88
  199.0 2.0 fusion.87
  201.0 1.1 fusion.88
  202.3 2.0 fusion.87
  204.3 1.1 fusion.88
  205.6 60.5 %all_gather.19 = f32[32,1,3072]{2,1,0:T(1,128)S(1)} all-gather(f32[1,1,3072]{2,1,0:T(1,128)S(1)} %all_gather_stack_reshape.6), channel_id=1, replica_groups=mesh['grp'=2,'ctx'=32,'kvh'=8] {'ctx'}, dimensions={0}, use_global_device_ids=true | all-gather | bytes 405504 | tf_op jit(solution)/shard_map/all_gather | solution.py:16
  266.1 62.5 %all_gather.20 = f32[32,1,3072]{2,1,0:T(1,128)S(1)} all-gather(f32[1,1,3072]{2,1,0:T(1,128)S(1)} %all_gather_stack_reshape.7), channel_id=1, replica_groups=mesh['grp'=2,'ctx'=32,'kvh'=8] {'ctx'}, dimensions={0}, use_global_device_ids=true | all-gather | bytes 405504 | tf_op jit(solution)/shard_map/all_gather | solution.py:16
  328.6 2.3 while.62
  330.9 0.5 broadcast.674
  331.4 0.7 reduce.22
  332.1 0.7 reduce.21
  332.8 20.2 %while.65 = (s32[]{:T(128)}, f32[2048]{0:T(1024)S(1)}, f32[6,512,128]{2,1,0:T(8,128)S(1)}, s32[6,512]{1,0:T(8,128)S(1)}, bf16[6,512,128]{2,1,0:T(8,128)(2,1)}, /...) while((s32[]{:T(128)}, f32[2048]{0:T(1024)S(1)}, ...), condition=%wide.region_8.9_spmd.clone, body=%wide.region_6.8_spmd.clone.sunk | while | flops 544215040 | bytes 5703835 | solution.py:82
  332.9 2.6 fusion.92
  335.4 0.7 fusion.93
  336.2 2.6 fusion.92
  338.8 0.7 fusion.93
  339.6 2.6 fusion.92
  342.2 0.7 fusion.93
  342.9 2.6 fusion.92
  345.5 0.7 fusion.93
  346.3 2.6 fusion.92
  348.9 0.7 fusion.93
  349.7 2.6 fusion.92
  352.2 0.7 fusion.93
  353.0 1.4 stack_reshape.3
  354.5 1.8 copy.42
  356.3 1.9 collective-permute-start
  358.4 1.3 dynamic-slice
  360.4 0.7 gather_fusion
  361.2 0.1 select_reduce_fusion.2
  361.3 0.6 broadcast_multiply_fusion
  361.9 121.6 %reduce-scatter.2.cloned.1.call-done = f32[8,1,12,128]{3,2,0,1:T(8,128)} async-done(((f32[256,1,12,128]{3,2,0,1:T(8,128)}), f32[8,1,12,128]{3,2,0,1:T(8,128)}) %reduce-scatter.2.cloned.1.call-update) | async-done | bytes 49168 | tf_op jit(solution)/shard_map/reduce_scatter | solution.py:198
  483.6 0.8 convert_bitcast_fusion
  484.4 0.6 copy.47
  485.0 2.3 gather_fusion.2
  487.3 0.1 bitcast_select_fusion.2
  487.7 0.4 fusion.61
  488.1 0.2 fusion.38
  488.4 0.2 dynamic-update-slice
  488.6 0.2 dynamic-update-slice.1
  488.8 62.4 %all-reduce.2 = (f32[768]{0:T(1024)S(1)}, f32[768]{0:T(1024)S(1)}) all-reduce(f32[768]{0:T(1024)S(1)} %dynamic-update-slice, f32[768]{0:T(1024)S(1)} %dynamic-update-slice.1), channel_id=2, replica_groups=mesh['grp'=2,'ctx'=32,'kvh'=8] {'ctx'}, use_global_device_ids=true, to_apply=%add | all-reduce | flops 1536 | bytes 12288
  551.4 1.0 copy.48
  552.4 0.3 fusion.37
  552.7 61.1 %all-gather.2 = f32[768,128]{1,0:T(8,128)S(1)} all-gather(f32[24,128]{1,0:T(8,128)S(1)} %fusion.37), channel_id=4, replica_groups=mesh['grp'=2,'ctx'=32,'kvh'=8] {'ctx'}, dimensions={0}, use_global_device_ids=true | all-gather | bytes 405504 | tf_op jit(solution)/shard_map/all_gather | solution.py:16
  613.8 3.8 while.63
  617.5 0.2 fusion.36
  617.8 0.6 copy.49
  (256 shorter events, 7.5 us)
Async XLA Ops:
  12.3 20.1 %copy-start = (bf16[1,2,2048,1,128]{4,2,3,1,0:T(8,128)(2,1)S(1)}, bf16[1,2,2048,1,128]{4,2,3,1,0:T(8,128)(2,1)}, u32[]{:S(2)}) copy-start(bf16[1,2,2048,1,128]{4,2,3,1,0:T(8,128)(2,1)} %param.15) | copy-start | bytes 3145732
  15.6 17.7 %copy-start.1 = (bf16[1,8,1,12,128]{4,1,3,2,0:T(8,128)(2,1)S(1)}, bf16[1,8,1,12,128]{4,1,3,2,0:T(8,128)(2,1)}, u32[]{:S(2)}) copy-start(bf16[1,8,1,12,128]{4,1,3,2,0:T(8,128)(2,1)} %param.14) | copy-start | bytes 73732
  15.6 338.8 %all-to-all-start = ((bf16[1,2,32,128,128]{4,3,1,0,2:T(8,128)(2,1)}), bf16[1,2,32,128,128]{4,3,1,0,2:T(8,128)(2,1)}, u32[]{:S(2)}, u32[]{:S(2)}) async-start(bf16[1,2,32,128,128]{4,3,1,0,2:T(8,128)(2,1)} %fusion.32), calls=%async_computation.1 | async-start | bytes 4194304 | tf_op jit(solution)/shard_map/all_to_all | solution.py:138
  32.3 451.3 %reduce-scatter.2.cloned.1.call-start = ((), (), s32[]{:S(2)}) async-start(), calls=%async_computation.2 | async-start | bytes 2162688 | tf_op jit(solution)/shard_map/reduce_scatter | solution.py:198
  353.0 5.3 copy-start.3
  353.0 5.4 copy-start.2
  354.4 6.7 %copy-start.4 = (bf16[1,2,2,1,128]{4,2,3,1,0:T(2,128)(2,1)S(1)}, bf16[1,2,2,1,128]{4,2,3,1,0:T(2,128)(2,1)}, u32[]{:S(2)}) copy-start(bf16[1,2,2,1,128]{4,2,3,1,0:T(2,128)(2,1)} %param.19) | copy-start | bytes 3076
  356.3 128.8 %collective-permute-start = (bf16[1,2,32,128,128]{4,3,2,1,0:T(8,128)(2,1)S(1)}, bf16[1,2,32,128,128]{4,3,2,1,0:T(8,128)(2,1)}, u32[]{:S(2)}, u32[]{:S(2)}) collective-permute-start(bf16[1,2,32,128,128]{4,3,2,1,0:T(8,128)(2,1)S(1)} %copy.42), channel_id=1, source_target_pairs={{0,256},{256,0},{1,257},{257,1},{2,258},{258,2},{3,259},{259,3},{4... | collective-permute-start | bytes 6291464 | tf_op jit(solution)/shard_map/ppermute | solution.py:12
Sparse Core Ops, SparseCore 0:
  354.6 128.9 reduce-scatter.1
where the time goes:
time: 627 us; the launch traced here: 625 us
  blocking collectives  397 us (63%)
  waiting for transfers between devices  122 us (19%)
  matrix products  32.6 us (5%)
  other arithmetic  20.6 us (3%)
  starting transfers between devices  18.6 us (3%)
  local copies, waits for them, and re-layouts  17.9 us (3%)
  between operations  15 us (2%)
    all_gather x3, blocking collectives, merged(): everything = jax.tree.map(lambda part: lax.all_gather(part, axis), array)  184 us
    all_gather x1, blocking collectives, local(): gathered = lax.all_gather(slab_query, 'ctx', axis=1, tiled=True)  151 us
    reduce_scatter x1, waiting for transfers between devices, local(): lax.psum_scatter(slab_terms, 'ctx', scatter_dimension=0, tiled=True)  122 us
    unnamed x1, blocking collectives  62.4 us
    all_to_all x1, starting transfers between devices, local(): lax.all_to_all(outgoing, 'ctx', split_axis=2, concat_axis=2, tiled=True)  16.7 us
    dot_general x6, matrix products, one_block(): jnp.einsum('rd,kd->rk', row_set, key_set, preferred_element_type=jnp.floa...  15.3 us
  transfers between devices with their start and end apart: 3, of which 1 were waited for; matrix products, arithmetic and copies ran while one was open for 9% of the time, Pallas kernels for 0%

commit v1 on v0

v1 whole, which is shorter than its diff:
```python
import math

import jax
import jax.numpy as jnp
from jax import lax
from jax.experimental import pallas as pl
from jax.experimental.pallas import tpu as pltpu
from jax.sharding import Mesh
from jax.sharding import PartitionSpec as P

BLK = 128
HD = 128
NZ = 16
NCTX = 32
ROWS = 96
HALF = NZ * ROWS
CTXL = 2048
SLAB = 256
RB = 384
NRB = HALF // RB
PER = RB // ROWS
SLOTS = 12
STEPR = 24
NEG = -1e30
C2 = math.log2(math.e) / math.sqrt(HD)
BF = jnp.bfloat16
F32 = jnp.float32

STAT = 3 * NZ
DEC = 32
XROWS = HALF + STAT + DEC
ZROWS = ROWS + STAT + DEC


def params(mib=40):
    return pltpu.CompilerParams(vmem_limit_bytes=mib * 1024 * 1024)


def parts_of(x):
    hi = x.astype(BF).astype(F32)
    mid = (x - hi).astype(BF).astype(F32)
    return hi, mid, x - hi - mid


def column(row):
    return jnp.broadcast_to(row, (128, 128)).T


def scores_t(k, q):
    return lax.dot_general(k, q, (((1,), (1,)), ((), ())), preferred_element_type=F32)


def mask_tail(info_ref, i, s_ref):
    @pl.when(info_ref[0] == NCTX - 1)
    def _():
        tail = s_ref[CTXL - SLAB :, :]
        key = lax.broadcasted_iota(jnp.int32, tail.shape, 0)
        row = lax.broadcasted_iota(jnp.int32, tail.shape, 1) + i * RB
        token = info_ref[1] * (SLAB // 2) + (row // ROWS) * 8 + row % 8
        s_ref[CTXL - SLAB :, :] = jnp.where(key <= token, tail, NEG)


def fill_vt(v, vt_ref):
    vt_ref[0:HD, :] = v.astype(F32).T.astype(BF)
    vt_ref[HD:, :] = jnp.ones((16, CTXL), BF)


def flash_kernel(info_ref, q_ref, k_ref, v_ref, d_ref, x_ref, vt_ref, s_ref, lse_ref):
    i = pl.program_id(0)

    @pl.when(i == 0)
    def _():
        fill_vt(v_ref[0], vt_ref)
        lse_ref[...] = jnp.zeros_like(lse_ref)

    s_ref[...] = scores_t(k_ref[0], q_ref[...])
    mask_tail(info_ref, i, s_ref)
    top = jnp.max(s_ref[...], axis=0, keepdims=True)
    p = jnp.exp2((s_ref[...] - top) * C2).astype(BF)
    acc = jnp.dot(vt_ref[...], p, preferred_element_type=F32)
    mass = acc[HD : HD + 1]
    x_ref[pl.ds(pl.multiple_of(i * RB, RB), RB), :] = (acc[0:HD] * (1.0 / mass)).T.astype(BF)
    lse = top * C2 + jnp.log2(mass)
    for j in range(PER):
        lse_ref[pl.ds(i * PER + j, 1), 0:ROWS] = lse[:, j * ROWS : (j + 1) * ROWS]

    @pl.when(i == NRB - 1)
    def _():
        for n, part in enumerate(parts_of(lse_ref[...])):
            x_ref[HALF + n * NZ : HALF + (n + 1) * NZ, :] = part.astype(BF)
        x_ref[HALF + STAT :, :] = d_ref[...]


def flash(info, q, kv, dec):
    return pl.pallas_call(
        flash_kernel,
        out_shape=jax.ShapeDtypeStruct((XROWS, HD), BF),
        grid=(NRB,),
        in_specs=[
            pl.BlockSpec(memory_space=pltpu.SMEM),
            pl.BlockSpec((RB, HD), lambda i: (i, 0)),
            pl.BlockSpec((1, CTXL, HD), lambda i: (0, 0, 0)),
            pl.BlockSpec((1, CTXL, HD), lambda i: (1, 0, 0)),
            pl.BlockSpec((DEC, HD), lambda i: (0, 0)),
        ],
        out_specs=pl.BlockSpec((XROWS, HD), lambda i: (0, 0)),
        scratch_shapes=[
            pltpu.VMEM((HD + 16, CTXL), BF),
            pltpu.VMEM((CTXL, RB), F32),
            pltpu.VMEM((NZ, HD), F32),
        ],
        compiler_params=params(),
        cost_estimate=pl.CostEstimate(
            flops=4 * HALF * CTXL * HD, bytes_accessed=2 * CTXL * HD * 2, transcendentals=HALF * CTXL
        ),
        name="slab_partial",
    )(info, q, kv, kv, dec)


def decode_kernel(flag_ref, q_ref, k_ref, v_ref, d_ref, vt_ref, s_ref, t_ref):
    fill_vt(v_ref[0], vt_ref)
    for b in range(CTXL // BLK):
        s = scores_t(k_ref[0, b * BLK : (b + 1) * BLK, :], q_ref[...])
        kept = jnp.broadcast_to(flag_ref[b], s.shape) > 0
        s_ref[b * BLK : (b + 1) * BLK, :] = jnp.where(kept, s, NEG)
    top = jnp.max(s_ref[...], axis=0, keepdims=True)
    p = jnp.exp2((s_ref[...] - top) * C2).astype(BF)
    acc = jnp.dot(vt_ref[...], p, preferred_element_type=F32)
    mass = acc[HD : HD + 1]
    out = (acc[0:HD] * (1.0 / mass)).T
    lse = jnp.maximum(top * C2 + jnp.log2(mass), NEG)
    put_decode(t_ref, out[0:STEPR], lse, d_ref)


def put_decode(t_ref, out, lse, d_ref):
    t_ref[...] = jnp.zeros_like(t_ref)
    t_ref[0:STEPR, :] = out
    for n, part in enumerate(parts_of(lse)):
        t_ref[STEPR + n : STEPR + n + 1, :] = part
    d_ref[...] = t_ref[...].astype(BF)


def decode_partial(flags, q, kv):
    return pl.pallas_call(
        decode_kernel,
        out_shape=jax.ShapeDtypeStruct((DEC, HD), BF),
        grid=(1,),
        in_specs=[
            pl.BlockSpec(memory_space=pltpu.SMEM),
            pl.BlockSpec((HD, HD), lambda i: (0, 0)),
            pl.BlockSpec((1, CTXL, HD), lambda i: (0, 0, 0)),
            pl.BlockSpec((1, CTXL, HD), lambda i: (1, 0, 0)),
        ],
        out_specs=pl.BlockSpec((DEC, HD), lambda i: (0, 0)),
        scratch_shapes=[
            pltpu.VMEM((HD + 16, CTXL), BF),
            pltpu.VMEM((CTXL, HD), F32),
            pltpu.VMEM((DEC, HD), F32),
        ],
        compiler_params=params(),
        name="decode_partial",
    )(flags, q, kv, kv)


def stats_of(x):
    return x[0:NZ].astype(F32) + x[NZ : 2 * NZ].astype(F32) + x[2 * NZ : 3 * NZ].astype(F32)


def dec_of(x):
    d = x.astype(F32)
    return d[0:STEPR], d[STEPR : STEPR + 1] + d[STEPR + 1 : STEPR + 2] + d[STEPR + 2 : STEPR + 3]


def merge_weights(lses):
    top = lses[0]
    for x in lses[1:]:
        top = jnp.maximum(top, x)
    es = [jnp.exp2(x - top) for x in lses]
    den = es[0]
    for e in es[1:]:
        den = den + e
    inv = 1.0 / den
    return [e * inv for e in es], top + jnp.log2(den)


def pair_kernel(a_ref, b_ref, z_ref, t_ref):
    la = stats_of(a_ref[HALF : HALF + STAT, :])
    lb = stats_of(b_ref[HALF : HALF + STAT, :])
    (wa, wb), lse = merge_weights([la, lb])
    da, sa = dec_of(a_ref[HALF + STAT :, :])
    db, sb = dec_of(b_ref[HALF + STAT :, :])
    (ua, ub), sd = merge_weights([sa, sb])
    put_decode(t_ref.at[0:DEC], da * column(ua)[0:STEPR] + db * column(ub)[0:STEPR], sd, z_ref.at[0, ROWS + STAT :, :])
    hi, mid, lo = parts_of(lse)
    stat = jnp.concatenate([hi, mid, lo], axis=0).astype(BF)
    dec = z_ref[0, ROWS + STAT :, :]
    for n in range(NZ):
        rows = slice(n * ROWS, (n + 1) * ROWS)
        wide_a = column(wa[n : n + 1])[0:ROWS]
        wide_b = column(wb[n : n + 1])[0:ROWS]
        z_ref[n, 0:ROWS, :] = (a_ref[rows, :].astype(F32) * wide_a + b_ref[rows, :].astype(F32) * wide_b).astype(BF)
        z_ref[n, ROWS : ROWS + STAT, :] = stat
        z_ref[n, ROWS + STAT :, :] = dec


def pair_merge(a, b):
    return pl.pallas_call(
        pair_kernel,
        out_shape=jax.ShapeDtypeStruct((NZ, ZROWS, HD), BF),
        scratch_shapes=[pltpu.VMEM((DEC, HD), F32)],
        compiler_params=params(),
        name="pair_merge",
    )(a, b)


def final_kernel(info_ref, r_ref, q_ref, nk_ref, nv_ref, slab_ref, lse_ref, step_ref, w_ref):
    ws, lse = merge_weights([stats_of(r_ref[s, ROWS : ROWS + STAT, :]) for s in range(NZ)])
    lse_ref[...] = lse
    for s in range(NZ):
        w_ref[s] = ws[s]
    z = info_ref[2]
    total = jnp.zeros((ROWS, HD), F32)
    for s in range(NZ):
        wide = column(w_ref[s, pl.ds(z, 1), :])[0:ROWS]
        total = total + r_ref[s, 0:ROWS, :].astype(F32) * wide
    slab_ref[...] = total.astype(BF)
    decs = [dec_of(r_ref[s, ROWS + STAT :, :]) for s in range(NZ)]
    fresh = scores_t(nk_ref[...], q_ref[...]) * C2
    lane = lax.broadcasted_iota(jnp.int32, (1, HD), 1)
    first = fresh[0:1]
    second = jnp.where(lane % 2 == 1, fresh[1:2], NEG)
    us, _ = merge_weights([d[1] for d in decs] + [first, second])
    nv = nv_ref[...].astype(F32)
    out = column(us[NZ])[0:STEPR] * nv[0:1] + column(us[NZ + 1])[0:STEPR] * nv[1:2]
    for s in range(NZ):
        out = out + decs[s][0] * column(us[s])[0:STEPR]
    step_ref[...] = out.astype(BF)


def final_merge(info, r, q, nk, nv):
    return pl.pallas_call(
        final_kernel,
        out_shape=(
            jax.ShapeDtypeStruct((ROWS, HD), BF),
            jax.ShapeDtypeStruct((NZ, HD), F32),
            jax.ShapeDtypeStruct((STEPR, HD), BF),
        ),
        in_specs=[pl.BlockSpec(memory_space=pltpu.SMEM)] + [pl.BlockSpec(memory_space=pltpu.VMEM)] * 4,
        out_specs=[pl.BlockSpec(memory_space=pltpu.VMEM)] * 3,
        scratch_shapes=[pltpu.VMEM((NZ, NZ, HD), F32)],
        compiler_params=params(),
        name="final_merge",
    )(info, r, q, nk, nv)


def heavy_kernel(info_ref, q_ref, k_ref, lse_ref, prev_ref, h_ref, s_ref, acc_ref):
    i = pl.program_id(0)

    @pl.when(i == 0)
    def _():
        acc_ref[...] = jnp.zeros_like(acc_ref)

    s_ref[...] = scores_t(k_ref[0], q_ref[...])
    mask_tail(info_ref, i, s_ref)
    w = jnp.exp2(s_ref[...] * C2 - lse_ref[0])
    acc_ref[...] += w[:, 0:128] + w[:, 128:256] + w[:, 256:384]

    @pl.when(i == NRB - 1)
    def _():
        ones = jnp.ones((8, 128), F32)
        sums = lax.dot_general(
            ones, acc_ref[...], (((1,), (1,)), ((), ())), precision=lax.Precision.HIGHEST, preferred_element_type=F32
        )
        h_ref[...] = sums[0:1] * (NCTX * CTXL / (12 * SLAB)) + prev_ref[...]


def heavy(info, q, kv, lse, prev):
    return pl.pallas_call(
        heavy_kernel,
        out_shape=jax.ShapeDtypeStruct((1, CTXL), F32),
        grid=(NRB,),
        in_specs=[
            pl.BlockSpec(memory_space=pltpu.SMEM),
            pl.BlockSpec((RB, HD), lambda i: (i, 0)),
            pl.BlockSpec((1, CTXL, HD), lambda i: (0, 0, 0)),
            pl.BlockSpec((1, 1, RB), lambda i: (i, 0, 0)),
            pl.BlockSpec((1, CTXL), lambda i: (0, 0)),
        ],
        out_specs=pl.BlockSpec((1, CTXL), lambda i: (0, 0)),
        scratch_shapes=[pltpu.VMEM((CTXL, RB), F32), pltpu.VMEM((CTXL, HD), F32)],
        compiler_params=params(),
        cost_estimate=pl.CostEstimate(
            flops=2 * HALF * CTXL * HD, bytes_accessed=CTXL * HD * 2, transcendentals=HALF * CTXL
        ),
        name="heavy_columns",
    )(info, q, kv, lse, prev)


def pack_kernel(pick_ref, kv_ref, dep_ref, out_ref, sems):
    copies = [
        pltpu.make_async_copy(kv_ref.at[:, pick_ref[d]], out_ref.at[d], sems.at[d]) for d in range(NCTX)
    ]
    for copy in copies:
        copy.start()
    for copy in copies:
        copy.wait()


def pack(pick, blocks, after):
    return pl.pallas_call(
        pack_kernel,
        out_shape=jax.ShapeDtypeStruct((NCTX, 2, BLK, HD), BF),
        in_specs=[
            pl.BlockSpec(memory_space=pltpu.SMEM),
            pl.BlockSpec(memory_space=pl.ANY),
            pl.BlockSpec(memory_space=pl.ANY),
        ],
        out_specs=pl.BlockSpec(memory_space=pl.ANY),
        scratch_shapes=[pltpu.SemaphoreType.DMA((NCTX,))],
        name="pack_blocks",
    )(pick, blocks, after)


def select_kernel(src_ref, in_ref, out_ref, sems):
    copies = [
        pltpu.make_async_copy(in_ref.at[src_ref[r]], out_ref.at[:, r], sems.at[r]) for r in range(SLOTS)
    ]
    for copy in copies:
        copy.start()
    for copy in copies:
        copy.wait()


def select(source, arrived):
    return pl.pallas_call(
        select_kernel,
        out_shape=jax.ShapeDtypeStruct((2, SLOTS, BLK, HD), BF),
        in_specs=[pl.BlockSpec(memory_space=pltpu.SMEM), pl.BlockSpec(memory_space=pl.ANY)],
        out_specs=pl.BlockSpec(memory_space=pl.ANY),
        scratch_shapes=[pltpu.SemaphoreType.DMA((SLOTS,))],
        name="select_slots",
    )(source, arrived)


SWAP = [(0, 1), (1, 0)]


def local(slab_query, kv_cache, kept_list, decode_place, step_query, step_cache):
    grp = lax.axis_index("grp")
    xl = lax.axis_index("xl")
    z = lax.axis_index("z")
    ctx = xl * NZ + z
    per_dev = CTXL // BLK

    own_list = lax.dynamic_index_in_dim(kept_list, grp, 0, keepdims=False)[0]
    own_place = lax.dynamic_index_in_dim(decode_place, grp, 0, keepdims=False)[0]
    lanes = jnp.arange(NCTX, dtype=jnp.int32)
    offset = own_list - ctx * per_dev
    mine = (offset >= 0) & (offset < per_dev)
    hit = mine[None, :] & (own_place[None, :] == lanes[:, None])
    pick = jnp.clip(jnp.sum(jnp.where(hit, offset[None, :], 0), axis=1), 0, per_dev - 1)
    flags = jnp.sum(
        (offset[None, :] == jnp.arange(per_dev, dtype=jnp.int32)[:, None]).astype(jnp.int32), axis=1
    )
    here = (own_place == ctx).reshape(SLOTS, NCTX)
    source = jnp.clip(
        jnp.sum(jnp.where(here, own_list.reshape(SLOTS, NCTX) // per_dev, 0), axis=1), 0, NCTX - 1
    )
    info_own = jnp.stack([ctx, xl, z]).astype(jnp.int32)
    info_other = jnp.stack([ctx, 1 - xl, z]).astype(jnp.int32)

    q = jnp.transpose(slab_query[0, :, 0], (1, 0, 2)).reshape(ROWS, HD)
    kv = kv_cache[0, :, :, 0]
    steps = jnp.transpose(step_query[0, :, 0], (1, 0, 2)).reshape(STEPR, HD)
    steps = jnp.pad(steps, ((0, HD - STEPR), (0, 0)))
    new = jnp.pad(step_cache[0, :, :, 0], ((0, 0), (0, 14), (0, 0)))

    dec = decode_partial(flags, lax.ppermute(steps, "grp", SWAP), kv)
    dec = lax.ppermute(dec, "grp", SWAP)
    q_own = lax.all_gather(q, "z", axis=0, tiled=True)
    outgoing = pack(pick, kv.reshape(2, per_dev, BLK, HD), q_own)
    arrived = lax.all_to_all(outgoing, ("xl", "z"), 0, 0, tiled=True)

    q_other = lax.ppermute(q_own, "xl", SWAP)
    part_own = flash(info_own, q_own, kv, dec)
    part_other = flash(info_other, q_other, kv, dec)
    part_partner = lax.ppermute(part_other, "xl", SWAP)
    merged = pair_merge(part_own, part_partner)
    received = lax.all_to_all(merged, "z", 0, 0, tiled=True)
    slab, lse, step = final_merge(info_own, received, steps, new[0], new[1])
    lse_own = lse[:, 0:ROWS].reshape(NRB, 1, RB)
    lse_other = lax.ppermute(lse_own, "xl", SWAP)
    columns = heavy(info_own, q_own, kv, lse_own, jnp.zeros((1, CTXL), F32))
    columns = heavy(info_other, q_other, kv, lse_other, columns)

    paged = lax.ppermute(select(source, arrived), "grp", SWAP)

    slab_out = jnp.transpose(slab.reshape(12, 8, HD), (1, 0, 2))[None, :, None]
    step_out = jnp.transpose(step.reshape(12, 2, HD), (1, 0, 2))[None, :, None]
    return (slab_out, columns[None], paged[None, None], step_out)


def solution(mesh):
    split = Mesh(mesh.devices.reshape(2, 2, NZ, 8), ("grp", "xl", "z", "kvh"))
    ctx = ("xl", "z")
    return jax.shard_map(
        local,
        mesh=split,
        in_specs=(
            P("grp", ctx, "kvh", None, None),
            P("grp", None, ctx, "kvh", None),
            P(None, "kvh", None),
            P(None, "kvh", None),
            P("grp", None, "kvh", None, None),
            P("grp", None, None, "kvh", None),
        ),
        out_specs=(
            P("grp", ctx, "kvh", None, None),
            P("grp", "kvh", ctx),
            P("grp", "kvh", None, ctx, None, None),
            P("grp", None, "kvh", None, None),
        ),
        check_vma=False,
    )
```

time: 627 us -> 262 us (0.42)
  blocking collectives: 397 us -> 40.1 us
  Pallas kernels: 0 us -> 125 us
  waiting for transfers between devices: 122 us -> 61.6 us
  matrix products: 32.6 us -> 0 us
  other arithmetic: 20.6 us -> 2.32 us
  local copies, waits for them, and re-layouts: 17.9 us -> 1.17 us
  between operations: 15 us -> 0.84 us
  starting transfers between devices: 18.6 us -> 30.4 us
    all_gather x4 -> x1, blocking collectives: 335 us -> 40.1 us  [local(): q_own = lax.all_gather(q, 'z', axis=0, tiled=True)]
    pallas_call x0 -> x9, Pallas kernels: none -> 125 us  [the longest x1 65.6 us: pack(): pl.pallas_call(pack_kernel, out_shape=jax.ShapeDtypeStruct((NCTX, 2, BLK,...]
    reduce_scatter x1 -> x0, waiting for transfers between devices: 122 us -> none  [local(): lax.psum_scatter(slab_terms, 'ctx', scatter_dimension=0, tiled=True)]
    unnamed x1 -> x0, blocking collectives: 62.4 us -> none
    all_to_all x1 -> x2, waiting for transfers between devices: 0.01 us -> 55.4 us  [the longest x1 51.4 us: local(): arrived = lax.all_to_all(outgoing, ('xl', 'z'), 0, 0, tiled=True)]
    dot_general x22 -> x0, matrix products: 32.6 us -> none  [the longest x6 15.3 us: one_block(): jnp.einsum('rd,kd->rk', row_set, key_set, preferred_element_type=jnp.floa...]
    ppermute x1 -> x6, starting transfers between devices: 1.92 us -> 14.2 us  [the longest x1 3.63 us: local(): q_other = lax.ppermute(q_own, 'xl', SWAP)]
    reduce_sum x10 -> x3, other arithmetic: 7.12 us -> 0.36 us  [the longest x1 0.12 us: local(): jnp.sum(jnp.where(here, own_list.reshape(SLOTS, NCTX) // per_dev, 0), axi...]
  transfers between devices with their start and end apart: 3 -> 8, of which waited for: 1 -> 5; matrix products, arithmetic and copies ran while one was open for 9% -> 0% of each run, Pallas kernels for 0% -> 23%
where the time goes in v1:
time: 262 us; the launch traced here: 261 us
  Pallas kernels  125 us (48%)
  waiting for transfers between devices  61.6 us (24%)
  blocking collectives  40.1 us (15%)
  starting transfers between devices  30.4 us (12%)
    pallas_call x1, Pallas kernels, pack(): pl.pallas_call(pack_kernel, out_shape=jax.ShapeDtypeStruct((NCTX, 2, BLK,...  65.6 us
    all_to_all x1, waiting for transfers between devices, local(): arrived = lax.all_to_all(outgoing, ('xl', 'z'), 0, 0, tiled=True)  51.4 us
    all_gather x1, blocking collectives, local(): q_own = lax.all_gather(q, 'z', axis=0, tiled=True)  40.1 us
    pallas_call x1, Pallas kernels, select(): pl.pallas_call(select_kernel, out_shape=jax.ShapeDtypeStruct((2, SLOTS, B...  25.7 us
    pallas_call x2, Pallas kernels, flash(): pl.pallas_call(flash_kernel, out_shape=jax.ShapeDtypeStruct((XROWS, HD),...  17 us
    pallas_call x2, Pallas kernels, heavy(): pl.pallas_call(heavy_kernel, out_shape=jax.ShapeDtypeStruct((1, CTXL), F3...  11.8 us
    all_to_all x1, starting transfers between devices, local(): arrived = lax.all_to_all(outgoing, ('xl', 'z'), 0, 0, tiled=True)  8.17 us
    all_to_all x1, starting transfers between devices, local(): received = lax.all_to_all(merged, 'z', 0, 0, tiled=True)  7.99 us
  transfers between devices with their start and end apart: 8, of which 5 were waited for; matrix products, arithmetic and copies ran while one was open for 0% of the time, Pallas kernels for 23%

profile of v1, /device:TPU:24, one launch (start us, length us, event | category | flops | bytes accessed | tf_op | source)
XLA Modules:
  0.0 261.3 jit_solution(17572359384690449498)
XLA Ops:
  0.6 0.7 dynamic-slice_reduce_fusion.1
  1.4 0.1 select_reduce_fusion
  1.5 0.5 broadcast_clamp_fusion.pick_ref
  2.0 40.1 %all_gather.3.q_ref.dep_ref = bf16[1536,128]{1,0:T(8,128)(2,1)} all-gather(bf16[96,128]{1,0:T(8,128)(2,1)} %bitcast.45), channel_id=1, replica_groups=mesh['grp'=2,'xl'=2,'z'=16,'kvh'=8] {'z'}, dimensions={0}, use_global_device_ids=true | all-gather | bytes 417792 | tf_op jit(solution)/shard_map/all_gather | solution.py:380
  42.1 65.6 %pack_blocks.1 = bf16[32,2,128,128]{3,2,1,0:T(8,128)(2,1)} custom-call(s32[32]{0:T(128)} %broadcast_clamp_fusion.pick_ref, bf16[2,16,128,128]{3,2,1,0:T(8,128)(2,1)} %bitcast.34, bf16[1536,128]{1,0:T(8,128)(2,1)} %all_gather.3.q_ref.dep_ref), custom_call_target="tpu_custom_call" | custom-call | tf_op jit(solution)/shard_map/pack_blocks/pallas_call | solution.py:310
  107.7 0.0 copy-start.1
  107.7 0.0 copy-start.2
  107.7 0.0 copy-start
  107.7 8.2 %all-to-all-start.1 = ((bf16[32,2,128,128]{3,2,1,0:T(8,128)(2,1)}), bf16[32,2,128,128]{3,2,1,0:T(8,128)(2,1)}, u32[]{:S(2)}, u32[]{:S(2)}) async-start(bf16[32,2,128,128]{3,2,1,0:T(8,128)(2,1)} %pack_blocks.1), calls=%async_computation.1 | async-start | bytes 4194304 | tf_op jit(solution)/shard_map/all_to_all | solution.py:382
  115.9 0.0 copy-done.1
  115.9 3.6 %collective-permute-start.2 = (bf16[1536,128]{1,0:T(8,128)(2,1)S(1)}, bf16[1536,128]{1,0:T(8,128)(2,1)S(1)}, u32[]{:S(2)}, u32[]{:S(2)}) collective-permute-start(bf16[1536,128]{1,0:T(8,128)(2,1)S(1)} %copy-done.1), channel_id=1, source_target_pairs={{0,128},{128,0},{1,129},{129,1},{2,130},{130,2},{3,131},{131,3},{4... | collective-permute-start | bytes 1179656 | tf_op jit(solution)/shard_map/ppermute | solution.py:384
  119.6 0.0 copy-done.2
  119.6 1.9 collective-permute-start
  121.5 0.1 convert_reduce_fusion.flag_ref
  121.6 1.1 collective-permute-done.q_ref
  122.7 0.0 copy-done
  122.7 1.5 decode_partial.1
  124.2 2.1 collective-permute-start.1
  126.3 0.1 add_add_fusion.1.info_ref
  126.4 0.9 collective-permute-done.1.d_ref
  127.3 0.0 collective-permute-done.2.q_ref
  127.3 8.5 %slab_partial.3 = bf16[1616,128]{1,0:T(8,128)(2,1)S(1)} custom-call(s32[3]{0:T(128)S(1)} %add_add_fusion.1.info_ref, bf16[1536,128]{1,0:T(8,128)(2,1)S(1)} %collective-permute-done.2.q_ref, bf16[2,2048,128]{2,1,0:T(8,128)(2,1)S(1)} %bitcast.37, bf16[2,2048,128]{2,1,0:T(8,128)(2,1)S(1)} %bitcast.38, bf16[32,128]{1,0:T(8,128)(2,1)S(1)} %collective-permute-done.1.d_ref), custom_call_target="tpu_custom_call" | custom-call | flops 1610612736 | bytes 1048576 | tf_op jit(solution)/shard_map/slab_partial/pallas_call | solution.py:95
  135.8 2.7 %collective-permute-start.3 = (bf16[1616,128]{1,0:T(8,128)(2,1)S(1)}, bf16[1616,128]{1,0:T(8,128)(2,1)S(1)}, u32[]{:S(2)}, u32[]{:S(2)}) collective-permute-start(bf16[1616,128]{1,0:T(8,128)(2,1)S(1)} %slab_partial.3), channel_id=1, source_target_pairs={{0,128},{128,0},{1,129},{129,1},{2,130},{130,2},{3,131},{131,3},{4... | collective-permute-start | bytes 1241096 | tf_op jit(solution)/shard_map/ppermute | solution.py:387
  138.6 0.1 add_add_fusion.info_ref
  138.6 8.5 %slab_partial.2.a_ref = bf16[1616,128]{1,0:T(8,128)(2,1)S(1)} custom-call(s32[3]{0:T(128)S(1)} %add_add_fusion.info_ref, bf16[1536,128]{1,0:T(8,128)(2,1)S(1)} %copy-done.1, bf16[2,2048,128]{2,1,0:T(8,128)(2,1)S(1)} %bitcast.39, bf16[2,2048,128]{2,1,0:T(8,128)(2,1)S(1)} %bitcast.40, bf16[32,128]{1,0:T(8,128)(2,1)S(1)} %collective-permute-done.1.d_ref), custom_call_target="tpu_custom_call" | custom-call | flops 1610612736 | bytes 1048576 | tf_op jit(solution)/shard_map/slab_partial/pallas_call | solution.py:95
  147.1 0.0 copy-start.3
  147.1 4.2 %collective-permute-done.3.b_ref = bf16[1616,128]{1,0:T(8,128)(2,1)S(1)} collective-permute-done((bf16[1616,128]{1,0:T(8,128)(2,1)S(1)}, bf16[1616,128]{1,0:T(8,128)(2,1)S(1)}, u32[]{:S(2)}, u32[]{:S(2)}) %collective-permute-start.3) | collective-permute-done | bytes 413728 | tf_op jit(solution)/shard_map/ppermute | solution.py:387
  151.4 1.5 pair_merge.1
  152.9 0.0 copy-start.4
  152.9 51.4 %all-to-all-done.1.in_ref = bf16[32,2,128,128]{3,2,1,0:T(8,128)(2,1)} async-done(((bf16[32,2,128,128]{3,2,1,0:T(8,128)(2,1)}), bf16[32,2,128,128]{3,2,1,0:T(8,128)(2,1)}, u32[]{:S(2)}, u32[]{:S(2)}) %all-to-all-start.1) | async-done | bytes 2097184 | tf_op jit(solution)/shard_map/all_to_all | solution.py:382
  204.3 8.0 %all-to-all-start = ((bf16[16,176,128]{2,1,0:T(8,128)(2,1)}), bf16[16,176,128]{2,1,0:T(8,128)(2,1)S(1)}, u32[]{:S(2)}, u32[]{:S(2)}) async-start(bf16[16,176,128]{2,1,0:T(8,128)(2,1)} %pair_merge.1), calls=%async_computation | async-start | bytes 1441792 | tf_op jit(solution)/shard_map/all_to_all | solution.py:389
  212.3 0.0 copy-done.3
  212.3 0.1 eq.47
  212.4 0.1 reshape_squeeze.6
  212.5 0.1 fusion.3
  212.6 0.5 broadcast_clamp_fusion.1.src_ref
  213.1 25.7 %select_slots.1 = bf16[2,12,128,128]{3,2,1,0:T(8,128)(2,1)} custom-call(s32[12]{0:T(128)} %broadcast_clamp_fusion.1.src_ref, bf16[32,2,128,128]{3,2,1,0:T(8,128)(2,1)} %all-to-all-done.1.in_ref), custom_call_target="tpu_custom_call" | custom-call | tf_op jit(solution)/shard_map/select_slots/pallas_call | solution.py:335
  238.8 1.9 collective-permute-start.5
  240.8 0.0 copy-done.4
  240.8 4.0 %all-to-all-done.r_ref = bf16[16,176,128]{2,1,0:T(8,128)(2,1)S(1)} async-done(((bf16[16,176,128]{2,1,0:T(8,128)(2,1)}), bf16[16,176,128]{2,1,0:T(8,128)(2,1)S(1)}, u32[]{:S(2)}, u32[]{:S(2)}) %all-to-all-start) | async-done | bytes 720928 | tf_op jit(solution)/shard_map/all_to_all | solution.py:389
  244.8 1.8 final_merge.1
  246.6 0.1 reshape.47.lse_ref
  246.7 1.9 collective-permute-start.4
  248.6 5.6 %heavy_columns.2.prev_ref = f32[1,2048]{1,0:T(1,128)S(1)} custom-call(s32[3]{0:T(128)S(1)} %add_add_fusion.info_ref, bf16[1536,128]{1,0:T(8,128)(2,1)S(1)} %copy-done.1, bf16[2,2048,128]{2,1,0:T(8,128)(2,1)S(1)} %bitcast.41, f32[4,1,384]{2,1,0:T(1,128)S(1)} %reshape.47.lse_ref, f32[1,2048]{1,0:T(1,128)S(1)} %broadcast_in_dim.35.prev_ref), custom_call_target="tpu_custom_call" | custom-call | flops 805306368 | bytes 524288 | tf_op jit(solution)/shard_map/heavy_columns/pallas_call | solution.py:278
  254.2 0.0 collective-permute-done.4.lse_ref
  254.2 6.2 %heavy_columns.3 = f32[1,2048]{1,0:T(1,128)} custom-call(s32[3]{0:T(128)S(1)} %add_add_fusion.1.info_ref, bf16[1536,128]{1,0:T(8,128)(2,1)S(1)} %collective-permute-done.2.q_ref, bf16[2,2048,128]{2,1,0:T(8,128)(2,1)S(1)} %bitcast.42, f32[4,1,384]{2,1,0:T(1,128)S(1)} %collective-permute-done.4.lse_ref, f32[1,2048]{1,0:T(1,128)S(1)} %heavy_columns.2.prev_ref), custom_call_target="tpu_custom_call" | custom-call | flops 805306368 | bytes 524288 | tf_op jit(solution)/shard_map/heavy_columns/pallas_call | solution.py:278
  260.4 0.0 collective-permute-done.5
  260.4 0.9 copy.11
  (5 shorter events, 0.1 us)
Async XLA Ops:
  107.7 8.2 %copy-start.1 = (bf16[1536,128]{1,0:T(8,128)(2,1)S(1)}, bf16[1536,128]{1,0:T(8,128)(2,1)}, u32[]{:S(2)}) copy-start(bf16[1536,128]{1,0:T(8,128)(2,1)} %all_gather.3.q_ref.dep_ref) | copy-start | bytes 1179652
  107.7 11.9 %copy-start.2 = (bf16[1,2,1,12,128]{4,1,3,2,0:T(2,128)(2,1)S(1)}, bf16[1,2,1,12,128]{4,1,3,2,0:T(2,128)(2,1)}, u32[]{:S(2)}) copy-start(bf16[1,2,1,12,128]{4,1,3,2,0:T(2,128)(2,1)} %param.10) | copy-start | bytes 18436
  107.7 15.0 %copy-start = (bf16[1,2,2048,1,128]{4,2,3,1,0:T(8,128)(2,1)S(1)}, bf16[1,2,2048,1,128]{4,2,3,1,0:T(8,128)(2,1)}, u32[]{:S(2)}) copy-start(bf16[1,2,2048,1,128]{4,2,3,1,0:T(8,128)(2,1)} %param.7) | copy-start | bytes 3145732
  107.7 96.5 %all-to-all-start.1 = ((bf16[32,2,128,128]{3,2,1,0:T(8,128)(2,1)}), bf16[32,2,128,128]{3,2,1,0:T(8,128)(2,1)}, u32[]{:S(2)}, u32[]{:S(2)}) async-start(bf16[32,2,128,128]{3,2,1,0:T(8,128)(2,1)} %pack_blocks.1), calls=%async_computation.1 | async-start | bytes 4194304 | tf_op jit(solution)/shard_map/all_to_all | solution.py:382
  115.9 11.4 %collective-permute-start.2 = (bf16[1536,128]{1,0:T(8,128)(2,1)S(1)}, bf16[1536,128]{1,0:T(8,128)(2,1)S(1)}, u32[]{:S(2)}, u32[]{:S(2)}) collective-permute-start(bf16[1536,128]{1,0:T(8,128)(2,1)S(1)} %copy-done.1), channel_id=1, source_target_pairs={{0,128},{128,0},{1,129},{129,1},{2,130},{130,2},{3,131},{131,3},{4... | collective-permute-start | bytes 1179656 | tf_op jit(solution)/shard_map/ppermute | solution.py:384
  119.6 3.1 %collective-permute-start = (bf16[128,128]{1,0:T(8,128)(2,1)S(1)}, bf16[128,128]{1,0:T(8,128)(2,1)S(1)}, u32[]{:S(2)}, u32[]{:S(2)}) collective-permute-start(bf16[128,128]{1,0:T(8,128)(2,1)S(1)} %pad.8.q_ref), channel_id=1, source_target_pairs={{0,256},{256,0},{1,257},{257,1},{2,258},{258,2},{3,259},{259,3},{4... | collective-permute-start | bytes 98312 | tf_op jit(solution)/shard_map/ppermute | solution.py:378
  124.2 3.1 %collective-permute-start.1 = (bf16[32,128]{1,0:T(8,128)(2,1)S(1)}, bf16[32,128]{1,0:T(8,128)(2,1)S(1)}, u32[]{:S(2)}, u32[]{:S(2)}) collective-permute-start(bf16[32,128]{1,0:T(8,128)(2,1)S(1)} %decode_partial.1), channel_id=1, source_target_pairs={{0,256},{256,0},{1,257},{257,1},{2,258},{258,2},{3,259},{259,3},{4... | collective-permute-start | bytes 24584 | tf_op jit(solution)/shard_map/ppermute | solution.py:379
  135.8 15.6 %collective-permute-start.3 = (bf16[1616,128]{1,0:T(8,128)(2,1)S(1)}, bf16[1616,128]{1,0:T(8,128)(2,1)S(1)}, u32[]{:S(2)}, u32[]{:S(2)}) collective-permute-start(bf16[1616,128]{1,0:T(8,128)(2,1)S(1)} %slab_partial.3), channel_id=1, source_target_pairs={{0,128},{128,0},{1,129},{129,1},{2,130},{130,2},{3,131},{131,3},{4... | collective-permute-start | bytes 1241096 | tf_op jit(solution)/shard_map/ppermute | solution.py:387
  147.1 65.2 %copy-start.3 = (s32[2,1,384]{2,1,0:T(1,128)S(1)}, s32[2,1,384]{2,1,0:T(1,128)}, u32[]{:S(2)}) copy-start(s32[2,1,384]{2,1,0:T(1,128)} %param.9) | copy-start | bytes 9220
  152.9 87.9 %copy-start.4 = (bf16[1,2,2,1,128]{4,2,3,1,0:T(2,128)(2,1)S(1)}, bf16[1,2,2,1,128]{4,2,3,1,0:T(2,128)(2,1)}, u32[]{:S(2)}) copy-start(bf16[1,2,2,1,128]{4,2,3,1,0:T(2,128)(2,1)} %param.11) | copy-start | bytes 3076
  204.3 40.5 %all-to-all-start = ((bf16[16,176,128]{2,1,0:T(8,128)(2,1)}), bf16[16,176,128]{2,1,0:T(8,128)(2,1)S(1)}, u32[]{:S(2)}, u32[]{:S(2)}) async-start(bf16[16,176,128]{2,1,0:T(8,128)(2,1)} %pair_merge.1), calls=%async_computation | async-start | bytes 1441792 | tf_op jit(solution)/shard_map/all_to_all | solution.py:389
  238.8 21.6 %collective-permute-start.5 = (bf16[2,12,128,128]{3,2,1,0:T(8,128)(2,1)}, bf16[2,12,128,128]{3,2,1,0:T(8,128)(2,1)S(1)}, u32[]{:S(2)}, u32[]{:S(2)}) collective-permute-start(bf16[2,12,128,128]{3,2,1,0:T(8,128)(2,1)} %select_slots.1), channel_id=1, source_target_pairs={{0,256},{256,0},{1,257},{257,1},{2,258},{258,2},{3,259},{259,3},{4... | collective-permute-start | bytes 2359304 | tf_op jit(solution)/shard_map/ppermute | solution.py:396
  246.7 7.5 %collective-permute-start.4 = (f32[4,1,384]{2,1,0:T(1,128)S(1)}, f32[4,1,384]{2,1,0:T(1,128)S(1)}, u32[]{:S(2)}, u32[]{:S(2)}) collective-permute-start(f32[4,1,384]{2,1,0:T(1,128)S(1)} %reshape.47.lse_ref), channel_id=1, source_target_pairs={{0,128},{128,0},{1,129},{129,1},{2,130},{130,2},{3,131},{131,3},{4... | collective-permute-start | bytes 18440 | tf_op jit(solution)/shard_map/ppermute | solution.py:392

commit v2 on v1

v2 whole, which is shorter than its diff:
```python
import functools
import math

import jax
import jax.numpy as jnp
from jax import lax
from jax.experimental import pallas as pl
from jax.experimental.pallas import tpu as pltpu
from jax.sharding import Mesh
from jax.sharding import PartitionSpec as P

BLK = 128
HD = 128
NZ = 16
NCTX = 32
ROWS = 96
HALF = NZ * ROWS
CTXL = 2048
SLAB = 256
RB = 384
NRB = HALF // RB
SLOTS = 12
STEPR = 24
NEG = -1e30
C2 = math.log2(math.e) / math.sqrt(HD)
BF = jnp.bfloat16
F32 = jnp.float32

LR = HALF // HD
DECR = 3 * LR
DSTAT = DECR + STEPR
TAIL = 64
XROWS = HALF + TAIL
ZROWS = ROWS + TAIL
DEC = 32


def params(mib=40):
    return pltpu.CompilerParams(vmem_limit_bytes=mib * 1024 * 1024)


def parts_of(x):
    hi = x.astype(BF).astype(F32)
    mid = (x - hi).astype(BF).astype(F32)
    return hi, mid, x - hi - mid


def column(row):
    return jnp.broadcast_to(row, (128, 128)).T


def scores_t(k, q):
    return lax.dot_general(k, q, (((1,), (1,)), ((), ())), preferred_element_type=F32)


def masked_tail(info_ref, half, i, tail):
    key = lax.broadcasted_iota(jnp.int32, tail.shape, 0)
    row = lax.broadcasted_iota(jnp.int32, tail.shape, 1) + i * RB
    token = half * (SLAB // 2) + (row // ROWS) * 8 + row % 8
    seen = (key <= token) | (info_ref[0] < NCTX - 1)
    return jnp.where(seen, tail, NEG)


def fill_vt(v, vt_ref):
    vt_ref[0:HD, :] = v.astype(F32).T.astype(BF)
    vt_ref[HD:, :] = jnp.ones((16, CTXL), BF)


def put_stats(t_ref, lse, dec, dec_lse):
    for n, part in enumerate(parts_of(lse)):
        t_ref[n * LR : (n + 1) * LR, :] = part
    t_ref[DECR:DSTAT, :] = dec
    for n, part in enumerate(parts_of(dec_lse)):
        t_ref[DSTAT + n : DSTAT + n + 1, :] = part
    t_ref[DSTAT + 3 :, :] = jnp.zeros((TAIL - DSTAT - 3, HD), F32)


def get_stats(t):
    t = t.astype(F32)
    lse = t[0:LR] + t[LR : 2 * LR] + t[2 * LR : 3 * LR]
    dec_lse = t[DSTAT : DSTAT + 1] + t[DSTAT + 1 : DSTAT + 2] + t[DSTAT + 2 : DSTAT + 3]
    return lse, t[DECR:DSTAT], dec_lse


def flash_kernel(other, info_ref, q_ref, k_ref, v_ref, d_ref, x_ref, vt_ref, s_ref, lse_ref, t_ref):
    i = pl.program_id(0)

    @pl.when(i == 0)
    def _():
        fill_vt(v_ref[0], vt_ref)

    s_ref[...] = scores_t(k_ref[0], q_ref[...])
    s_ref[CTXL - SLAB :, :] = masked_tail(info_ref, info_ref[1] ^ other, i, s_ref[CTXL - SLAB :, :])
    top = jnp.max(s_ref[...], axis=0, keepdims=True)
    p = jnp.exp2((s_ref[...] - top) * C2).astype(BF)
    acc = jnp.dot(vt_ref[...], p, preferred_element_type=F32)
    mass = acc[HD : HD + 1]
    x_ref[pl.ds(pl.multiple_of(i * RB, RB), RB), :] = (acc[0:HD] * (1.0 / mass)).T.astype(BF)
    lse = top * C2 + jnp.log2(mass)
    for j in range(RB // HD):
        lse_ref[pl.ds(i * (RB // HD) + j, 1), :] = lse[:, j * HD : (j + 1) * HD]

    @pl.when(i == NRB - 1)
    def _():
        d = d_ref[...]
        put_stats(t_ref, lse_ref[0:LR, :], d[0:STEPR], d[STEPR : STEPR + 1])
        x_ref[HALF:, :] = t_ref[...].astype(BF)


def flash(other, info, q, kv, dec):
    return pl.pallas_call(
        functools.partial(flash_kernel, other),
        out_shape=jax.ShapeDtypeStruct((XROWS, HD), BF),
        grid=(NRB,),
        in_specs=[
            pl.BlockSpec(memory_space=pltpu.SMEM),
            pl.BlockSpec((RB, HD), lambda i: (i, 0)),
            pl.BlockSpec((1, CTXL, HD), lambda i: (0, 0, 0)),
            pl.BlockSpec((1, CTXL, HD), lambda i: (1, 0, 0)),
            pl.BlockSpec((DEC, HD), lambda i: (0, 0)),
        ],
        out_specs=pl.BlockSpec((XROWS, HD), lambda i: (0, 0)),
        scratch_shapes=[
            pltpu.VMEM((HD + 16, CTXL), BF),
            pltpu.VMEM((CTXL, RB), F32),
            pltpu.VMEM((16, HD), F32),
            pltpu.VMEM((TAIL, HD), F32),
        ],
        compiler_params=params(),
        cost_estimate=pl.CostEstimate(
            flops=4 * HALF * CTXL * HD, bytes_accessed=2 * CTXL * HD * 2, transcendentals=HALF * CTXL
        ),
        name="slab_partial",
    )(info, q, kv, kv, dec)


def decode_kernel(flag_ref, q_ref, k_ref, v_ref, d_ref, vt_ref, s_ref):
    fill_vt(v_ref[0], vt_ref)
    for b in range(CTXL // BLK):
        s = scores_t(k_ref[0, b * BLK : (b + 1) * BLK, :], q_ref[...])
        kept = jnp.broadcast_to(flag_ref[b], s.shape) > 0
        s_ref[b * BLK : (b + 1) * BLK, :] = jnp.where(kept, s, NEG)
    top = jnp.max(s_ref[...], axis=0, keepdims=True)
    p = jnp.exp2((s_ref[...] - top) * C2).astype(BF)
    acc = jnp.dot(vt_ref[...], p, preferred_element_type=F32)
    mass = acc[HD : HD + 1]
    out = (acc[0:HD] * (1.0 / mass)).T
    lse = jnp.maximum(top * C2 + jnp.log2(mass), NEG)
    d_ref[...] = jnp.zeros_like(d_ref)
    d_ref[0:STEPR, :] = out[0:STEPR]
    d_ref[STEPR : STEPR + 1, :] = lse


def decode_partial(flags, q, kv):
    return pl.pallas_call(
        decode_kernel,
        out_shape=jax.ShapeDtypeStruct((DEC, HD), F32),
        grid=(1,),
        in_specs=[
            pl.BlockSpec(memory_space=pltpu.SMEM),
            pl.BlockSpec((HD, HD), lambda i: (0, 0)),
            pl.BlockSpec((1, CTXL, HD), lambda i: (0, 0, 0)),
            pl.BlockSpec((1, CTXL, HD), lambda i: (1, 0, 0)),
        ],
        out_specs=pl.BlockSpec((DEC, HD), lambda i: (0, 0)),
        scratch_shapes=[
            pltpu.VMEM((HD + 16, CTXL), BF),
            pltpu.VMEM((CTXL, HD), F32),
        ],
        compiler_params=params(),
        name="decode_partial",
    )(flags, q, kv, kv)


def merge_weights(lses):
    top = lses[0]
    for x in lses[1:]:
        top = jnp.maximum(top, x)
    es = [jnp.exp2(x - top) for x in lses]
    den = es[0]
    for e in es[1:]:
        den = den + e
    inv = 1.0 / den
    return [e * inv for e in es], top + jnp.log2(den)


def pair_kernel(a_ref, b_ref, z_ref, t_ref):
    la, da, sa = get_stats(a_ref[HALF:, :])
    lb, db, sb = get_stats(b_ref[HALF:, :])
    (wa, wb), lse = merge_weights([la, lb])
    (ua, ub), sd = merge_weights([sa, sb])
    put_stats(t_ref, lse, da * column(ua)[0:STEPR] + db * column(ub)[0:STEPR], sd)
    tail = t_ref[...].astype(BF)
    for n in range(NZ):
        z_ref[n, ROWS:, :] = tail
    for g in range(LR):
        rows = slice(g * HD, (g + 1) * HD)
        mixed = a_ref[rows, :].astype(F32) * column(wa[g : g + 1]) + b_ref[rows, :].astype(F32) * column(wb[g : g + 1])
        mixed = mixed.astype(BF)
        for j in range(0, HD, 32):
            n, at = divmod(g * HD + j, ROWS)
            z_ref[n, at : at + 32, :] = mixed[j : j + 32]


def pair_merge(a, b):
    return pl.pallas_call(
        pair_kernel,
        out_shape=jax.ShapeDtypeStruct((NZ, ZROWS, HD), BF),
        scratch_shapes=[pltpu.VMEM((TAIL, HD), F32)],
        compiler_params=params(),
        name="pair_merge",
    )(a, b)


def final_kernel(info_ref, r_ref, q_ref, nk_ref, nv_ref, slab_ref, lse_ref, step_ref, l_ref, w_ref):
    stats = [get_stats(r_ref[s, ROWS:, :]) for s in range(NZ)]
    top = stats[0][0]
    for s in range(1, NZ):
        top = jnp.maximum(top, stats[s][0])
    den = jnp.zeros_like(top)
    for s in range(NZ):
        den = den + jnp.exp2(stats[s][0] - top)
        l_ref[0:LR, s, :] = stats[s][0]
        l_ref[LR, s, :] = jnp.zeros((HD,), F32)
    lse = top + jnp.log2(den)
    lse_ref[...] = lse
    l_ref[0:LR, NZ, :] = lse
    l_ref[LR, NZ, :] = jnp.zeros((HD,), F32)
    first = info_ref[2] * ROWS
    both = jnp.concatenate([l_ref[first // HD], l_ref[first // HD + 1]], axis=1)
    own = pltpu.roll(both, (2 * HD - first % HD) % (2 * HD), 1)[:, 0:HD]
    w_ref[...] = jnp.zeros_like(w_ref)
    w_ref[0:NZ, :] = jnp.exp2(own[0:NZ] - own[NZ : NZ + 1])
    weights = w_ref[...].T
    total = jnp.zeros((ROWS, HD), F32)
    for s in range(NZ):
        total = total + r_ref[s, 0:ROWS, :].astype(F32) * weights[0:ROWS, s : s + 1]
    slab_ref[...] = total.astype(BF)
    fresh = scores_t(nk_ref[...], q_ref[...]) * C2
    lane = lax.broadcasted_iota(jnp.int32, (1, HD), 1)
    first_new = fresh[0:1]
    second_new = jnp.where(lane % 2 == 1, fresh[1:2], NEG)
    us, _ = merge_weights([t[2] for t in stats] + [first_new, second_new])
    for s in range(NZ + 2):
        w_ref[s : s + 1, :] = us[s]
    shares = w_ref[...].T
    nv = nv_ref[...].astype(F32)
    out = shares[0:STEPR, NZ : NZ + 1] * nv[0:1] + shares[0:STEPR, NZ + 1 : NZ + 2] * nv[1:2]
    for s in range(NZ):
        out = out + stats[s][1] * shares[0:STEPR, s : s + 1]
    step_ref[...] = out.astype(BF)


def final_merge(info, r, q, nk, nv):
    return pl.pallas_call(
        final_kernel,
        out_shape=(
            jax.ShapeDtypeStruct((ROWS, HD), BF),
            jax.ShapeDtypeStruct((LR, HD), F32),
            jax.ShapeDtypeStruct((STEPR, HD), BF),
        ),
        in_specs=[pl.BlockSpec(memory_space=pltpu.SMEM)] + [pl.BlockSpec(memory_space=pltpu.VMEM)] * 4,
        out_specs=[pl.BlockSpec(memory_space=pltpu.VMEM)] * 3,
        scratch_shapes=[pltpu.VMEM((LR + 1, 24, HD), F32), pltpu.VMEM((HD, HD), F32)],
        compiler_params=params(),
        name="final_merge",
    )(info, r, q, nk, nv)


def heavy_kernel(other, info_ref, q_ref, k_ref, lse_ref, prev_ref, h_ref, acc_ref):
    i = pl.program_id(0)

    @pl.when(i == 0)
    def _():
        acc_ref[...] = jnp.zeros_like(acc_ref)

    q = q_ref[...]
    per = RB // HD
    lse = jnp.concatenate([lse_ref[pl.ds(i * per + j, 1), :] for j in range(per)], axis=1)
    for c in range(CTXL // SLAB):
        keys = slice(c * SLAB, (c + 1) * SLAB)
        s = scores_t(k_ref[0, keys, :], q)
        if c == CTXL // SLAB - 1:
            s = masked_tail(info_ref, info_ref[1] ^ other, i, s)
        w = jnp.exp2(s * C2 - lse)
        acc_ref[keys, :] += w[:, 0:128] + w[:, 128:256] + w[:, 256:384]

    @pl.when(i == NRB - 1)
    def _():
        ones = jnp.ones((8, 128), F32)
        sums = lax.dot_general(
            ones, acc_ref[...], (((1,), (1,)), ((), ())), precision=lax.Precision.HIGHEST, preferred_element_type=F32
        )
        h_ref[...] = sums[0:1] * (NCTX * CTXL / (12 * SLAB)) + prev_ref[...]


def heavy(other, info, q, kv, lse, prev):
    return pl.pallas_call(
        functools.partial(heavy_kernel, other),
        out_shape=jax.ShapeDtypeStruct((1, CTXL), F32),
        grid=(NRB,),
        in_specs=[
            pl.BlockSpec(memory_space=pltpu.SMEM),
            pl.BlockSpec((RB, HD), lambda i: (i, 0)),
            pl.BlockSpec((1, CTXL, HD), lambda i: (0, 0, 0)),
            pl.BlockSpec((LR, HD), lambda i: (0, 0)),
            pl.BlockSpec((1, CTXL), lambda i: (0, 0)),
        ],
        out_specs=pl.BlockSpec((1, CTXL), lambda i: (0, 0)),
        scratch_shapes=[pltpu.VMEM((CTXL, HD), F32)],
        compiler_params=params(),
        cost_estimate=pl.CostEstimate(
            flops=2 * HALF * CTXL * HD, bytes_accessed=CTXL * HD * 2, transcendentals=HALF * CTXL
        ),
        name="heavy_columns",
    )(info, q, kv, lse, prev)


def pack_kernel(pick_ref, kv_ref, out_ref, sems):
    copies = [
        pltpu.make_async_copy(kv_ref.at[n, pick_ref[d]], out_ref.at[d, n], sems.at[n, d])
        for d in range(NCTX)
        for n in range(2)
    ]
    for copy in copies:
        copy.start()
    for copy in copies:
        copy.wait()


def pack(pick, blocks):
    return pl.pallas_call(
        pack_kernel,
        out_shape=jax.ShapeDtypeStruct((NCTX, 2, BLK, HD), BF),
        in_specs=[pl.BlockSpec(memory_space=pltpu.SMEM), pl.BlockSpec(memory_space=pltpu.VMEM)],
        out_specs=pl.BlockSpec(memory_space=pl.ANY),
        scratch_shapes=[pltpu.SemaphoreType.DMA((2, NCTX))],
        compiler_params=params(),
        name="pack_blocks",
    )(pick, blocks)


def after_kernel(x_ref, after_ref, out_ref):
    del x_ref, after_ref, out_ref


def after(x, other):
    return pl.pallas_call(
        after_kernel,
        out_shape=jax.ShapeDtypeStruct(x.shape, x.dtype),
        in_specs=[pl.BlockSpec(memory_space=pl.ANY)] * 2,
        out_specs=pl.BlockSpec(memory_space=pl.ANY),
        input_output_aliases={0: 0},
        name="after",
    )(x, other)


def select_kernel(src_ref, in_ref, out_ref, sems):
    copies = [
        pltpu.make_async_copy(in_ref.at[src_ref[r], n], out_ref.at[n, r], sems.at[n, r])
        for n in range(2)
        for r in range(SLOTS)
    ]
    for copy in copies:
        copy.start()
    for copy in copies:
        copy.wait()


def select(source, arrived):
    return pl.pallas_call(
        select_kernel,
        out_shape=jax.ShapeDtypeStruct((2, SLOTS, BLK, HD), BF),
        in_specs=[pl.BlockSpec(memory_space=pltpu.SMEM), pl.BlockSpec(memory_space=pl.ANY)],
        out_specs=pl.BlockSpec(memory_space=pltpu.VMEM),
        scratch_shapes=[pltpu.SemaphoreType.DMA((2, SLOTS))],
        compiler_params=params(),
        name="select_slots",
    )(source, arrived)


def spread_kernel(q_ref, out_ref):
    for n in range(NZ):
        out_ref[n] = q_ref[...]


def spread(q):
    return pl.pallas_call(
        spread_kernel,
        out_shape=jax.ShapeDtypeStruct((NZ, ROWS, HD), BF),
        compiler_params=params(),
        name="spread_queries",
    )(q)


SWAP = [(0, 1), (1, 0)]


def local(slab_query, kv_cache, kept_list, decode_place, step_query, step_cache):
    grp = lax.axis_index("grp")
    xl = lax.axis_index("xl")
    z = lax.axis_index("z")
    ctx = xl * NZ + z
    per_dev = CTXL // BLK

    kept = lax.dynamic_index_in_dim(kept_list, 1 - grp, 0, keepdims=False)[0]
    place = lax.dynamic_index_in_dim(decode_place, 1 - grp, 0, keepdims=False)[0]
    lanes = jnp.arange(NCTX, dtype=jnp.int32)
    offset = kept - ctx * per_dev
    mine = (offset >= 0) & (offset < per_dev)
    hit = mine[None, :] & (place[None, :] == lanes[:, None])
    pick = jnp.clip(jnp.sum(jnp.where(hit, offset[None, :], 0), axis=1), 0, per_dev - 1)
    flags = jnp.sum(
        (offset[None, :] == jnp.arange(per_dev, dtype=jnp.int32)[:, None]).astype(jnp.int32), axis=1
    )
    here = (place == ctx).reshape(SLOTS, NCTX)
    source = jnp.clip(
        jnp.sum(jnp.where(here, kept.reshape(SLOTS, NCTX) // per_dev, 0), axis=1), 0, NCTX - 1
    )
    info = jnp.stack([ctx, xl, z]).astype(jnp.int32)

    q = jnp.transpose(slab_query[0, :, 0], (1, 0, 2)).reshape(ROWS, HD)
    kv = kv_cache[0, :, :, 0]
    steps = jnp.transpose(step_query[0, :, 0], (1, 0, 2)).reshape(STEPR, HD)
    steps = jnp.pad(steps, ((0, HD - STEPR), (0, 0)))
    new = jnp.pad(step_cache[0, :, :, 0], ((0, 0), (0, 14), (0, 0)))

    q_own = lax.all_to_all(spread(q), "z", 0, 0, tiled=True).reshape(HALF, HD)
    kv_decode = lax.ppermute(kv, "grp", SWAP)
    blocks = kv_decode.reshape(2, per_dev, BLK, HD)
    dec = decode_partial(flags, steps, kv_decode)

    outgoing = after(pack(pick, blocks), q_own)
    arrived = lax.all_to_all(outgoing, ("xl", "z"), 0, 0, tiled=True)
    q_other = lax.ppermute(q_own, "xl", SWAP)
    part_own = flash(0, info, q_own, kv, dec)
    part_other = flash(1, info, q_other, kv, dec)
    part_partner = lax.ppermute(part_other, "xl", SWAP)
    merged = after(pair_merge(part_own, part_partner), arrived)
    received = lax.all_to_all(merged, "z", 0, 0, tiled=True)

    slab, lse, step = final_merge(info, received, steps, new[0], new[1])
    lse_other = lax.ppermute(lse, "xl", SWAP)
    columns = heavy(0, info, q_own, kv, lse, jnp.zeros((1, CTXL), F32))
    columns = heavy(1, info, q_other, kv, lse_other, columns)

    paged = select(source, arrived)

    slab_out = jnp.transpose(slab.reshape(12, 8, HD), (1, 0, 2))[None, :, None]
    step_out = jnp.transpose(step.reshape(12, 2, HD), (1, 0, 2))[None, :, None]
    return (slab_out, columns[None], paged[None, None], step_out)


def solution(mesh):
    split = Mesh(mesh.devices.reshape(2, 2, NZ, 8), ("grp", "xl", "z", "kvh"))
    ctx = ("xl", "z")
    return jax.shard_map(
        local,
        mesh=split,
        in_specs=(
            P("grp", ctx, "kvh", None, None),
            P("grp", None, ctx, "kvh", None),
            P(None, "kvh", None),
            P(None, "kvh", None),
            P("grp", None, "kvh", None, None),
            P("grp", None, None, "kvh", None),
        ),
        out_specs=(
            P("grp", ctx, "kvh", None, None),
            P("grp", "kvh", ctx),
            P("grp", "kvh", None, ctx, None, None),
            P("grp", None, "kvh", None, None),
        ),
        check_vma=False,
    )
```

time: 262 us -> 202 us (0.77)
  Pallas kernels: 125 us -> 36 us
  waiting for transfers between devices: 61.6 us -> 111 us
  blocking collectives: 40.1 us -> 0 us
  starting transfers between devices: 30.4 us -> 42.6 us
  local copies, waits for them, and re-layouts: 1.17 us -> 8.95 us
    pallas_call x1, Pallas kernels: 65.6 us -> 4.02 us  [pack(): pl.pallas_call(pack_kernel, out_shape=jax.ShapeDtypeStruct((NCTX, 2, BLK,...]
    all_gather x1 -> x0, blocking collectives: 40.1 us -> none  [local(): q_own = lax.all_gather(q, 'z', axis=0, tiled=True)]
    all_to_all x1, waiting for transfers between devices: 4.03 us -> 27.6 us  [local(): received = lax.all_to_all(merged, 'z', 0, 0, tiled=True)]
    pallas_call x1, Pallas kernels: 25.7 us -> 2.7 us  [select(): pl.pallas_call(select_kernel, out_shape=jax.ShapeDtypeStruct((2, SLOTS, B...]
    all_to_all x0 -> x1, starting transfers between devices: none -> 15.2 us  [local(): q_own = lax.all_to_all(spread(q), 'z', 0, 0, tiled=True).reshape(HALF, HD)]
    all_to_all x0 -> x1, waiting for transfers between devices: none -> 13.6 us  [local(): q_own = lax.all_to_all(spread(q), 'z', 0, 0, tiled=True).reshape(HALF, HD)]
    ppermute x1, waiting for transfers between devices: 0.01 us -> 8.47 us  [local(): q_other = lax.ppermute(q_own, 'xl', SWAP)]
    unnamed x11 -> x28, local copies, waits for them, and re-layouts: 0.91 us -> 7.4 us
  transfers between devices with their start and end apart: 8 -> 7, of which waited for: 5 -> 6; matrix products, arithmetic and copies ran while one was open for 0% -> 1% of each run, Pallas kernels for 23% -> 14%
where the time goes in v2:
time: 202 us; the launch traced here: 201 us
  waiting for transfers between devices  111 us (55%)
  starting transfers between devices  42.6 us (21%)
  Pallas kernels  36 us (18%)
  local copies, waits for them, and re-layouts  8.95 us (4%)
    all_to_all x1, waiting for transfers between devices, local(): arrived = lax.all_to_all(outgoing, ('xl', 'z'), 0, 0, tiled=True)  57.4 us
    all_to_all x1, waiting for transfers between devices, local(): received = lax.all_to_all(merged, 'z', 0, 0, tiled=True)  27.6 us
    pallas_call x2, Pallas kernels, flash(): pl.pallas_call(functools.partial(flash_kernel, other), out_shape=jax.Shap...  15.6 us
    all_to_all x1, starting transfers between devices, local(): q_own = lax.all_to_all(spread(q), 'z', 0, 0, tiled=True).reshape(HALF, HD)  15.2 us
    all_to_all x1, waiting for transfers between devices, local(): q_own = lax.all_to_all(spread(q), 'z', 0, 0, tiled=True).reshape(HALF, HD)  13.6 us
    pallas_call x2, Pallas kernels, heavy(): pl.pallas_call(functools.partial(heavy_kernel, other), out_shape=jax.Shap...  8.92 us
    ppermute x1, waiting for transfers between devices, local(): q_other = lax.ppermute(q_own, 'xl', SWAP)  8.47 us
    all_to_all x1, starting transfers between devices, local(): received = lax.all_to_all(merged, 'z', 0, 0, tiled=True)  8.3 us
  transfers between devices with their start and end apart: 7, of which 6 were waited for; matrix products, arithmetic and copies ran while one was open for 1% of the time, Pallas kernels for 14%

profile of v2, /device:TPU:24, one launch (start us, length us, event | category | flops | bytes accessed | tf_op | source)
XLA Modules:
  0.0 200.6 jit_solution(14918602201464774252)
XLA Ops:
  0.6 0.0 copy-start.8
  0.6 0.7 copy-done.8
  1.4 0.8 spread_queries.1
  2.2 15.2 %all-to-all-start = ((bf16[16,96,128]{2,1,0:T(8,128)(2,1)}), bf16[16,96,128]{2,1,0:T(8,128)(2,1)S(1)}, u32[]{:S(2)}, u32[]{:S(2)}) async-start(bf16[16,96,128]{2,1,0:T(8,128)(2,1)} %spread_queries.1), calls=%async_computation | async-start | bytes 786432 | tf_op jit(solution)/shard_map/all_to_all | solution.py:428
  17.4 1.9 collective-permute-start
  19.3 0.7 dynamic-slice_reduce_fusion.1
  20.0 0.1 select_reduce_fusion
  20.2 2.0 collective-permute-done.k_ref.v_ref
  22.1 4.0 %pack_blocks.1.x_ref = bf16[32,2,128,128]{3,2,1,0:T(8,128)(2,1)S(1)} custom-call(s32[32]{0:T(128)S(1)} %broadcast_clamp_fusion.1.pick_ref, bf16[2,16,128,128]{3,2,1,0:T(8,128)(2,1)S(1)} %bitcast.33), custom_call_target="tpu_custom_call" | custom-call | tf_op jit(solution)/shard_map/pack_blocks/pallas_call | solution.py:332
  26.2 0.0 copy-start.2
  26.2 1.3 copy-done.2
  27.5 13.6 %all-to-all-done = bf16[16,96,128]{2,1,0:T(8,128)(2,1)S(1)} async-done(((bf16[16,96,128]{2,1,0:T(8,128)(2,1)}), bf16[16,96,128]{2,1,0:T(8,128)(2,1)S(1)}, u32[]{:S(2)}, u32[]{:S(2)}) %all-to-all-start) | async-done | bytes 393248 | tf_op jit(solution)/shard_map/all_to_all | solution.py:428
  41.1 0.0 copy-start.4
  41.1 0.7 copy-done.4
  41.9 0.0 copy-start.5
  41.9 7.3 %all-to-all-start.1 = ((bf16[32,2,128,128]{3,2,1,0:T(8,128)(2,1)}), bf16[32,2,128,128]{3,2,1,0:T(8,128)(2,1)S(1)}, u32[]{:S(2)}, u32[]{:S(2)}) async-start(bf16[32,2,128,128]{3,2,1,0:T(8,128)(2,1)} %after.2), calls=%async_computation.1 | async-start | bytes 4194304 | tf_op jit(solution)/shard_map/all_to_all | solution.py:434
  49.2 0.0 copy-done.5
  49.2 0.0 copy-start.9
  49.3 3.8 %collective-permute-start.1 = (bf16[1536,128]{1,0:T(8,128)(2,1)S(1)}, bf16[1536,128]{1,0:T(8,128)(2,1)S(1)}, u32[]{:S(2)}, u32[]{:S(2)}) collective-permute-start(bf16[1536,128]{1,0:T(8,128)(2,1)S(1)} %bitcast.35), channel_id=1, source_target_pairs={{0,128},{128,0},{1,129},{129,1},{2,130},{130,2},{3,131},{131,3},{4... | collective-permute-start | bytes 1179656 | tf_op jit(solution)/shard_map/ppermute | solution.py:435
  53.1 0.7 pad.8.q_ref
  53.8 0.0 copy-start.6
  53.8 0.1 pad_add_fusion.info_ref
  53.9 0.1 convert_reduce_fusion.flag_ref
  54.0 1.5 decode_partial.1.d_ref
  55.5 0.0 copy-done.6
  55.5 8.5 %collective-permute-done.1.q_ref = bf16[1536,128]{1,0:T(8,128)(2,1)S(1)} collective-permute-done((bf16[1536,128]{1,0:T(8,128)(2,1)S(1)}, bf16[1536,128]{1,0:T(8,128)(2,1)S(1)}, u32[]{:S(2)}, u32[]{:S(2)}) %collective-permute-start.1) | collective-permute-done | bytes 393248 | tf_op jit(solution)/shard_map/ppermute | solution.py:435
  64.0 0.0 copy-done.9
  64.0 7.8 %slab_partial.3 = bf16[1600,128]{1,0:T(8,128)(2,1)S(1)} custom-call(s32[3]{0:T(128)S(1)} %pad_add_fusion.info_ref, bf16[1536,128]{1,0:T(8,128)(2,1)S(1)} %collective-permute-done.1.q_ref, bf16[2,2048,128]{2,1,0:T(8,128)(2,1)S(1)} %bitcast.40, bf16[2,2048,128]{2,1,0:T(8,128)(2,1)S(1)} %bitcast.41, f32[32,128]{1,0:T(8,128)S(1)} %decode_partial.1.d_ref), custom_call_target="tpu_custom_call" | custom-call | flops 1610612736 | bytes 1048576 | tf_op jit(solution)/shard_map/slab_partial/pallas_call | solution.py:111
  71.8 0.0 copy-start.11
  71.8 0.8 copy-done.11
  72.6 3.2 %collective-permute-start.2 = (bf16[1600,128]{1,0:T(8,128)(2,1)S(1)}, bf16[1600,128]{1,0:T(8,128)(2,1)S(1)}, u32[]{:S(2)}, u32[]{:S(2)}) collective-permute-start(bf16[1600,128]{1,0:T(8,128)(2,1)S(1)} %slab_partial.3), channel_id=1, source_target_pairs={{0,128},{128,0},{1,129},{129,1},{2,130},{130,2},{3,131},{131,3},{4... | collective-permute-start | bytes 1228808 | tf_op jit(solution)/shard_map/ppermute | solution.py:438
  75.8 7.8 %slab_partial.2.a_ref = bf16[1600,128]{1,0:T(8,128)(2,1)S(1)} custom-call(s32[3]{0:T(128)S(1)} %pad_add_fusion.info_ref, bf16[1536,128]{1,0:T(8,128)(2,1)S(1)} %bitcast.36, bf16[2,2048,128]{2,1,0:T(8,128)(2,1)S(1)} %bitcast.42, bf16[2,2048,128]{2,1,0:T(8,128)(2,1)S(1)} %bitcast.43, f32[32,128]{1,0:T(8,128)S(1)} %decode_partial.1.d_ref), custom_call_target="tpu_custom_call" | custom-call | flops 1610612736 | bytes 1048576 | tf_op jit(solution)/shard_map/slab_partial/pallas_call | solution.py:111
  83.7 1.9 collective-permute-done.2.b_ref
  85.6 0.5 pair_merge.1.x_ref
  86.1 0.0 copy-start.3
  86.1 0.8 copy-done.3
  87.0 0.0 copy-start.13
  87.0 57.4 %all-to-all-done.1.after_ref.in_ref = bf16[32,2,128,128]{3,2,1,0:T(8,128)(2,1)S(1)} async-done(((bf16[32,2,128,128]{3,2,1,0:T(8,128)(2,1)}), bf16[32,2,128,128]{3,2,1,0:T(8,128)(2,1)S(1)}, u32[]{:S(2)}, u32[]{:S(2)}) %all-to-all-start.1) | async-done | bytes 2097184 | tf_op jit(solution)/shard_map/all_to_all | solution.py:434
  144.4 0.0 copy-start
  144.4 1.4 copy-done
  145.7 0.0 copy-start.7
  145.7 0.0 copy-start.10
  145.7 8.3 %all-to-all-start.2 = ((bf16[16,160,128]{2,1,0:T(8,128)(2,1)}), bf16[16,160,128]{2,1,0:T(8,128)(2,1)S(1)}, u32[]{:S(2)}, u32[]{:S(2)}) async-start(bf16[16,160,128]{2,1,0:T(8,128)(2,1)} %after.3), calls=%async_computation.2 | async-start | bytes 1310720 | tf_op jit(solution)/shard_map/all_to_all | solution.py:440
  154.0 0.1 reshape_squeeze.3
  154.1 0.0 copy-done.13
  154.1 0.1 eq.51
  154.2 0.7 fusion.6
  154.9 0.1 fusion.3
  155.0 0.0 copy-start.1
  155.0 1.6 copy-done.1
  156.6 2.7 %select_slots.1 = bf16[2,12,128,128]{3,2,1,0:T(8,128)(2,1)} custom-call(s32[12]{0:T(128)S(1)} %broadcast_clamp_fusion.src_ref, bf16[32,2,128,128]{3,2,1,0:T(8,128)(2,1)S(1)} %copy-done.1), custom_call_target="tpu_custom_call" | custom-call | tf_op jit(solution)/shard_map/select_slots/pallas_call | solution.py:371
  159.3 27.6 %all-to-all-done.2.r_ref = bf16[16,160,128]{2,1,0:T(8,128)(2,1)S(1)} async-done(((bf16[16,160,128]{2,1,0:T(8,128)(2,1)}), bf16[16,160,128]{2,1,0:T(8,128)(2,1)S(1)}, u32[]{:S(2)}, u32[]{:S(2)}) %all-to-all-start.2) | async-done | bytes 655392 | tf_op jit(solution)/shard_map/all_to_all | solution.py:440
  187.0 0.0 copy-done.7
  187.0 1.9 final_merge.1
  188.9 2.8 %collective-permute-start.3 = (f32[12,128]{1,0:T(8,128)S(1)}, f32[12,128]{1,0:T(8,128)S(1)}, u32[]{:S(2)}, u32[]{:S(2)}) collective-permute-start(f32[12,128]{1,0:T(8,128)S(1)} %get-tuple-element.8.lse_ref), channel_id=1, source_target_pairs={{0,128},{128,0},{1,129},{129,1},{2,130},{130,2},{3,131},{131,3},{4... | collective-permute-start | bytes 18440 | tf_op jit(solution)/shard_map/ppermute | solution.py:443
  191.7 0.0 copy-done.10
  191.7 0.0 copy-start.12
  191.7 4.2 %heavy_columns.2.prev_ref = f32[1,2048]{1,0:T(1,128)S(1)} custom-call(s32[3]{0:T(128)S(1)} %pad_add_fusion.info_ref, bf16[1536,128]{1,0:T(8,128)(2,1)S(1)} %bitcast.37, bf16[2,2048,128]{2,1,0:T(8,128)(2,1)S(1)} %bitcast.44, f32[12,128]{1,0:T(8,128)S(1)} %get-tuple-element.8.lse_ref, f32[1,2048]{1,0:T(1,128)S(1)} %broadcast_in_dim.37.prev_ref), custom_call_target="tpu_custom_call" | custom-call | flops 805306368 | bytes 524288 | tf_op jit(solution)/shard_map/heavy_columns/pallas_call | solution.py:298
  195.8 0.0 collective-permute-done.3.lse_ref
  195.8 0.0 copy-done.12
  195.9 4.8 %heavy_columns.3 = f32[1,2048]{1,0:T(1,128)} custom-call(s32[3]{0:T(128)S(1)} %pad_add_fusion.info_ref, bf16[1536,128]{1,0:T(8,128)(2,1)S(1)} %copy-done.12, bf16[2,2048,128]{2,1,0:T(8,128)(2,1)S(1)} %bitcast.45, f32[12,128]{1,0:T(8,128)S(1)} %collective-permute-done.3.lse_ref, f32[1,2048]{1,0:T(1,128)S(1)} %heavy_columns.2.prev_ref), custom_call_target="tpu_custom_call" | custom-call | flops 805306368 | bytes 524288 | tf_op jit(solution)/shard_map/heavy_columns/pallas_call | solution.py:298
  (7 shorter events, 0.1 us)
Async XLA Ops:
  0.6 0.7 copy-start.8
  2.2 39.0 %all-to-all-start = ((bf16[16,96,128]{2,1,0:T(8,128)(2,1)}), bf16[16,96,128]{2,1,0:T(8,128)(2,1)S(1)}, u32[]{:S(2)}, u32[]{:S(2)}) async-start(bf16[16,96,128]{2,1,0:T(8,128)(2,1)} %spread_queries.1), calls=%async_computation | async-start | bytes 786432 | tf_op jit(solution)/shard_map/all_to_all | solution.py:428
  17.4 4.8 %collective-permute-start = (bf16[2,2048,128]{2,1,0:T(8,128)(2,1)}, bf16[2,2048,128]{2,1,0:T(8,128)(2,1)S(1)}, u32[]{:S(2)}, u32[]{:S(2)}) collective-permute-start(bf16[2,2048,128]{2,1,0:T(8,128)(2,1)} %bitcast.39), channel_id=1, source_target_pairs={{0,256},{256,0},{1,257},{257,1},{2,258},{258,2},{3,259},{259,3},{4... | collective-permute-start | bytes 3145736 | tf_op jit(solution)/shard_map/ppermute | solution.py:429
  26.2 1.4 copy-start.2
  41.1 0.7 copy-start.4
  41.9 7.4 %copy-start.5 = (bf16[16,96,128]{2,1,0:T(8,128)(2,1)S(1)}, bf16[16,96,128]{2,1,0:T(8,128)(2,1)}, u32[]{:S(2)}) copy-start(bf16[16,96,128]{2,1,0:T(8,128)(2,1)} %copy-done.4) | copy-start | bytes 1179652
  41.9 102.5 %all-to-all-start.1 = ((bf16[32,2,128,128]{3,2,1,0:T(8,128)(2,1)}), bf16[32,2,128,128]{3,2,1,0:T(8,128)(2,1)S(1)}, u32[]{:S(2)}, u32[]{:S(2)}) async-start(bf16[32,2,128,128]{3,2,1,0:T(8,128)(2,1)} %after.2), calls=%async_computation.1 | async-start | bytes 4194304 | tf_op jit(solution)/shard_map/all_to_all | solution.py:434
  49.2 14.8 %copy-start.9 = (bf16[1,2,2048,1,128]{4,2,3,1,0:T(8,128)(2,1)S(1)}, bf16[1,2,2048,1,128]{4,2,3,1,0:T(8,128)(2,1)}, u32[]{:S(2)}) copy-start(bf16[1,2,2048,1,128]{4,2,3,1,0:T(8,128)(2,1)} %param.7) | copy-start | bytes 3145732
  49.3 14.8 %collective-permute-start.1 = (bf16[1536,128]{1,0:T(8,128)(2,1)S(1)}, bf16[1536,128]{1,0:T(8,128)(2,1)S(1)}, u32[]{:S(2)}, u32[]{:S(2)}) collective-permute-start(bf16[1536,128]{1,0:T(8,128)(2,1)S(1)} %bitcast.35), channel_id=1, source_target_pairs={{0,128},{128,0},{1,129},{129,1},{2,130},{130,2},{3,131},{131,3},{4... | collective-permute-start | bytes 1179656 | tf_op jit(solution)/shard_map/ppermute | solution.py:435
  53.8 1.7 copy-start.6
  71.8 0.8 copy-start.11
  72.6 13.0 %collective-permute-start.2 = (bf16[1600,128]{1,0:T(8,128)(2,1)S(1)}, bf16[1600,128]{1,0:T(8,128)(2,1)S(1)}, u32[]{:S(2)}, u32[]{:S(2)}) collective-permute-start(bf16[1600,128]{1,0:T(8,128)(2,1)S(1)} %slab_partial.3), channel_id=1, source_target_pairs={{0,128},{128,0},{1,129},{129,1},{2,130},{130,2},{3,131},{131,3},{4... | collective-permute-start | bytes 1228808 | tf_op jit(solution)/shard_map/ppermute | solution.py:438
  86.1 0.9 copy-start.3
  87.0 67.2 %copy-start.13 = (s32[2,1,384]{2,1,0:T(1,128)S(1)}, s32[2,1,384]{2,1,0:T(1,128)}, u32[]{:S(2)}) copy-start(s32[2,1,384]{2,1,0:T(1,128)} %param.9) | copy-start | bytes 9220
  144.4 1.4 copy-start
  145.7 41.3 %copy-start.7 = (bf16[128,128]{1,0:T(8,128)(2,1)S(1)}, bf16[128,128]{1,0:T(8,128)(2,1)}, u32[]{:S(2)}) copy-start(bf16[128,128]{1,0:T(8,128)(2,1)} %copy-done.6) | copy-start | bytes 98308
  145.7 45.9 %copy-start.10 = (bf16[1,2,2048,1,128]{4,2,3,1,0:T(8,128)(2,1)S(1)}, bf16[1,2,2048,1,128]{4,2,3,1,0:T(8,128)(2,1)}, u32[]{:S(2)}) copy-start(bf16[1,2,2048,1,128]{4,2,3,1,0:T(8,128)(2,1)} %param.7) | copy-start | bytes 3145732
  145.7 41.2 %all-to-all-start.2 = ((bf16[16,160,128]{2,1,0:T(8,128)(2,1)}), bf16[16,160,128]{2,1,0:T(8,128)(2,1)S(1)}, u32[]{:S(2)}, u32[]{:S(2)}) async-start(bf16[16,160,128]{2,1,0:T(8,128)(2,1)} %after.3), calls=%async_computation.2 | async-start | bytes 1310720 | tf_op jit(solution)/shard_map/all_to_all | solution.py:440
  155.0 1.6 copy-start.1
  188.9 7.0 %collective-permute-start.3 = (f32[12,128]{1,0:T(8,128)S(1)}, f32[12,128]{1,0:T(8,128)S(1)}, u32[]{:S(2)}, u32[]{:S(2)}) collective-permute-start(f32[12,128]{1,0:T(8,128)S(1)} %get-tuple-element.8.lse_ref), channel_id=1, source_target_pairs={{0,128},{128,0},{1,129},{129,1},{2,130},{130,2},{3,131},{131,3},{4... | collective-permute-start | bytes 18440 | tf_op jit(solution)/shard_map/ppermute | solution.py:443
  191.7 4.2 %copy-start.12 = (bf16[1536,128]{1,0:T(8,128)(2,1)S(1)}, bf16[1536,128]{1,0:T(8,128)(2,1)}, u32[]{:S(2)}) copy-start(bf16[1536,128]{1,0:T(8,128)(2,1)} %copy-done.11) | copy-start | bytes 1179652

commit v3 on v2

--- a/solution.py
+++ b/solution.py
@@ -17,7 +17,7 @@
 HALF = NZ * ROWS
 CTXL = 2048
 SLAB = 256
-RB = 384
+RB = 512
 NRB = HALF // RB
 SLOTS = 12
 STEPR = 24
@@ -31,6 +31,9 @@
 DSTAT = DECR + STEPR
 TAIL = 64
 XROWS = HALF + TAIL
+NS = NZ // 2
+KEEP = NS * ROWS
+MROWS = KEEP + TAIL
 ZROWS = ROWS + TAIL
 DEC = 32
 
@@ -184,56 +187,96 @@
     return [e * inv for e in es], top + jnp.log2(den)
 
 
-def pair_kernel(a_ref, b_ref, z_ref, t_ref):
-    la, da, sa = get_stats(a_ref[HALF:, :])
-    lb, db, sb = get_stats(b_ref[HALF:, :])
-    (wa, wb), lse = merge_weights([la, lb])
+def merge_stats(a, b, t_ref, w_ref):
+    la, da, sa = get_stats(a)
+    lb, db, sb = get_stats(b)
+    (wa, _), lse = merge_weights([la, lb])
     (ua, ub), sd = merge_weights([sa, sb])
-    put_stats(t_ref, lse, da * column(ua)[0:STEPR] + db * column(ub)[0:STEPR], sd)
+    dec = da * column(ua)[0:STEPR] + db * column(ub)[0:STEPR]
+    put_stats(t_ref, lse, dec, sd)
+    w_ref[0:LR, 0, :] = wa
+    w_ref[LR, 0, :] = jnp.zeros((HD,), F32)
+    return lse, dec, sd
+
+
+def mix(a_ref, b_ref, w_ref, k, owner):
+    first = owner * ROWS
+    both = jnp.concatenate([w_ref[first // HD], w_ref[first // HD + 1]], axis=1)
+    share = column(pltpu.roll(both, (2 * HD - first % HD) % (2 * HD), 1)[0:1, 0:HD])[0:ROWS]
+    a = a_ref[k * ROWS : (k + 1) * ROWS, :].astype(F32)
+    b = b_ref[k * ROWS : (k + 1) * ROWS, :].astype(F32)
+    return b + (a - b) * share
+
+
+def pair_kernel(info_ref, a_ref, b_ref, keep_ref, give_ref, t_ref, w_ref):
+    merge_stats(a_ref[HALF:, :], b_ref[HALF:, :], t_ref, w_ref)
     tail = t_ref[...].astype(BF)
-    for n in range(NZ):
-        z_ref[n, ROWS:, :] = tail
-    for g in range(LR):
-        rows = slice(g * HD, (g + 1) * HD)
-        mixed = a_ref[rows, :].astype(F32) * column(wa[g : g + 1]) + b_ref[rows, :].astype(F32) * column(wb[g : g + 1])
-        mixed = mixed.astype(BF)
-        for j in range(0, HD, 32):
-            n, at = divmod(g * HD + j, ROWS)
-            z_ref[n, at : at + 32, :] = mixed[j : j + 32]
-
-
-def pair_merge(a, b):
+    keep_ref[KEEP:, :] = tail
+    give_ref[KEEP:, :] = tail
+    odd = info_ref[2] % 2 > 0
+    for k in range(NS):
+        even_rows = mix(a_ref, b_ref, w_ref, 2 * k, 2 * k).astype(BF)
+        odd_rows = mix(a_ref, b_ref, w_ref, 2 * k + 1, 2 * k + 1).astype(BF)
+        rows = slice(k * ROWS, (k + 1) * ROWS)
+        keep_ref[rows, :] = jnp.where(odd, odd_rows, even_rows)
+        give_ref[rows, :] = jnp.where(odd, even_rows, odd_rows)
+
+
+def pair_merge(info, a, b):
+    half = jax.ShapeDtypeStruct((MROWS, HD), BF)
     return pl.pallas_call(
         pair_kernel,
-        out_shape=jax.ShapeDtypeStruct((NZ, ZROWS, HD), BF),
-        scratch_shapes=[pltpu.VMEM((TAIL, HD), F32)],
+        out_shape=(half, half),
+        in_specs=[pl.BlockSpec(memory_space=pltpu.SMEM)] + [pl.BlockSpec(memory_space=pltpu.VMEM)] * 2,
+        out_specs=[pl.BlockSpec(memory_space=pltpu.VMEM)] * 2,
+        scratch_shapes=[pltpu.VMEM((TAIL, HD), F32), pltpu.VMEM((LR + 1, 8, HD), F32)],
         compiler_params=params(),
         name="pair_merge",
-    )(a, b)
-
-
-def final_kernel(info_ref, r_ref, q_ref, nk_ref, nv_ref, slab_ref, lse_ref, step_ref, l_ref, w_ref):
-    stats = [get_stats(r_ref[s, ROWS:, :]) for s in range(NZ)]
+    )(info, a, b)
+
+
+def next_kernel(info_ref, a_ref, b_ref, after_ref, z_ref, t_ref, w_ref):
+    merge_stats(a_ref[KEEP:, :], b_ref[KEEP:, :], t_ref, w_ref)
+    tail = t_ref[...].astype(BF)
+    for k in range(NS):
+        z_ref[k, 0:ROWS, :] = mix(a_ref, b_ref, w_ref, k, 2 * k + info_ref[2] % 2).astype(BF)
+        z_ref[k, ROWS:, :] = tail
+
+
+def next_merge(info, a, b, after):
+    return pl.pallas_call(
+        next_kernel,
+        out_shape=jax.ShapeDtypeStruct((NS, ZROWS, HD), BF),
+        in_specs=[pl.BlockSpec(memory_space=pltpu.SMEM)] + [pl.BlockSpec(memory_space=pltpu.VMEM)] * 3,
+        out_specs=pl.BlockSpec(memory_space=pltpu.VMEM),
+        scratch_shapes=[pltpu.VMEM((TAIL, HD), F32), pltpu.VMEM((LR + 1, 8, HD), F32)],
+        compiler_params=params(),
+        name="next_merge",
+    )(info, a, b, after)
+
+
+def final_kernel(info_ref, r_ref, q_ref, nk_ref, nv_ref, after_ref, slab_ref, lse_ref, step_ref, l_ref, w_ref):
+    stats = [get_stats(r_ref[s, ROWS:, :]) for s in range(NS)]
     top = stats[0][0]
-    for s in range(1, NZ):
+    for s in range(1, NS):
         top = jnp.maximum(top, stats[s][0])
     den = jnp.zeros_like(top)
-    for s in range(NZ):
+    for s in range(NS):
         den = den + jnp.exp2(stats[s][0] - top)
         l_ref[0:LR, s, :] = stats[s][0]
         l_ref[LR, s, :] = jnp.zeros((HD,), F32)
     lse = top + jnp.log2(den)
     lse_ref[...] = lse
-    l_ref[0:LR, NZ, :] = lse
-    l_ref[LR, NZ, :] = jnp.zeros((HD,), F32)
+    l_ref[0:LR, NS, :] = lse
+    l_ref[LR, NS, :] = jnp.zeros((HD,), F32)
     first = info_ref[2] * ROWS
     both = jnp.concatenate([l_ref[first // HD], l_ref[first // HD + 1]], axis=1)
     own = pltpu.roll(both, (2 * HD - first % HD) % (2 * HD), 1)[:, 0:HD]
     w_ref[...] = jnp.zeros_like(w_ref)
-    w_ref[0:NZ, :] = jnp.exp2(own[0:NZ] - own[NZ : NZ + 1])
+    w_ref[0:NS, :] = jnp.exp2(own[0:NS] - own[NS : NS + 1])
     weights = w_ref[...].T
     total = jnp.zeros((ROWS, HD), F32)
-    for s in range(NZ):
+    for s in range(NS):
         total = total + r_ref[s, 0:ROWS, :].astype(F32) * weights[0:ROWS, s : s + 1]
     slab_ref[...] = total.astype(BF)
     fresh = scores_t(nk_ref[...], q_ref[...]) * C2
@@ -241,17 +284,17 @@
     first_new = fresh[0:1]
     second_new = jnp.where(lane % 2 == 1, fresh[1:2], NEG)
     us, _ = merge_weights([t[2] for t in stats] + [first_new, second_new])
-    for s in range(NZ + 2):
+    for s in range(NS + 2):
         w_ref[s : s + 1, :] = us[s]
     shares = w_ref[...].T
     nv = nv_ref[...].astype(F32)
-    out = shares[0:STEPR, NZ : NZ + 1] * nv[0:1] + shares[0:STEPR, NZ + 1 : NZ + 2] * nv[1:2]
-    for s in range(NZ):
+    out = shares[0:STEPR, NS : NS + 1] * nv[0:1] + shares[0:STEPR, NS + 1 : NS + 2] * nv[1:2]
+    for s in range(NS):
         out = out + stats[s][1] * shares[0:STEPR, s : s + 1]
     step_ref[...] = out.astype(BF)
 
 
-def final_merge(info, r, q, nk, nv):
+def final_merge(info, r, q, nk, nv, after):
     return pl.pallas_call(
         final_kernel,
         out_shape=(
@@ -259,12 +302,12 @@
             jax.ShapeDtypeStruct((LR, HD), F32),
             jax.ShapeDtypeStruct((STEPR, HD), BF),
         ),
-        in_specs=[pl.BlockSpec(memory_space=pltpu.SMEM)] + [pl.BlockSpec(memory_space=pltpu.VMEM)] * 4,
+        in_specs=[pl.BlockSpec(memory_space=pltpu.SMEM)] + [pl.BlockSpec(memory_space=pltpu.VMEM)] * 5,
         out_specs=[pl.BlockSpec(memory_space=pltpu.VMEM)] * 3,
-        scratch_shapes=[pltpu.VMEM((LR + 1, 24, HD), F32), pltpu.VMEM((HD, HD), F32)],
+        scratch_shapes=[pltpu.VMEM((LR + 1, 16, HD), F32), pltpu.VMEM((HD, HD), F32)],
         compiler_params=params(),
         name="final_merge",
-    )(info, r, q, nk, nv)
+    )(info, r, q, nk, nv, after)
 
 
 def heavy_kernel(other, info_ref, q_ref, k_ref, lse_ref, prev_ref, h_ref, acc_ref):
@@ -283,15 +326,14 @@
         if c == CTXL // SLAB - 1:
             s = masked_tail(info_ref, info_ref[1] ^ other, i, s)
         w = jnp.exp2(s * C2 - lse)
-        acc_ref[keys, :] += w[:, 0:128] + w[:, 128:256] + w[:, 256:384]
+        acc_ref[keys, :] += (w[:, 0:128] + w[:, 128:256]) + (w[:, 256:384] + w[:, 384:512])
 
     @pl.when(i == NRB - 1)
     def _():
-        ones = jnp.ones((8, 128), F32)
-        sums = lax.dot_general(
-            ones, acc_ref[...], (((1,), (1,)), ((), ())), precision=lax.Precision.HIGHEST, preferred_element_type=F32
-        )
-        h_ref[...] = sums[0:1] * (NCTX * CTXL / (12 * SLAB)) + prev_ref[...]
+        for t in range(CTXL // HD):
+            at = slice(t * HD, (t + 1) * HD)
+            sums = jnp.sum(acc_ref[at, :].T, axis=0, keepdims=True)
+            h_ref[:, at] = sums * (NCTX * CTXL / (12 * SLAB)) + prev_ref[:, at]
 
 
 def heavy(other, info, q, kv, lse, prev):
@@ -340,21 +382,6 @@
     )(pick, blocks)
 
 
-def after_kernel(x_ref, after_ref, out_ref):
-    del x_ref, after_ref, out_ref
-
-
-def after(x, other):
-    return pl.pallas_call(
-        after_kernel,
-        out_shape=jax.ShapeDtypeStruct(x.shape, x.dtype),
-        in_specs=[pl.BlockSpec(memory_space=pl.ANY)] * 2,
-        out_specs=pl.BlockSpec(memory_space=pl.ANY),
-        input_output_aliases={0: 0},
-        name="after",
-    )(x, other)
-
-
 def select_kernel(src_ref, in_ref, out_ref, sems):
     copies = [
         pltpu.make_async_copy(in_ref.at[src_ref[r], n], out_ref.at[n, r], sems.at[n, r])
@@ -396,10 +423,14 @@
 SWAP = [(0, 1), (1, 0)]
 
 
+Z = ("zh", "zp")
+CTX = ("xl", "zh", "zp")
+
+
 def local(slab_query, kv_cache, kept_list, decode_place, step_query, step_cache):
     grp = lax.axis_index("grp")
     xl = lax.axis_index("xl")
-    z = lax.axis_index("z")
+    z = lax.axis_index("zh") * 2 + lax.axis_index("zp")
     ctx = xl * NZ + z
     per_dev = CTXL // BLK
 
@@ -425,50 +456,47 @@
     steps = jnp.pad(steps, ((0, HD - STEPR), (0, 0)))
     new = jnp.pad(step_cache[0, :, :, 0], ((0, 0), (0, 14), (0, 0)))
 
-    q_own = lax.all_to_all(spread(q), "z", 0, 0, tiled=True).reshape(HALF, HD)
+    q_own = lax.all_to_all(spread(q), Z, 0, 0, tiled=True).reshape(HALF, HD)
     kv_decode = lax.ppermute(kv, "grp", SWAP)
     blocks = kv_decode.reshape(2, per_dev, BLK, HD)
     dec = decode_partial(flags, steps, kv_decode)
 
-    outgoing = after(pack(pick, blocks), q_own)
-    arrived = lax.all_to_all(outgoing, ("xl", "z"), 0, 0, tiled=True)
+    arrived = lax.all_to_all(pack(pick, blocks), CTX, 0, 0, tiled=True)
     q_other = lax.ppermute(q_own, "xl", SWAP)
     part_own = flash(0, info, q_own, kv, dec)
     part_other = flash(1, info, q_other, kv, dec)
     part_partner = lax.ppermute(part_other, "xl", SWAP)
-    merged = after(pair_merge(part_own, part_partner), arrived)
-    received = lax.all_to_all(merged, "z", 0, 0, tiled=True)
-
-    slab, lse, step = final_merge(info, received, steps, new[0], new[1])
+    keep, give = pair_merge(info, part_own, part_partner)
+    merged = next_merge(info, keep, lax.ppermute(give, "zp", SWAP), arrived[0, 0, 0:16])
+    received = lax.all_to_all(merged, "zh", 0, 0, tiled=True)
+    paged = select(source, arrived)
+    slab, lse, step = final_merge(info, received, steps, new[0], new[1], paged[0, 0, 0:16])
     lse_other = lax.ppermute(lse, "xl", SWAP)
     columns = heavy(0, info, q_own, kv, lse, jnp.zeros((1, CTXL), F32))
     columns = heavy(1, info, q_other, kv, lse_other, columns)
 
-    paged = select(source, arrived)
-
     slab_out = jnp.transpose(slab.reshape(12, 8, HD), (1, 0, 2))[None, :, None]
     step_out = jnp.transpose(step.reshape(12, 2, HD), (1, 0, 2))[None, :, None]
     return (slab_out, columns[None], paged[None, None], step_out)
 
 
 def solution(mesh):
-    split = Mesh(mesh.devices.reshape(2, 2, NZ, 8), ("grp", "xl", "z", "kvh"))
-    ctx = ("xl", "z")
+    split = Mesh(mesh.devices.reshape(2, 2, NS, 2, 8), ("grp", "xl", "zh", "zp", "kvh"))
     return jax.shard_map(
         local,
         mesh=split,
         in_specs=(
-            P("grp", ctx, "kvh", None, None),
-            P("grp", None, ctx, "kvh", None),
+            P("grp", CTX, "kvh", None, None),
+            P("grp", None, CTX, "kvh", None),
             P(None, "kvh", None),
             P(None, "kvh", None),
             P("grp", None, "kvh", None, None),
             P("grp", None, None, "kvh", None),
         ),
         out_specs=(
-            P("grp", ctx, "kvh", None, None),
-            P("grp", "kvh", ctx),
-            P("grp", "kvh", None, ctx, None, None),
+            P("grp", CTX, "kvh", None, None),
+            P("grp", "kvh", CTX),
+            P("grp", "kvh", None, CTX, None, None),
             P("grp", None, "kvh", None, None),
         ),
         check_vma=False,

time: 202 us -> 194 us (0.960)
  waiting for transfers between devices: 111 us -> 104 us
  starting transfers between devices: 42.6 us -> 48.8 us
  local copies, waits for them, and re-layouts: 8.95 us -> 5.6 us
  Pallas kernels: 36 us -> 33.2 us
    all_to_all x3, waiting for transfers between devices: 98.7 us -> 87.4 us  [the longest x1 54.7 us: local(): arrived = lax.all_to_all(pack(pick, blocks), CTX, 0, 0, tiled=True)]
    unnamed x28 -> x20, local copies, waits for them, and re-layouts: 7.4 us -> 4.03 us
    pallas_call x2, Pallas kernels: 15.6 us -> 12.7 us  [flash(): pl.pallas_call(functools.partial(flash_kernel, other), out_shape=jax.Shap...]
    ppermute x0 -> x1, starting transfers between devices: none -> 2.69 us  [local(): lax.ppermute(give, 'zp', SWAP)]
    all_to_all x3, starting transfers between devices: 30.8 us -> 33.5 us  [the longest x1 15.2 us: local(): q_own = lax.all_to_all(spread(q), Z, 0, 0, tiled=True).reshape(HALF, HD)]
    ppermute x0 -> x1, waiting for transfers between devices: none -> 2.03 us  [local(): lax.ppermute(give, 'zp', SWAP)]
  transfers between devices with their start and end apart: 7 -> 8, of which waited for: 6 -> 7; matrix products, arithmetic and copies ran while one was open for 1% -> 1% of each run, Pallas kernels for 14% -> 13%
where the time goes in v3:
time: 194 us; the launch traced here: 193 us
  waiting for transfers between devices  104 us (54%)
  starting transfers between devices  48.8 us (25%)
  Pallas kernels  33.2 us (17%)
  local copies, waits for them, and re-layouts  5.6 us (3%)
    all_to_all x1, waiting for transfers between devices, local(): arrived = lax.all_to_all(pack(pick, blocks), CTX, 0, 0, tiled=True)  54.7 us
    all_to_all x1, waiting for transfers between devices, local(): received = lax.all_to_all(merged, 'zh', 0, 0, tiled=True)  19 us
    all_to_all x1, starting transfers between devices, local(): q_own = lax.all_to_all(spread(q), Z, 0, 0, tiled=True).reshape(HALF, HD)  15.2 us
    all_to_all x1, waiting for transfers between devices, local(): q_own = lax.all_to_all(spread(q), Z, 0, 0, tiled=True).reshape(HALF, HD)  13.6 us
    pallas_call x2, Pallas kernels, flash(): pl.pallas_call(functools.partial(flash_kernel, other), out_shape=jax.Shap...  12.7 us
    all_to_all x1, starting transfers between devices, local(): received = lax.all_to_all(merged, 'zh', 0, 0, tiled=True)  11.1 us
    ppermute x1, waiting for transfers between devices, local(): q_other = lax.ppermute(q_own, 'xl', SWAP)  8.48 us
    pallas_call x2, Pallas kernels, heavy(): pl.pallas_call(functools.partial(heavy_kernel, other), out_shape=jax.Shap...  7.28 us
  transfers between devices with their start and end apart: 8, of which 7 were waited for; matrix products, arithmetic and copies ran while one was open for 1% of the time, Pallas kernels for 13%

profile of v3, /device:TPU:24, one launch (start us, length us, event | category | flops | bytes accessed | tf_op | source)
XLA Modules:
  0.0 193.2 jit_solution(2944043571134788386)
XLA Ops:
  0.6 0.0 copy-start.3
  0.6 0.7 copy-done.3
  1.4 0.8 spread_queries.1
  2.2 15.2 %all-to-all-start = ((bf16[16,96,128]{2,1,0:T(8,128)(2,1)}), bf16[16,96,128]{2,1,0:T(8,128)(2,1)S(1)}, u32[]{:S(2)}, u32[]{:S(2)}) async-start(bf16[16,96,128]{2,1,0:T(8,128)(2,1)} %spread_queries.1), calls=%async_computation | async-start | bytes 786432 | tf_op jit(solution)/shard_map/all_to_all | solution.py:459
  17.4 1.9 collective-permute-start
  19.3 0.7 dynamic-slice_reduce_fusion.1
  20.0 0.1 select_reduce_fusion
  20.2 2.0 %collective-permute-done.k_ref.v_ref = bf16[2,2048,128]{2,1,0:T(8,128)(2,1)S(1)} collective-permute-done((bf16[2,2048,128]{2,1,0:T(8,128)(2,1)}, bf16[2,2048,128]{2,1,0:T(8,128)(2,1)S(1)}, u32[]{:S(2)}, u32[]{:S(2)}) %collective-permute-start) | collective-permute-done | bytes 1048608 | tf_op jit(solution)/shard_map/ppermute | solution.py:460
  22.1 4.0 %pack_blocks.1 = bf16[32,2,128,128]{3,2,1,0:T(8,128)(2,1)S(1)} custom-call(s32[32]{0:T(128)S(1)} %broadcast_clamp_fusion.1.pick_ref, bf16[2,16,128,128]{3,2,1,0:T(8,128)(2,1)S(1)} %bitcast.37), custom_call_target="tpu_custom_call" | custom-call | tf_op jit(solution)/shard_map/pack_blocks/pallas_call | solution.py:374
  26.2 0.0 copy-start
  26.2 1.3 copy-done
  27.5 13.6 %all-to-all-done = bf16[16,96,128]{2,1,0:T(8,128)(2,1)S(1)} async-done(((bf16[16,96,128]{2,1,0:T(8,128)(2,1)}), bf16[16,96,128]{2,1,0:T(8,128)(2,1)S(1)}, u32[]{:S(2)}, u32[]{:S(2)}) %all-to-all-start) | async-done | bytes 393248 | tf_op jit(solution)/shard_map/all_to_all | solution.py:459
  41.1 7.2 %all-to-all-start.1 = ((bf16[32,2,128,128]{3,2,1,0:T(8,128)(2,1)}), bf16[32,2,128,128]{3,2,1,0:T(8,128)(2,1)S(1)}, u32[]{:S(2)}, u32[]{:S(2)}) async-start(bf16[32,2,128,128]{3,2,1,0:T(8,128)(2,1)} %copy-done), calls=%async_computation.1 | async-start | bytes 4194304 | tf_op jit(solution)/shard_map/all_to_all | solution.py:464
  48.4 0.0 copy-start.4
  48.4 3.8 %collective-permute-start.1 = (bf16[1536,128]{1,0:T(8,128)(2,1)S(1)}, bf16[1536,128]{1,0:T(8,128)(2,1)S(1)}, u32[]{:S(2)}, u32[]{:S(2)}) collective-permute-start(bf16[1536,128]{1,0:T(8,128)(2,1)S(1)} %bitcast.38), channel_id=1, source_target_pairs={{0,128},{128,0},{1,129},{129,1},{2,130},{130,2},{3,131},{131,3},{4... | collective-permute-start | bytes 1179656 | tf_op jit(solution)/shard_map/ppermute | solution.py:465
  52.2 0.7 pad.8.q_ref
  52.9 0.0 copy-start.1
  52.9 0.1 pad_add_fusion.info_ref
  53.0 0.1 convert_reduce_fusion.flag_ref
  53.1 1.5 decode_partial.1.d_ref
  54.6 0.0 copy-done.1
  54.6 8.5 %collective-permute-done.1.q_ref = bf16[1536,128]{1,0:T(8,128)(2,1)S(1)} collective-permute-done((bf16[1536,128]{1,0:T(8,128)(2,1)S(1)}, bf16[1536,128]{1,0:T(8,128)(2,1)S(1)}, u32[]{:S(2)}, u32[]{:S(2)}) %collective-permute-start.1) | collective-permute-done | bytes 393248 | tf_op jit(solution)/shard_map/ppermute | solution.py:465
  63.1 0.0 copy-done.4
  63.1 6.3 %slab_partial.3 = bf16[1600,128]{1,0:T(8,128)(2,1)S(1)} custom-call(s32[3]{0:T(128)S(1)} %pad_add_fusion.info_ref, bf16[1536,128]{1,0:T(8,128)(2,1)S(1)} %collective-permute-done.1.q_ref, bf16[2,2048,128]{2,1,0:T(8,128)(2,1)S(1)} %bitcast.43, bf16[2,2048,128]{2,1,0:T(8,128)(2,1)S(1)} %bitcast.44, f32[32,128]{1,0:T(8,128)S(1)} %decode_partial.1.d_ref), custom_call_target="tpu_custom_call" | custom-call | flops 1610612736 | bytes 1048576 | tf_op jit(solution)/shard_map/slab_partial/pallas_call | solution.py:114
  69.5 0.0 copy-start.6
  69.5 0.7 copy-done.6
  70.2 3.2 %collective-permute-start.2 = (bf16[1600,128]{1,0:T(8,128)(2,1)S(1)}, bf16[1600,128]{1,0:T(8,128)(2,1)S(1)}, u32[]{:S(2)}, u32[]{:S(2)}) collective-permute-start(bf16[1600,128]{1,0:T(8,128)(2,1)S(1)} %slab_partial.3), channel_id=1, source_target_pairs={{0,128},{128,0},{1,129},{129,1},{2,130},{130,2},{3,131},{131,3},{4... | collective-permute-start | bytes 1228808 | tf_op jit(solution)/shard_map/ppermute | solution.py:468
  73.4 6.3 %slab_partial.2.a_ref = bf16[1600,128]{1,0:T(8,128)(2,1)S(1)} custom-call(s32[3]{0:T(128)S(1)} %pad_add_fusion.info_ref, bf16[1536,128]{1,0:T(8,128)(2,1)S(1)} %bitcast.39, bf16[2,2048,128]{2,1,0:T(8,128)(2,1)S(1)} %bitcast.45, bf16[2,2048,128]{2,1,0:T(8,128)(2,1)S(1)} %bitcast.46, f32[32,128]{1,0:T(8,128)S(1)} %decode_partial.1.d_ref), custom_call_target="tpu_custom_call" | custom-call | flops 1610612736 | bytes 1048576 | tf_op jit(solution)/shard_map/slab_partial/pallas_call | solution.py:114
  79.8 0.0 copy-start.8
  79.8 0.0 copy-start.9
  79.8 3.7 %collective-permute-done.2.b_ref = bf16[1600,128]{1,0:T(8,128)(2,1)S(1)} collective-permute-done((bf16[1600,128]{1,0:T(8,128)(2,1)S(1)}, bf16[1600,128]{1,0:T(8,128)(2,1)S(1)}, u32[]{:S(2)}, u32[]{:S(2)}) %collective-permute-start.2) | collective-permute-done | bytes 409632 | tf_op jit(solution)/shard_map/ppermute | solution.py:468
  83.6 1.0 pair_merge.1
  84.6 2.7 %collective-permute-start.3 = (bf16[832,128]{1,0:T(8,128)(2,1)S(1)}, bf16[832,128]{1,0:T(8,128)(2,1)S(1)}, u32[]{:S(2)}, u32[]{:S(2)}) collective-permute-start(bf16[832,128]{1,0:T(8,128)(2,1)S(1)} %get-tuple-element.10), channel_id=1, source_target_pairs={{0,8},{8,0},{1,9},{9,1},{2,10},{10,2},{3,11},{11,3},{4,12},{12,4},... | collective-permute-start | bytes 638984 | tf_op jit(solution)/shard_map/ppermute | solution.py:470
  87.3 54.7 %all-to-all-done.1.in_ref = bf16[32,2,128,128]{3,2,1,0:T(8,128)(2,1)S(1)} async-done(((bf16[32,2,128,128]{3,2,1,0:T(8,128)(2,1)}), bf16[32,2,128,128]{3,2,1,0:T(8,128)(2,1)S(1)}, u32[]{:S(2)}, u32[]{:S(2)}) %all-to-all-start.1) | async-done | bytes 2097184 | tf_op jit(solution)/shard_map/all_to_all | solution.py:464
  142.0 2.0 %collective-permute-done.3.b_ref = bf16[832,128]{1,0:T(8,128)(2,1)S(1)} collective-permute-done((bf16[832,128]{1,0:T(8,128)(2,1)S(1)}, bf16[832,128]{1,0:T(8,128)(2,1)S(1)}, u32[]{:S(2)}, u32[]{:S(2)}) %collective-permute-start.3) | collective-permute-done | bytes 213024 | tf_op jit(solution)/shard_map/ppermute | solution.py:470
  144.0 0.0 copy-start.2
  144.0 1.6 next_merge.1
  145.6 11.1 %all-to-all-start.2 = ((bf16[8,160,128]{2,1,0:T(8,128)(2,1)}), bf16[8,160,128]{2,1,0:T(8,128)(2,1)S(1)}, u32[]{:S(2)}, u32[]{:S(2)}) async-start(bf16[8,160,128]{2,1,0:T(8,128)(2,1)} %next_merge.1), calls=%async_computation.2 | async-start | bytes 655360 | tf_op jit(solution)/shard_map/all_to_all | solution.py:471
  156.7 0.1 reshape_squeeze.3
  156.7 0.0 copy-done.8
  156.8 0.1 eq.51
  156.9 0.0 copy-done.9
  156.9 0.1 fusion.3
  157.0 2.7 %select_slots.1 = bf16[2,12,128,128]{3,2,1,0:T(8,128)(2,1)} custom-call(s32[12]{0:T(128)S(1)} %broadcast_clamp_fusion.src_ref, bf16[32,2,128,128]{3,2,1,0:T(8,128)(2,1)S(1)} %all-to-all-done.1.in_ref), custom_call_target="tpu_custom_call" | custom-call | tf_op jit(solution)/shard_map/select_slots/pallas_call | solution.py:398
  159.7 0.7 slice_bitcast_fusion.after_ref
  160.4 19.0 %all-to-all-done.2.r_ref = bf16[8,160,128]{2,1,0:T(8,128)(2,1)S(1)} async-done(((bf16[8,160,128]{2,1,0:T(8,128)(2,1)}), bf16[8,160,128]{2,1,0:T(8,128)(2,1)S(1)}, u32[]{:S(2)}, u32[]{:S(2)}) %all-to-all-start.2) | async-done | bytes 327712 | tf_op jit(solution)/shard_map/all_to_all | solution.py:471
  179.4 0.0 copy-done.2
  179.4 1.7 final_merge.1
  181.0 3.6 %collective-permute-start.4 = (f32[12,128]{1,0:T(8,128)S(1)}, f32[12,128]{1,0:T(8,128)S(1)}, u32[]{:S(2)}, u32[]{:S(2)}) collective-permute-start(f32[12,128]{1,0:T(8,128)S(1)} %get-tuple-element.12.lse_ref), channel_id=1, source_target_pairs={{0,128},{128,0},{1,129},{129,1},{2,130},{130,2},{3,131},{131,3},{4... | collective-permute-start | bytes 18440 | tf_op jit(solution)/shard_map/ppermute | solution.py:474
  184.7 0.0 copy-start.5
  184.7 1.2 copy-done.5
  185.9 0.0 copy-start.7
  185.9 3.3 %heavy_columns.2.prev_ref = f32[1,2048]{1,0:T(1,128)S(1)} custom-call(s32[3]{0:T(128)S(1)} %pad_add_fusion.info_ref, bf16[1536,128]{1,0:T(8,128)(2,1)S(1)} %bitcast.40, bf16[2,2048,128]{2,1,0:T(8,128)(2,1)S(1)} %bitcast.47, f32[12,128]{1,0:T(8,128)S(1)} %get-tuple-element.12.lse_ref, f32[1,2048]{1,0:T(1,128)S(1)} %broadcast_in_dim.37.prev_ref), custom_call_target="tpu_custom_call" | custom-call | flops 805306368 | bytes 524288 | tf_op jit(solution)/shard_map/heavy_columns/pallas_call | solution.py:340
  189.3 0.0 collective-permute-done.4.lse_ref
  189.3 0.0 copy-done.7
  189.3 4.0 %heavy_columns.3 = f32[1,2048]{1,0:T(1,128)} custom-call(s32[3]{0:T(128)S(1)} %pad_add_fusion.info_ref, bf16[1536,128]{1,0:T(8,128)(2,1)S(1)} %copy-done.7, bf16[2,2048,128]{2,1,0:T(8,128)(2,1)S(1)} %bitcast.48, f32[12,128]{1,0:T(8,128)S(1)} %collective-permute-done.4.lse_ref, f32[1,2048]{1,0:T(1,128)S(1)} %heavy_columns.2.prev_ref), custom_call_target="tpu_custom_call" | custom-call | flops 805306368 | bytes 524288 | tf_op jit(solution)/shard_map/heavy_columns/pallas_call | solution.py:340
  (7 shorter events, 0.1 us)
Async XLA Ops:
  0.6 0.7 copy-start.3
  2.2 39.0 %all-to-all-start = ((bf16[16,96,128]{2,1,0:T(8,128)(2,1)}), bf16[16,96,128]{2,1,0:T(8,128)(2,1)S(1)}, u32[]{:S(2)}, u32[]{:S(2)}) async-start(bf16[16,96,128]{2,1,0:T(8,128)(2,1)} %spread_queries.1), calls=%async_computation | async-start | bytes 786432 | tf_op jit(solution)/shard_map/all_to_all | solution.py:459
  17.4 4.8 %collective-permute-start = (bf16[2,2048,128]{2,1,0:T(8,128)(2,1)}, bf16[2,2048,128]{2,1,0:T(8,128)(2,1)S(1)}, u32[]{:S(2)}, u32[]{:S(2)}) collective-permute-start(bf16[2,2048,128]{2,1,0:T(8,128)(2,1)} %bitcast.42), channel_id=1, source_target_pairs={{0,256},{256,0},{1,257},{257,1},{2,258},{258,2},{3,259},{259,3},{4... | collective-permute-start | bytes 3145736 | tf_op jit(solution)/shard_map/ppermute | solution.py:460
  26.2 1.3 copy-start
  41.1 100.9 %all-to-all-start.1 = ((bf16[32,2,128,128]{3,2,1,0:T(8,128)(2,1)}), bf16[32,2,128,128]{3,2,1,0:T(8,128)(2,1)S(1)}, u32[]{:S(2)}, u32[]{:S(2)}) async-start(bf16[32,2,128,128]{3,2,1,0:T(8,128)(2,1)} %copy-done), calls=%async_computation.1 | async-start | bytes 4194304 | tf_op jit(solution)/shard_map/all_to_all | solution.py:464
  48.4 14.8 %copy-start.4 = (bf16[1,2,2048,1,128]{4,2,3,1,0:T(8,128)(2,1)S(1)}, bf16[1,2,2048,1,128]{4,2,3,1,0:T(8,128)(2,1)}, u32[]{:S(2)}) copy-start(bf16[1,2,2048,1,128]{4,2,3,1,0:T(8,128)(2,1)} %param.7) | copy-start | bytes 3145732
  48.4 14.8 %collective-permute-start.1 = (bf16[1536,128]{1,0:T(8,128)(2,1)S(1)}, bf16[1536,128]{1,0:T(8,128)(2,1)S(1)}, u32[]{:S(2)}, u32[]{:S(2)}) collective-permute-start(bf16[1536,128]{1,0:T(8,128)(2,1)S(1)} %bitcast.38), channel_id=1, source_target_pairs={{0,128},{128,0},{1,129},{129,1},{2,130},{130,2},{3,131},{131,3},{4... | collective-permute-start | bytes 1179656 | tf_op jit(solution)/shard_map/ppermute | solution.py:465
  52.9 1.7 copy-start.1
  69.5 0.7 copy-start.6
  70.2 13.4 %collective-permute-start.2 = (bf16[1600,128]{1,0:T(8,128)(2,1)S(1)}, bf16[1600,128]{1,0:T(8,128)(2,1)S(1)}, u32[]{:S(2)}, u32[]{:S(2)}) collective-permute-start(bf16[1600,128]{1,0:T(8,128)(2,1)S(1)} %slab_partial.3), channel_id=1, source_target_pairs={{0,128},{128,0},{1,129},{129,1},{2,130},{130,2},{3,131},{131,3},{4... | collective-permute-start | bytes 1228808 | tf_op jit(solution)/shard_map/ppermute | solution.py:468
  79.8 76.9 %copy-start.8 = (s32[2,1,384]{2,1,0:T(1,128)S(1)}, s32[2,1,384]{2,1,0:T(1,128)}, u32[]{:S(2)}) copy-start(s32[2,1,384]{2,1,0:T(1,128)} %param.9) | copy-start | bytes 9220
  79.8 77.0 %copy-start.9 = (bf16[1,2,2,1,128]{4,2,3,1,0:T(2,128)(2,1)S(1)}, bf16[1,2,2,1,128]{4,2,3,1,0:T(2,128)(2,1)}, u32[]{:S(2)}) copy-start(bf16[1,2,2,1,128]{4,2,3,1,0:T(2,128)(2,1)} %param.11) | copy-start | bytes 3076
  84.6 59.5 %collective-permute-start.3 = (bf16[832,128]{1,0:T(8,128)(2,1)S(1)}, bf16[832,128]{1,0:T(8,128)(2,1)S(1)}, u32[]{:S(2)}, u32[]{:S(2)}) collective-permute-start(bf16[832,128]{1,0:T(8,128)(2,1)S(1)} %get-tuple-element.10), channel_id=1, source_target_pairs={{0,8},{8,0},{1,9},{9,1},{2,10},{10,2},{3,11},{11,3},{4,12},{12,4},... | collective-permute-start | bytes 638984 | tf_op jit(solution)/shard_map/ppermute | solution.py:470
  144.0 35.3 %copy-start.2 = (bf16[128,128]{1,0:T(8,128)(2,1)S(1)}, bf16[128,128]{1,0:T(8,128)(2,1)}, u32[]{:S(2)}) copy-start(bf16[128,128]{1,0:T(8,128)(2,1)} %copy-done.1) | copy-start | bytes 98308
  145.6 33.8 %all-to-all-start.2 = ((bf16[8,160,128]{2,1,0:T(8,128)(2,1)}), bf16[8,160,128]{2,1,0:T(8,128)(2,1)S(1)}, u32[]{:S(2)}, u32[]{:S(2)}) async-start(bf16[8,160,128]{2,1,0:T(8,128)(2,1)} %next_merge.1), calls=%async_computation.2 | async-start | bytes 655360 | tf_op jit(solution)/shard_map/all_to_all | solution.py:471
  181.0 8.2 %collective-permute-start.4 = (f32[12,128]{1,0:T(8,128)S(1)}, f32[12,128]{1,0:T(8,128)S(1)}, u32[]{:S(2)}, u32[]{:S(2)}) collective-permute-start(f32[12,128]{1,0:T(8,128)S(1)} %get-tuple-element.12.lse_ref), channel_id=1, source_target_pairs={{0,128},{128,0},{1,129},{129,1},{2,130},{130,2},{3,131},{131,3},{4... | collective-permute-start | bytes 18440 | tf_op jit(solution)/shard_map/ppermute | solution.py:474
  184.7 1.2 copy-start.5
  185.9 3.3 %copy-start.7 = (bf16[1536,128]{1,0:T(8,128)(2,1)S(1)}, bf16[1536,128]{1,0:T(8,128)(2,1)}, u32[]{:S(2)}) copy-start(bf16[1536,128]{1,0:T(8,128)(2,1)} %copy-done.6) | copy-start | bytes 1179652

commit v4 on v2

v4 whole, which is shorter than its diff:
```python
import functools
import math

import jax
import jax.numpy as jnp
from jax import lax
from jax.experimental import pallas as pl
from jax.experimental.pallas import tpu as pltpu
from jax.sharding import Mesh
from jax.sharding import PartitionSpec as P

BLK = 128
HD = 128
NZ = 16
NCTX = 32
ROWS = 96
HALF = NZ * ROWS
CTXL = 2048
SLAB = 256
RB = 512
NRB = HALF // RB
SLOTS = 12
STEPR = 24
NEG = -1e30
C2 = math.log2(math.e) / math.sqrt(HD)
BF = jnp.bfloat16
F32 = jnp.float32

LR = HALF // HD
NQ = 4
QROWS = NZ // NQ * ROWS
FIRST = 32
DECR = 6 * LR
DSTAT = DECR + STEPR
TAIL = 112
DEC = 32


def params(mib=40):
    return pltpu.CompilerParams(vmem_limit_bytes=mib * 1024 * 1024)


def parts_of(x):
    hi = x.astype(BF).astype(F32)
    mid = (x - hi).astype(BF).astype(F32)
    return hi, mid, x - hi - mid


def column(row):
    return jnp.broadcast_to(row, (128, 128)).T


def scores_t(k, q):
    return lax.dot_general(k, q, (((1,), (1,)), ((), ())), preferred_element_type=F32)


def masked_tail(info_ref, half, i, tail):
    key = lax.broadcasted_iota(jnp.int32, tail.shape, 0)
    row = lax.broadcasted_iota(jnp.int32, tail.shape, 1) + i * RB
    token = half * (SLAB // 2) + (row // ROWS) * 8 + row % 8
    seen = (key <= token) | (info_ref[0] < NCTX - 1)
    return jnp.where(seen, tail, NEG)


def fill_vt(v, vt_ref):
    vt_ref[0:HD, :] = v.astype(F32).T.astype(BF)
    vt_ref[HD:, :] = jnp.ones((16, CTXL), BF)


def put_tail(t_ref, lses, dec, dec_lse):
    for m, lse in enumerate(lses):
        for n, part in enumerate(parts_of(lse)):
            t_ref[(3 * m + n) * LR : (3 * m + n + 1) * LR, :] = part
    t_ref[DECR:DSTAT, :] = dec
    for n, part in enumerate(parts_of(dec_lse)):
        t_ref[DSTAT + n : DSTAT + n + 1, :] = part
    t_ref[DSTAT + 3 :, :] = jnp.zeros((TAIL - DSTAT - 3, HD), F32)


def get_tail(t):
    t = t.astype(F32)
    lses = [sum(t[(3 * m + n) * LR : (3 * m + n + 1) * LR] for n in range(3)) for m in range(2)]
    dec_lse = t[DSTAT : DSTAT + 1] + t[DSTAT + 1 : DSTAT + 2] + t[DSTAT + 2 : DSTAT + 3]
    return lses, t[DECR:DSTAT], dec_lse


def flash_kernel(other, info_ref, q_ref, k_ref, v_ref, after_ref, x_ref, lse_ref, vt_ref, s_ref):
    i = pl.program_id(0)

    @pl.when(i == 0)
    def _():
        fill_vt(v_ref[0], vt_ref)

    s_ref[...] = scores_t(k_ref[0], q_ref[...])
    s_ref[CTXL - SLAB :, :] = masked_tail(info_ref, info_ref[1] ^ other, i, s_ref[CTXL - SLAB :, :])
    top = jnp.max(s_ref[...], axis=0, keepdims=True)
    p = jnp.exp2((s_ref[...] - top) * C2).astype(BF)
    acc = jnp.dot(vt_ref[...], p, preferred_element_type=F32)
    mass = acc[HD : HD + 1]
    x_ref[...] = (acc[0:HD] * (1.0 / mass)).T.astype(BF)
    lse = top * C2 + jnp.log2(mass)
    for j in range(RB // HD):
        lse_ref[pl.ds(i * (RB // HD) + j, 1), :] = lse[:, j * HD : (j + 1) * HD]


def flash(other, info, q, kv, after):
    return pl.pallas_call(
        functools.partial(flash_kernel, other),
        out_shape=(jax.ShapeDtypeStruct((HALF, HD), BF), jax.ShapeDtypeStruct((LR, HD), F32)),
        grid=(NRB,),
        in_specs=[
            pl.BlockSpec(memory_space=pltpu.SMEM),
            pl.BlockSpec((RB, HD), lambda i: (i, 0)),
            pl.BlockSpec((1, CTXL, HD), lambda i: (0, 0, 0)),
            pl.BlockSpec((1, CTXL, HD), lambda i: (1, 0, 0)),
            pl.BlockSpec((8, HD), lambda i: (0, 0)),
        ],
        out_specs=(pl.BlockSpec((RB, HD), lambda i: (i, 0)), pl.BlockSpec((LR, HD), lambda i: (0, 0))),
        scratch_shapes=[pltpu.VMEM((HD + 16, CTXL), BF), pltpu.VMEM((CTXL, RB), F32)],
        compiler_params=params(),
        cost_estimate=pl.CostEstimate(
            flops=20000000000, bytes_accessed=2 * CTXL * HD * 2, transcendentals=HALF * CTXL
        ),
        name="slab_partial",
    )(info, q, kv, kv, after)


def decode_kernel(flag_ref, q_ref, k_ref, v_ref, d_ref, vt_ref, s_ref):
    fill_vt(v_ref[0], vt_ref)
    for b in range(CTXL // BLK):
        s = scores_t(k_ref[0, b * BLK : (b + 1) * BLK, :], q_ref[...])
        kept = jnp.broadcast_to(flag_ref[b], s.shape) > 0
        s_ref[b * BLK : (b + 1) * BLK, :] = jnp.where(kept, s, NEG)
    top = jnp.max(s_ref[...], axis=0, keepdims=True)
    p = jnp.exp2((s_ref[...] - top) * C2).astype(BF)
    acc = jnp.dot(vt_ref[...], p, preferred_element_type=F32)
    mass = acc[HD : HD + 1]
    out = (acc[0:HD] * (1.0 / mass)).T
    lse = jnp.maximum(top * C2 + jnp.log2(mass), NEG)
    d_ref[...] = jnp.zeros_like(d_ref)
    d_ref[0:STEPR, :] = out[0:STEPR]
    d_ref[STEPR : STEPR + 1, :] = lse


def decode_partial(flags, q, kv):
    return pl.pallas_call(
        decode_kernel,
        out_shape=jax.ShapeDtypeStruct((DEC, HD), F32),
        grid=(1,),
        in_specs=[
            pl.BlockSpec(memory_space=pltpu.SMEM),
            pl.BlockSpec((HD, HD), lambda i: (0, 0)),
            pl.BlockSpec((1, CTXL, HD), lambda i: (0, 0, 0)),
            pl.BlockSpec((1, CTXL, HD), lambda i: (1, 0, 0)),
        ],
        out_specs=pl.BlockSpec((DEC, HD), lambda i: (0, 0)),
        scratch_shapes=[
            pltpu.VMEM((HD + 16, CTXL), BF),
            pltpu.VMEM((CTXL, HD), F32),
        ],
        compiler_params=params(),
        name="decode_partial",
    )(flags, q, kv, kv)


def merge_weights(lses):
    top = lses[0]
    for x in lses[1:]:
        top = jnp.maximum(top, x)
    es = [jnp.exp2(x - top) for x in lses]
    den = es[0]
    for e in es[1:]:
        den = den + e
    inv = 1.0 / den
    return [e * inv for e in es], top + jnp.log2(den)


def merge_tails(tails, t_ref):
    shares, lse = merge_weights([t[0][0] for t in tails])
    _, lse_other = merge_weights([t[0][1] for t in tails])
    dec_shares, dec_lse = merge_weights([t[2] for t in tails])
    dec = sum(t[1] * column(u)[0:STEPR] for t, u in zip(tails, dec_shares))
    put_tail(t_ref, (lse, lse_other), dec, dec_lse)
    return shares, (lse, lse_other), dec, dec_lse


def put_shares(w_ref, shares):
    for n, share in enumerate(shares):
        w_ref[0:LR, n, :] = share
        w_ref[LR, n, :] = jnp.zeros((HD,), F32)


def mix(pieces, w_ref, owner):
    first = owner * ROWS
    both = jnp.concatenate([w_ref[first // HD], w_ref[first // HD + 1]], axis=1)
    own = pltpu.roll(both, (2 * HD - first % HD) % (2 * HD), 1)[:, 0:HD]
    return sum(piece.astype(F32) * column(own[n : n + 1])[0:ROWS] for n, piece in enumerate(pieces))


def pair_kernel(info_ref, a_ref, b_ref, lo_ref, la_ref, da_ref, sb_ref, m_ref, t_ref):
    mine = ((la_ref[...], lo_ref[...]), da_ref[0:STEPR, :], da_ref[STEPR : STEPR + 1, :])
    small = sb_ref[...]
    lse_b, lse_p = small[0:LR], small[16 : 16 + LR]
    theirs = ((lse_b, lse_p), small[32 : 32 + STEPR], small[32 + STEPR : 33 + STEPR])
    (wa, wb), _, _, _ = merge_tails([mine, theirs], t_ref)
    tail = t_ref[...].astype(BF)
    for s in range(NQ):
        m_ref[s, QROWS:, :] = tail
    zl = info_ref[2] % NQ
    for g in range(LR):
        rows = slice(g * HD, (g + 1) * HD)
        a, b = a_ref[rows, :].astype(F32), b_ref[rows, :].astype(F32)
        mixed = (a * column(wa[g : g + 1]) + b * column(wb[g : g + 1])).astype(BF)
        for j in range(0, HD, 32):
            n, at = divmod(g * HD + j, ROWS)
            at += n // NQ * ROWS
            m_ref[zl ^ (n % NQ), at : at + 32, :] = mixed[j : j + 32]


def pair_merge(info, *parts):
    return pl.pallas_call(
        pair_kernel,
        out_shape=jax.ShapeDtypeStruct((NQ, QROWS + TAIL, HD), BF),
        in_specs=[pl.BlockSpec(memory_space=pltpu.SMEM)] + [pl.BlockSpec(memory_space=pltpu.VMEM)] * 6,
        out_specs=pl.BlockSpec(memory_space=pltpu.VMEM),
        scratch_shapes=[pltpu.VMEM((TAIL, HD), F32)],
        compiler_params=params(),
        name="pair_merge",
    )(info, *parts)


def quad_kernel(info_ref, a_ref, b_ref, c_ref, d_ref, z_ref, t_ref, w_ref):
    refs = (a_ref, b_ref, c_ref, d_ref)
    shares, _, _, _ = merge_tails([get_tail(ref[QROWS:, :]) for ref in refs], t_ref)
    put_shares(w_ref, shares)
    tail = t_ref[...].astype(BF)
    zl, zh = info_ref[2] % NQ, info_ref[2] // NQ
    for k in range(NZ // NQ):
        rows = slice(k * ROWS, (k + 1) * ROWS)
        z_ref[zh ^ k, 0:ROWS, :] = mix([ref[rows, :] for ref in refs], w_ref, NQ * k + zl).astype(BF)
        z_ref[k, ROWS:, :] = tail


def quad_merge(info, parts):
    return pl.pallas_call(
        quad_kernel,
        out_shape=jax.ShapeDtypeStruct((NZ // NQ, ROWS + TAIL, HD), BF),
        in_specs=[pl.BlockSpec(memory_space=pltpu.SMEM)] + [pl.BlockSpec(memory_space=pltpu.VMEM)] * 4,
        out_specs=pl.BlockSpec(memory_space=pltpu.VMEM),
        scratch_shapes=[pltpu.VMEM((TAIL, HD), F32), pltpu.VMEM((LR + 1, 8, HD), F32)],
        compiler_params=params(),
        cost_estimate=pl.CostEstimate(flops=100000000000, bytes_accessed=1 << 20, transcendentals=0),
        name="quad_merge",
    )(info, *parts)


def final_kernel(info_ref, a_ref, b_ref, c_ref, d_ref, q_ref, nk_ref, nv_ref, after_ref, slab_ref, lse_ref, step_ref, t_ref, w_ref):
    refs = (a_ref, b_ref, c_ref, d_ref)
    tails = [get_tail(ref[ROWS:, :]) for ref in refs]
    shares, lses, dec, dec_lse = merge_tails(tails, t_ref)
    lse_ref[0:LR, :] = lses[0]
    lse_ref[LR:, :] = lses[1]
    put_shares(w_ref, shares)
    slab_ref[...] = mix([ref[0:ROWS, :] for ref in refs], w_ref, info_ref[2]).astype(BF)
    fresh = scores_t(nk_ref[...], q_ref[...]) * C2
    lane = lax.broadcasted_iota(jnp.int32, (1, HD), 1)
    second = jnp.where(lane % 2 == 1, fresh[1:2], NEG)
    (kept, new_0, new_1), _ = merge_weights([dec_lse, fresh[0:1], second])
    nv = nv_ref[...].astype(F32)
    out = dec * column(kept)[0:STEPR]
    out = out + column(new_0)[0:STEPR] * nv[0:1] + column(new_1)[0:STEPR] * nv[1:2]
    step_ref[...] = out.astype(BF)


def final_merge(info, parts, q, nk, nv, after):
    return pl.pallas_call(
        final_kernel,
        out_shape=(
            jax.ShapeDtypeStruct((ROWS, HD), BF),
            jax.ShapeDtypeStruct((2 * LR, HD), F32),
            jax.ShapeDtypeStruct((STEPR, HD), BF),
        ),
        in_specs=[pl.BlockSpec(memory_space=pltpu.SMEM)] + [pl.BlockSpec(memory_space=pltpu.VMEM)] * 8,
        out_specs=[pl.BlockSpec(memory_space=pltpu.VMEM)] * 3,
        scratch_shapes=[pltpu.VMEM((TAIL, HD), F32), pltpu.VMEM((LR + 1, 8, HD), F32)],
        compiler_params=params(),
        name="final_merge",
    )(info, *parts, q, nk, nv, after)


def heavy_kernel(info_ref, q_ref, k_ref, lse_ref, h_ref, acc_ref):
    i = pl.program_id(0)

    @pl.when(i == 0)
    def _():
        acc_ref[...] = jnp.zeros_like(acc_ref)

    q = q_ref[...]
    per = RB // HD
    other = i // NRB
    lse = jnp.concatenate([lse_ref[pl.ds(i * per + j, 1), :] for j in range(per)], axis=1)
    for c in range(CTXL // SLAB):
        keys = slice(c * SLAB, (c + 1) * SLAB)
        s = scores_t(k_ref[0, keys, :], q)
        if c == CTXL // SLAB - 1:
            s = masked_tail(info_ref, info_ref[1] ^ other, i - other * NRB, s)
        w = jnp.exp2(s * C2 - lse)
        acc_ref[keys, :] += (w[:, 0:128] + w[:, 128:256]) + (w[:, 256:384] + w[:, 384:512])

    @pl.when(i == 2 * NRB - 1)
    def _():
        for t in range(CTXL // HD):
            at = slice(t * HD, (t + 1) * HD)
            sums = jnp.sum(acc_ref[at, :].T, axis=0, keepdims=True)
            h_ref[:, at] = sums * (NCTX * CTXL / (12 * SLAB))


def heavy(info, q, kv, lse):
    return pl.pallas_call(
        heavy_kernel,
        out_shape=jax.ShapeDtypeStruct((1, CTXL), F32),
        grid=(2 * NRB,),
        in_specs=[
            pl.BlockSpec(memory_space=pltpu.SMEM),
            pl.BlockSpec((RB, HD), lambda i: (i, 0)),
            pl.BlockSpec((1, CTXL, HD), lambda i: (0, 0, 0)),
            pl.BlockSpec((2 * LR, HD), lambda i: (0, 0)),
        ],
        out_specs=pl.BlockSpec((1, CTXL), lambda i: (0, 0)),
        scratch_shapes=[pltpu.VMEM((CTXL, HD), F32)],
        compiler_params=params(),
        cost_estimate=pl.CostEstimate(
            flops=4 * HALF * CTXL * HD, bytes_accessed=CTXL * HD * 2, transcendentals=2 * HALF * CTXL
        ),
        name="heavy_columns",
    )(info, q, kv, lse)


def pack_kernel(spans, pick_ref, kv_ref, after_ref, out_ref, sems):
    copies, at = [], 0
    for n, (part, start, count) in enumerate(spans):
        for d in range(NCTX):
            source = kv_ref.at[part, pick_ref[d], start : start + count]
            copies.append(pltpu.make_async_copy(source, out_ref.at[d, at : at + count], sems.at[n, d]))
        at += count
    for copy in copies:
        copy.start()
    for copy in copies:
        copy.wait()


def pack(spans, pick, blocks, after):
    return pl.pallas_call(
        functools.partial(pack_kernel, spans),
        out_shape=jax.ShapeDtypeStruct((NCTX, sum(span[2] for span in spans), HD), BF),
        in_specs=[pl.BlockSpec(memory_space=pltpu.SMEM)] + [pl.BlockSpec(memory_space=pltpu.VMEM)] * 2,
        out_specs=pl.BlockSpec(memory_space=pl.ANY),
        scratch_shapes=[pltpu.SemaphoreType.DMA((len(spans), NCTX))],
        compiler_params=params(),
        name="pack_blocks",
    )(pick, blocks, after)


def held_kernel(x_ref, after_ref, out_ref):
    out_ref[...] = x_ref[...]


def held(x, other):
    return pl.pallas_call(
        held_kernel,
        out_shape=jax.ShapeDtypeStruct(x.shape, x.dtype),
        compiler_params=params(),
        name="held",
    )(x, other)


def after_kernel(x_ref, after_ref, out_ref):
    del x_ref, after_ref, out_ref


def after(x, other):
    return pl.pallas_call(
        after_kernel,
        out_shape=jax.ShapeDtypeStruct(x.shape, x.dtype),
        in_specs=[pl.BlockSpec(memory_space=pl.ANY), pl.BlockSpec(memory_space=pltpu.VMEM)],
        out_specs=pl.BlockSpec(memory_space=pl.ANY),
        input_output_aliases={0: 0},
        name="after",
    )(x, other)


def select_kernel(src_ref, a_ref, b_ref, out_ref, sems):
    copies = []
    for r in range(SLOTS):
        at = src_ref[r]
        for n, (source, target) in enumerate((
            (a_ref.at[at, 0:BLK], out_ref.at[0, r]),
            (a_ref.at[at, BLK : BLK + FIRST], out_ref.at[1, r, 0:FIRST]),
            (b_ref.at[at], out_ref.at[1, r, FIRST:BLK]),
        )):
            copies.append(pltpu.make_async_copy(source, target, sems.at[n, r]))
    for copy in copies:
        copy.start()
    for copy in copies:
        copy.wait()


def select(source, first, second):
    return pl.pallas_call(
        select_kernel,
        out_shape=jax.ShapeDtypeStruct((2, SLOTS, BLK, HD), BF),
        in_specs=[pl.BlockSpec(memory_space=pltpu.SMEM)] + [pl.BlockSpec(memory_space=pl.ANY)] * 2,
        out_specs=pl.BlockSpec(memory_space=pltpu.VMEM),
        scratch_shapes=[pltpu.SemaphoreType.DMA((3, SLOTS))],
        compiler_params=params(),
        name="select_slots",
    )(source, first, second)


def spread_kernel(q_ref, out_ref):
    for n in range(NZ // 2):
        out_ref[n] = q_ref[...]


def spread(q):
    return pl.pallas_call(
        spread_kernel,
        out_shape=jax.ShapeDtypeStruct((NZ // 2, ROWS, HD), BF),
        compiler_params=params(),
        name="spread_queries",
    )(q)


SWAP = [(0, 1), (1, 0)]


CTX = ("xl", "zh", "zm", "zp")
BLOCKS = ("zh", "zm", "zp", "xl")


def local(slab_query, kv_cache, kept_list, decode_place, step_query, step_cache):
    grp = lax.axis_index("grp")
    xl = lax.axis_index("xl")
    zp = lax.axis_index("zp")
    z = lax.axis_index("zh") * NQ + lax.axis_index("zm") * 2 + zp
    ctx = xl * NZ + z
    per_dev = CTXL // BLK

    kept = lax.dynamic_index_in_dim(kept_list, 1 - grp, 0, keepdims=False)[0]
    place = lax.dynamic_index_in_dim(decode_place, 1 - grp, 0, keepdims=False)[0]
    slots = jnp.arange(NCTX, dtype=jnp.int32)
    lanes = slots % 2 * NZ + slots // 2
    offset = kept - ctx * per_dev
    mine = (offset >= 0) & (offset < per_dev)
    hit = mine[None, :] & (place[None, :] == lanes[:, None])
    pick = jnp.clip(jnp.sum(jnp.where(hit, offset[None, :], 0), axis=1), 0, per_dev - 1)
    flags = jnp.sum(
        (offset[None, :] == jnp.arange(per_dev, dtype=jnp.int32)[:, None]).astype(jnp.int32), axis=1
    )
    here = (place == ctx).reshape(SLOTS, NCTX)
    owner = jnp.sum(jnp.where(here, kept.reshape(SLOTS, NCTX) // per_dev, 0), axis=1)
    source = jnp.clip(owner % NZ * 2 + owner // NZ, 0, NCTX - 1)
    info = jnp.stack([ctx, xl, z]).astype(jnp.int32)

    q = jnp.transpose(slab_query[0, :, 0], (1, 0, 2)).reshape(ROWS, HD)
    kv = kv_cache[0, :, :, 0]
    steps = jnp.transpose(step_query[0, :, 0], (1, 0, 2)).reshape(STEPR, HD)
    steps = jnp.pad(steps, ((0, HD - STEPR), (0, 0)))
    new = jnp.pad(step_cache[0, :, :, 0], ((0, 0), (0, 14), (0, 0)))

    kv_decode = lax.ppermute(kv, "grp", SWAP)
    blocks = kv_decode.reshape(2, per_dev, BLK, HD)
    q_same = lax.all_to_all(spread(q), ("zh", "zm"), 0, 0, tiled=True)
    packed = pack(((0, 0, BLK), (1, 0, FIRST)), pick, blocks, steps[0:16])
    q_next = lax.ppermute(held(q_same, packed[0, 0:16]), "zp", SWAP)
    even, odd = jnp.where(zp == 0, q_same, q_next), jnp.where(zp == 0, q_next, q_same)
    q_own = jnp.stack([even, odd], axis=1).reshape(HALF, HD)
    dec = decode_partial(flags, steps, kv_decode)

    keys = lax.all_to_all(packed, BLOCKS, 0, 0, tiled=True)
    q_other = lax.ppermute(q_own, "xl", SWAP)
    part_own, lse_own = flash(0, info, q_own, kv, dec[0:8])
    part_other, lse_other = flash(1, info, q_other, kv, lse_own[0:8])
    blank = jnp.zeros((16 - LR, HD), F32)
    small = lax.ppermute(jnp.concatenate([lse_other, blank, lse_own, blank, dec], axis=0), "xl", SWAP)
    part_beside = lax.ppermute(part_other, "xl", SWAP)
    parts = pair_merge(info, part_own, part_beside, lse_other, lse_own, dec, small)
    near = [lax.ppermute(parts[s], ("zm", "zp"), [(i, i ^ s) for i in range(NQ)]) for s in range(1, NQ)]
    rest = pack(((1, FIRST, BLK - FIRST),), pick, blocks, parts[0, 0:16])
    values = lax.all_to_all(after(rest, keys[0, 0:16]), BLOCKS, 0, 0, tiled=True)
    merged = quad_merge(info, [parts[0]] + near)
    far = [lax.ppermute(merged[s], "zh", [(i, i ^ s) for i in range(NZ // NQ)]) for s in range(1, NZ // NQ)]
    paged = select(source, keys, values)
    slab, lse, step = final_merge(info, [merged[0]] + far, steps, new[0], new[1], paged[0, 0, 0:16])
    columns = heavy(info, jnp.concatenate([q_own, q_other], axis=0), kv, lse)

    slab_out = jnp.transpose(slab.reshape(12, 8, HD), (1, 0, 2))[None, :, None]
    step_out = jnp.transpose(step.reshape(12, 2, HD), (1, 0, 2))[None, :, None]
    return (slab_out, columns[None], paged[None, None], step_out)


def solution(mesh):
    split = Mesh(mesh.devices.reshape(2, 2, NZ // NQ, 2, 2, 8), ("grp", "xl", "zh", "zm", "zp", "kvh"))
    return jax.shard_map(
        local,
        mesh=split,
        in_specs=(
            P("grp", CTX, "kvh", None, None),
            P("grp", None, CTX, "kvh", None),
            P(None, "kvh", None),
            P(None, "kvh", None),
            P("grp", None, "kvh", None, None),
            P("grp", None, None, "kvh", None),
        ),
        out_specs=(
            P("grp", CTX, "kvh", None, None),
            P("grp", "kvh", CTX),
            P("grp", "kvh", None, CTX, None, None),
            P("grp", None, "kvh", None, None),
        ),
        check_vma=False,
    )
```

time: 202 us -> 182 us (0.901)
  the two profiles are of different devices: /device:TPU:24 before, /device:TPU:56 now
where the time goes in v4:
time: 182 us; the launch traced here: 180 us
  starting transfers between devices  70.1 us (39%)
  waiting for transfers between devices  59.9 us (33%)
  Pallas kernels  34.5 us (19%)
  local copies, waits for them, and re-layouts  11.3 us (6%)
  other arithmetic  3.6 us (2%)
    all_to_all x1, waiting for transfers between devices, local(): lax.all_to_all(after(rest, keys[0, 0:16]), BLOCKS, 0, 0, tiled=True)  27.7 us
    ppermute x3, starting transfers between devices, local(): lax.ppermute(merged[s], 'zh', [(i, i ^ s) for i in range(NZ // NQ)])  17 us
    all_to_all x1, starting transfers between devices, local(): q_same = lax.all_to_all(spread(q), ('zh', 'zm'), 0, 0, tiled=True)  14.2 us
    pallas_call x2, Pallas kernels, flash(): pl.pallas_call(functools.partial(flash_kernel, other), out_shape=(jax.Sha...  13.3 us
    all_to_all x1, waiting for transfers between devices, local(): keys = lax.all_to_all(packed, BLOCKS, 0, 0, tiled=True)  13.2 us
    all_to_all x1, waiting for transfers between devices, local(): q_same = lax.all_to_all(spread(q), ('zh', 'zm'), 0, 0, tiled=True)  12.4 us
    ppermute x3, starting transfers between devices, local(): lax.ppermute(parts[s], ('zm', 'zp'), [(i, i ^ s) for i in range(NQ)])  11.2 us
    all_to_all x1, starting transfers between devices, local(): lax.all_to_all(after(rest, keys[0, 0:16]), BLOCKS, 0, 0, tiled=True)  7.69 us
  transfers between devices with their start and end apart: 14, of which 5 were waited for; matrix products, arithmetic and copies ran while one was open for 6% of the time, Pallas kernels for 15%

profile of v4, /device:TPU:56, one launch (start us, length us, event | category | flops | bytes accessed | tf_op | source)
XLA Modules:
  0.0 180.5 jit_solution(5267841819412424397)
XLA Ops:
  0.6 1.9 %collective-permute-start = (bf16[2,2048,128]{2,1,0:T(8,128)(2,1)}, bf16[2,2048,128]{2,1,0:T(8,128)(2,1)S(1)}, u32[]{:S(2)}, u32[]{:S(2)}) collective-permute-start(bf16[2,2048,128]{2,1,0:T(8,128)(2,1)} %bitcast.69), channel_id=1, source_target_pairs={{0,256},{256,0},{1,257},{257,1},{2,258},{258,2},{3,259},{259,3},{4... | collective-permute-start | bytes 3145736 | tf_op jit(solution)/shard_map/ppermute | solution.py:471
  2.6 0.7 copy-done.11
  3.3 0.7 spread_queries.1
  4.0 14.2 %all-to-all-start = ((bf16[8,96,128]{2,1,0:T(8,128)(2,1)}), bf16[8,96,128]{2,1,0:T(8,128)(2,1)S(1)}, u32[]{:S(2)}, u32[]{:S(2)}) async-start(bf16[8,96,128]{2,1,0:T(8,128)(2,1)} %spread_queries.1), calls=%async_computation | async-start | bytes 393216 | tf_op jit(solution)/shard_map/all_to_all | solution.py:473
  18.2 0.7 compare_reduce_fusion
  18.9 0.1 eq.60
  19.0 0.7 dynamic-slice_reduce_fusion.1
  19.7 0.1 reshape_squeeze.3
  19.8 0.2 select_reduce_fusion
  20.0 0.1 fusion.2
  20.1 0.7 slice.73
  20.8 0.5 fusion.10.src_ref
  21.3 0.0 collective-permute-done.k_ref.v_ref
  21.3 3.1 %pack_blocks.2 = bf16[32,160,128]{2,1,0:T(8,128)(2,1)S(1)} custom-call(s32[32]{0:T(128)S(1)} %broadcast_clamp_fusion.pick_ref, bf16[2,16,128,128]{3,2,1,0:T(8,128)(2,1)S(1)} %bitcast.62, bf16[16,128]{1,0:T(8,128)(2,1)S(1)} %bitcast.68), custom_call_target="tpu_custom_call" | custom-call | tf_op jit(solution)/shard_map/pack_blocks/pallas_call | solution.py:353
  24.5 12.4 %all-to-all-done.x_ref = bf16[8,96,128]{2,1,0:T(8,128)(2,1)S(1)} async-done(((bf16[8,96,128]{2,1,0:T(8,128)(2,1)}), bf16[8,96,128]{2,1,0:T(8,128)(2,1)S(1)}, u32[]{:S(2)}, u32[]{:S(2)}) %all-to-all-start) | async-done | bytes 196640 | tf_op jit(solution)/shard_map/all_to_all | solution.py:473
  36.9 3.5 %collective-permute-start.1 = (bf16[8,96,128]{2,1,0:T(8,128)(2,1)S(1)}, bf16[8,96,128]{2,1,0:T(8,128)(2,1)S(1)}, u32[]{:S(2)}, u32[]{:S(2)}) collective-permute-start(bf16[8,96,128]{2,1,0:T(8,128)(2,1)S(1)} %held.1), channel_id=1, source_target_pairs={{0,8},{8,0},{1,9},{9,1},{2,10},{10,2},{3,11},{11,3},{4,12},{12,4},... | collective-permute-start | bytes 589832 | tf_op jit(solution)/shard_map/ppermute | solution.py:475
  40.4 0.1 convert_reduce_fusion.flag_ref
  40.5 5.1 %all-to-all-start.1 = ((bf16[32,160,128]{2,1,0:T(8,128)(2,1)}), bf16[32,160,128]{2,1,0:T(8,128)(2,1)S(1)}, u32[]{:S(2)}, u32[]{:S(2)}) async-start(bf16[32,160,128]{2,1,0:T(8,128)(2,1)} %copy-done.1), calls=%async_computation.1 | async-start | bytes 2621440 | tf_op jit(solution)/shard_map/all_to_all | solution.py:480
  45.6 0.1 pad_add_fusion.info_ref
  45.7 1.5 decode_partial.1.da_ref
  47.3 0.0 collective-permute-done.1
  47.3 0.1 select_bitcast_fusion.1
  47.5 3.5 %collective-permute-start.2 = (bf16[1536,128]{1,0:T(8,128)(2,1)S(1)}, bf16[1536,128]{1,0:T(8,128)(2,1)S(1)}, u32[]{:S(2)}, u32[]{:S(2)}) collective-permute-start(bf16[1536,128]{1,0:T(8,128)(2,1)S(1)} %bitcast.64), channel_id=1, source_target_pairs={{0,128},{128,0},{1,129},{129,1},{2,130},{130,2},{3,131},{131,3},{4... | collective-permute-start | bytes 1179656 | tf_op jit(solution)/shard_map/ppermute | solution.py:481
  51.0 6.4 %slab_partial.2 = (bf16[1536,128]{1,0:T(8,128)(2,1)S(1)}, f32[12,128]{1,0:T(8,128)S(1)}) custom-call(s32[3]{0:T(128)S(1)} %pad_add_fusion.info_ref, bf16[1536,128]{1,0:T(8,128)(2,1)S(1)} %bitcast.65, bf16[2,2048,128]{2,1,0:T(8,128)(2,1)S(1)} %bitcast.70, bf16[2,2048,128]{2,1,0:T(8,128)(2,1)S(1)} %bitcast.71, f32[8,128]{1,0:T(8,128)S(1)} %slice.75.after_ref), custom_call_target="tpu_custom_call" | custom-call | flops 20000000000 | bytes 1048576 | tf_op jit(solution)/shard_map/slab_partial/pallas_call | solution.py:107
  57.3 0.0 copy-start.2
  57.4 0.7 copy-done.2
  58.1 4.6 %collective-permute-done.2.q_ref = bf16[1536,128]{1,0:T(8,128)(2,1)S(1)} collective-permute-done((bf16[1536,128]{1,0:T(8,128)(2,1)S(1)}, bf16[1536,128]{1,0:T(8,128)(2,1)S(1)}, u32[]{:S(2)}, u32[]{:S(2)}) %collective-permute-start.2) | collective-permute-done | bytes 393248 | tf_op jit(solution)/shard_map/ppermute | solution.py:481
  62.7 7.0 %slab_partial.3 = (bf16[1536,128]{1,0:T(8,128)(2,1)}, f32[12,128]{1,0:T(8,128)S(1)}) custom-call(s32[3]{0:T(128)S(1)} %pad_add_fusion.info_ref, bf16[1536,128]{1,0:T(8,128)(2,1)S(1)} %collective-permute-done.2.q_ref, bf16[2,2048,128]{2,1,0:T(8,128)(2,1)S(1)} %bitcast.72, bf16[2,2048,128]{2,1,0:T(8,128)(2,1)S(1)} %bitcast.73, f32[8,128]{1,0:T(8,128)S(1)} %slice.59.after_ref), custom_call_target="tpu_custom_call" | custom-call | flops 20000000000 | bytes 1048576 | tf_op jit(solution)/shard_map/slab_partial/pallas_call | solution.py:107
  69.7 2.5 %collective-permute-start.3 = (bf16[1536,128]{1,0:T(8,128)(2,1)}, bf16[1536,128]{1,0:T(8,128)(2,1)}, u32[]{:S(2)}, u32[]{:S(2)}) collective-permute-start(bf16[1536,128]{1,0:T(8,128)(2,1)} %get-tuple-element.13), channel_id=1, source_target_pairs={{0,128},{128,0},{1,129},{129,1},{2,130},{130,2},{3,131},{131,3},{4... | collective-permute-start | bytes 1179656 | tf_op jit(solution)/shard_map/ppermute | solution.py:486
  72.2 0.6 fusion.5
  72.8 4.3 %concatenate.6 = f32[64,128]{1,0:T(8,128)} concatenate(f32[12,128]{1,0:T(8,128)S(1)} %get-tuple-element.14.lo_ref, f32[4,128]{1,0:T(4,128)S(1)} %broadcast_in_dim.36, f32[12,128]{1,0:T(8,128)S(1)} %get-tuple-element.12.la_ref, f32[4,128]{1,0:T(4,128)S(1)} %broadcast_in_dim.36, f32[32,128]{1,0:T(8,128)S(1)} %decode_partial.1.da_ref), dimensions={0} | concatenate | bytes 65536 | tf_op jit(solution)/shard_map/concatenate | solution.py:485
  77.1 3.5 %collective-permute-start.4 = (f32[64,128]{1,0:T(8,128)}, f32[64,128]{1,0:T(8,128)S(1)}, u32[]{:S(2)}, u32[]{:S(2)}) collective-permute-start(f32[64,128]{1,0:T(8,128)} %concatenate.6), channel_id=1, source_target_pairs={{0,128},{128,0},{1,129},{129,1},{2,130},{130,2},{3,131},{131,3},{4... | collective-permute-start | bytes 98312 | tf_op jit(solution)/shard_map/ppermute | solution.py:485
  80.6 0.0 copy-start.10
  80.7 1.1 pad_maximum_fusion.q_ref
  81.7 1.9 %collective-permute-done.4.sb_ref = f32[64,128]{1,0:T(8,128)S(1)} collective-permute-done((f32[64,128]{1,0:T(8,128)}, f32[64,128]{1,0:T(8,128)S(1)}, u32[]{:S(2)}, u32[]{:S(2)}) %collective-permute-start.4) | collective-permute-done | bytes 32800 | tf_op jit(solution)/shard_map/ppermute | solution.py:485
  83.6 0.0 collective-permute-done.3.b_ref
  83.7 0.0 copy-start.3
  83.7 1.0 copy-done.3
  84.7 1.5 pair_merge.1
  86.2 2.0 %pack_blocks.3.x_ref = bf16[32,96,128]{2,1,0:T(8,128)(2,1)S(1)} custom-call(s32[32]{0:T(128)S(1)} %copy-done.18, bf16[2,16,128,128]{3,2,1,0:T(8,128)(2,1)S(1)} %bitcast.63, bf16[16,128]{1,0:T(8,128)(2,1)S(1)} %slice_bitcast_fusion.10.after_ref), custom_call_target="tpu_custom_call" | custom-call | tf_op jit(solution)/shard_map/pack_blocks/pallas_call | solution.py:353
  88.2 0.0 copy-start
  88.2 0.9 copy-done
  89.1 0.7 slice_bitcast_fusion
  89.8 4.6 %collective-permute-start.7 = (bf16[496,128]{1,0:T(8,128)(2,1)}, bf16[496,128]{1,0:T(8,128)(2,1)S(1)}, u32[]{:S(2)}, u32[]{:S(2)}) collective-permute-start(bf16[496,128]{1,0:T(8,128)(2,1)} %get-tuple-element.20), channel_id=1, source_target_pairs={{0,24},{8,16},{16,8},{24,0},{1,25},{9,17},{17,9},{25,1},{2,26},{10... | collective-permute-start | bytes 380936 | tf_op jit(solution)/shard_map/ppermute | solution.py:488
  94.5 3.2 %collective-permute-start.6 = (bf16[496,128]{1,0:T(8,128)(2,1)}, bf16[496,128]{1,0:T(8,128)(2,1)S(1)}, u32[]{:S(2)}, u32[]{:S(2)}) collective-permute-start(bf16[496,128]{1,0:T(8,128)(2,1)} %get-tuple-element.21), channel_id=1, source_target_pairs={{0,16},{8,24},{16,0},{24,8},{1,17},{9,25},{17,1},{25,9},{2,18},{10... | collective-permute-start | bytes 380936 | tf_op jit(solution)/shard_map/ppermute | solution.py:488
  97.7 3.4 %collective-permute-start.5 = (bf16[496,128]{1,0:T(8,128)(2,1)S(1)}, bf16[496,128]{1,0:T(8,128)(2,1)S(1)}, u32[]{:S(2)}, u32[]{:S(2)}) collective-permute-start(bf16[496,128]{1,0:T(8,128)(2,1)S(1)} %get-tuple-element.22), channel_id=1, source_target_pairs={{0,8},{8,0},{16,24},{24,16},{1,9},{9,1},{17,25},{25,17},{2,10},{10... | collective-permute-start | bytes 380936 | tf_op jit(solution)/shard_map/ppermute | solution.py:488
  101.1 13.2 %all-to-all-done.1.a_ref = bf16[32,160,128]{2,1,0:T(8,128)(2,1)S(1)} async-done(((bf16[32,160,128]{2,1,0:T(8,128)(2,1)}), bf16[32,160,128]{2,1,0:T(8,128)(2,1)S(1)}, u32[]{:S(2)}, u32[]{:S(2)}) %all-to-all-start.1) | async-done | bytes 1310752 | tf_op jit(solution)/shard_map/all_to_all | solution.py:480
  114.3 0.6 slice_bitcast_fusion.9.after_ref
  114.9 0.7 after.1
  115.6 7.7 %all-to-all-start.2 = ((bf16[32,96,128]{2,1,0:T(8,128)(2,1)}), bf16[32,96,128]{2,1,0:T(8,128)(2,1)S(1)}, u32[]{:S(2)}, u32[]{:S(2)}) async-start(bf16[32,96,128]{2,1,0:T(8,128)(2,1)} %after.1), calls=%async_computation.2 | async-start | bytes 1572864 | tf_op jit(solution)/shard_map/all_to_all | solution.py:490
  123.3 0.0 collective-permute-done.6.c_ref
  123.3 1.0 quad_merge.1
  124.4 6.4 %collective-permute-start.10 = (bf16[208,128]{1,0:T(8,128)(2,1)S(1)}, bf16[208,128]{1,0:T(8,128)(2,1)S(1)}, u32[]{:S(2)}, u32[]{:S(2)}) collective-permute-start(bf16[208,128]{1,0:T(8,128)(2,1)S(1)} %get-tuple-element.26), channel_id=1, source_target_pairs={{0,96},{32,64},{64,32},{96,0},{1,97},{33,65},{65,33},{97,1},{2,98}... | collective-permute-start | bytes 159752 | tf_op jit(solution)/shard_map/ppermute | solution.py:492
  130.8 8.1 %collective-permute-start.9 = (bf16[208,128]{1,0:T(8,128)(2,1)S(1)}, bf16[208,128]{1,0:T(8,128)(2,1)S(1)}, u32[]{:S(2)}, u32[]{:S(2)}) collective-permute-start(bf16[208,128]{1,0:T(8,128)(2,1)S(1)} %get-tuple-element.27), channel_id=1, source_target_pairs={{0,64},{32,96},{64,0},{96,32},{1,65},{33,97},{65,1},{97,33},{2,66}... | collective-permute-start | bytes 159752 | tf_op jit(solution)/shard_map/ppermute | solution.py:492
  139.0 0.0 copy-start.12
  139.0 2.5 %collective-permute-start.8 = (bf16[208,128]{1,0:T(8,128)(2,1)S(1)}, bf16[208,128]{1,0:T(8,128)(2,1)S(1)}, u32[]{:S(2)}, u32[]{:S(2)}) collective-permute-start(bf16[208,128]{1,0:T(8,128)(2,1)S(1)} %get-tuple-element.28), channel_id=1, source_target_pairs={{0,32},{32,0},{64,96},{96,64},{1,33},{33,1},{65,97},{97,65},{2,34}... | collective-permute-start | bytes 159752 | tf_op jit(solution)/shard_map/ppermute | solution.py:492
  141.5 27.7 %all-to-all-done.2.b_ref = bf16[32,96,128]{2,1,0:T(8,128)(2,1)S(1)} async-done(((bf16[32,96,128]{2,1,0:T(8,128)(2,1)}), bf16[32,96,128]{2,1,0:T(8,128)(2,1)S(1)}, u32[]{:S(2)}, u32[]{:S(2)}) %all-to-all-start.2) | async-done | bytes 786464 | tf_op jit(solution)/shard_map/all_to_all | solution.py:490
  169.1 2.8 %select_slots.1 = bf16[2,12,128,128]{3,2,1,0:T(8,128)(2,1)} custom-call(s32[12]{0:T(128)S(1)} %copy-done.19, bf16[32,160,128]{2,1,0:T(8,128)(2,1)S(1)} %all-to-all-done.1.a_ref, bf16[32,96,128]{2,1,0:T(8,128)(2,1)S(1)} %all-to-all-done.2.b_ref), custom_call_target="tpu_custom_call" | custom-call | tf_op jit(solution)/shard_map/select_slots/pallas_call | solution.py:409
  172.0 0.7 slice_bitcast_fusion.8.after_ref
  172.7 0.0 collective-permute-done.10.d_ref
  172.7 0.0 collective-permute-done.9.c_ref
  172.7 0.0 collective-permute-done.8.b_ref
  172.7 1.4 final_merge.1
  174.2 6.3 %heavy_columns.1 = f32[1,2048]{1,0:T(1,128)} custom-call(s32[3]{0:T(128)S(1)} %copy-done.16, bf16[3072,128]{1,0:T(8,128)(2,1)S(1)} %pad_maximum_fusion.q_ref, bf16[2,2048,128]{2,1,0:T(8,128)(2,1)S(1)} %bitcast.74, f32[24,128]{1,0:T(8,128)S(1)} %get-tuple-element.16.lse_ref), custom_call_target="tpu_custom_call" | custom-call | flops 1610612736 | bytes 524288 | tf_op jit(solution)/shard_map/heavy_columns/pallas_call | solution.py:319
  (54 shorter events, 0.2 us)
Async XLA Ops:
  0.6 20.7 %collective-permute-start = (bf16[2,2048,128]{2,1,0:T(8,128)(2,1)}, bf16[2,2048,128]{2,1,0:T(8,128)(2,1)S(1)}, u32[]{:S(2)}, u32[]{:S(2)}) collective-permute-start(bf16[2,2048,128]{2,1,0:T(8,128)(2,1)} %bitcast.69), channel_id=1, source_target_pairs={{0,256},{256,0},{1,257},{257,1},{2,258},{258,2},{3,259},{259,3},{4... | collective-permute-start | bytes 3145736 | tf_op jit(solution)/shard_map/ppermute | solution.py:471
  2.6 0.7 copy-start.11
  4.0 32.9 %all-to-all-start = ((bf16[8,96,128]{2,1,0:T(8,128)(2,1)}), bf16[8,96,128]{2,1,0:T(8,128)(2,1)S(1)}, u32[]{:S(2)}, u32[]{:S(2)}) async-start(bf16[8,96,128]{2,1,0:T(8,128)(2,1)} %spread_queries.1), calls=%async_computation | async-start | bytes 393216 | tf_op jit(solution)/shard_map/all_to_all | solution.py:473
  20.8 3.6 %copy-start.17 = (s32[32]{0:T(128)}, s32[32]{0:T(128)S(1)}, u32[]{:S(2)}) copy-start(s32[32]{0:T(128)S(1)} %broadcast_clamp_fusion.pick_ref) | copy-start | bytes 388
  24.4 16.0 %copy-start.1 = (bf16[32,160,128]{2,1,0:T(8,128)(2,1)}, bf16[32,160,128]{2,1,0:T(8,128)(2,1)S(1)}, u32[]{:S(2)}) copy-start(bf16[32,160,128]{2,1,0:T(8,128)(2,1)S(1)} %pack_blocks.2) | copy-start | bytes 3932164
  36.9 10.4 %collective-permute-start.1 = (bf16[8,96,128]{2,1,0:T(8,128)(2,1)S(1)}, bf16[8,96,128]{2,1,0:T(8,128)(2,1)S(1)}, u32[]{:S(2)}, u32[]{:S(2)}) collective-permute-start(bf16[8,96,128]{2,1,0:T(8,128)(2,1)S(1)} %held.1), channel_id=1, source_target_pairs={{0,8},{8,0},{1,9},{9,1},{2,10},{10,2},{3,11},{11,3},{4,12},{12,4},... | collective-permute-start | bytes 589832 | tf_op jit(solution)/shard_map/ppermute | solution.py:475
  40.5 5.2 %copy-start.22 = (bf16[1,2,1,12,128]{4,1,3,2,0:T(2,128)(2,1)S(1)}, bf16[1,2,1,12,128]{4,1,3,2,0:T(2,128)(2,1)}, u32[]{:S(2)}) copy-start(bf16[1,2,1,12,128]{4,1,3,2,0:T(2,128)(2,1)} %param.10) | copy-start | bytes 18436
  40.5 73.8 %all-to-all-start.1 = ((bf16[32,160,128]{2,1,0:T(8,128)(2,1)}), bf16[32,160,128]{2,1,0:T(8,128)(2,1)S(1)}, u32[]{:S(2)}, u32[]{:S(2)}) async-start(bf16[32,160,128]{2,1,0:T(8,128)(2,1)} %copy-done.1), calls=%async_computation.1 | async-start | bytes 2621440 | tf_op jit(solution)/shard_map/all_to_all | solution.py:480
  45.7 17.0 %copy-start.14 = (s32[3]{0:T(128)}, s32[3]{0:T(128)S(1)}, u32[]{:S(2)}) copy-start(s32[3]{0:T(128)S(1)} %pad_add_fusion.info_ref) | copy-start | bytes 40
  45.7 1.6 copy-start.5
  47.3 3.7 %copy-start.20 = (bf16[1,2,2048,1,128]{4,2,3,1,0:T(8,128)(2,1)S(1)}, bf16[1,2,2048,1,128]{4,2,3,1,0:T(8,128)(2,1)}, u32[]{:S(2)}) copy-start(bf16[1,2,2048,1,128]{4,2,3,1,0:T(8,128)(2,1)} %param.7) | copy-start | bytes 3145732
  47.5 15.2 %collective-permute-start.2 = (bf16[1536,128]{1,0:T(8,128)(2,1)S(1)}, bf16[1536,128]{1,0:T(8,128)(2,1)S(1)}, u32[]{:S(2)}, u32[]{:S(2)}) collective-permute-start(bf16[1536,128]{1,0:T(8,128)(2,1)S(1)} %bitcast.64), channel_id=1, source_target_pairs={{0,128},{128,0},{1,129},{129,1},{2,130},{130,2},{3,131},{131,3},{4... | collective-permute-start | bytes 1179656 | tf_op jit(solution)/shard_map/ppermute | solution.py:481
  57.3 0.7 copy-start.2
  58.1 14.7 %copy-start.7 = (f32[12,128]{1,0:T(8,128)}, f32[12,128]{1,0:T(8,128)S(1)}, u32[]{:S(2)}) copy-start(f32[12,128]{1,0:T(8,128)S(1)} %get-tuple-element.12.la_ref) | copy-start | bytes 18436
  58.1 14.1 %copy-start.23 = (bf16[1,2,2,1,128]{4,2,3,1,0:T(2,128)(2,1)S(1)}, bf16[1,2,2,1,128]{4,2,3,1,0:T(2,128)(2,1)}, u32[]{:S(2)}) copy-start(bf16[1,2,2,1,128]{4,2,3,1,0:T(2,128)(2,1)} %param.11) | copy-start | bytes 3076
  62.7 7.0 %copy-start.4 = (bf16[1536,128]{1,0:T(8,128)(2,1)}, bf16[1536,128]{1,0:T(8,128)(2,1)S(1)}, u32[]{:S(2)}) copy-start(bf16[1536,128]{1,0:T(8,128)(2,1)S(1)} %collective-permute-done.2.q_ref) | copy-start | bytes 1179652
  69.7 7.4 %copy-start.9 = (f32[12,128]{1,0:T(8,128)}, f32[12,128]{1,0:T(8,128)S(1)}, u32[]{:S(2)}) copy-start(f32[12,128]{1,0:T(8,128)S(1)} %get-tuple-element.14.lo_ref) | copy-start | bytes 18436
  69.7 14.0 %collective-permute-start.3 = (bf16[1536,128]{1,0:T(8,128)(2,1)}, bf16[1536,128]{1,0:T(8,128)(2,1)}, u32[]{:S(2)}, u32[]{:S(2)}) collective-permute-start(bf16[1536,128]{1,0:T(8,128)(2,1)} %get-tuple-element.13), channel_id=1, source_target_pairs={{0,128},{128,0},{1,129},{129,1},{2,130},{130,2},{3,131},{131,3},{4... | collective-permute-start | bytes 1179656 | tf_op jit(solution)/shard_map/ppermute | solution.py:486
  77.1 6.5 %copy-start.8 = (f32[12,128]{1,0:T(8,128)S(1)}, f32[12,128]{1,0:T(8,128)}, u32[]{:S(2)}) copy-start(f32[12,128]{1,0:T(8,128)} %copy-done.7) | copy-start | bytes 18436
  77.1 6.5 %copy-start.15 = (s32[3]{0:T(128)S(1)}, s32[3]{0:T(128)}, u32[]{:S(2)}) copy-start(s32[3]{0:T(128)} %copy-done.14) | copy-start | bytes 40
  77.1 9.1 %copy-start.18 = (s32[32]{0:T(128)S(1)}, s32[32]{0:T(128)}, u32[]{:S(2)}) copy-start(s32[32]{0:T(128)} %copy-done.17) | copy-start | bytes 388
  77.1 6.5 %collective-permute-start.4 = (f32[64,128]{1,0:T(8,128)}, f32[64,128]{1,0:T(8,128)S(1)}, u32[]{:S(2)}, u32[]{:S(2)}) collective-permute-start(f32[64,128]{1,0:T(8,128)} %concatenate.6), channel_id=1, source_target_pairs={{0,128},{128,0},{1,129},{129,1},{2,130},{130,2},{3,131},{131,3},{4... | collective-permute-start | bytes 98312 | tf_op jit(solution)/shard_map/ppermute | solution.py:485
  80.6 3.0 %copy-start.10 = (f32[12,128]{1,0:T(8,128)S(1)}, f32[12,128]{1,0:T(8,128)}, u32[]{:S(2)}) copy-start(f32[12,128]{1,0:T(8,128)} %copy-done.9) | copy-start | bytes 18436
  83.7 1.0 copy-start.3
  88.2 0.9 copy-start
  89.8 33.5 %collective-permute-start.7 = (bf16[496,128]{1,0:T(8,128)(2,1)}, bf16[496,128]{1,0:T(8,128)(2,1)S(1)}, u32[]{:S(2)}, u32[]{:S(2)}) collective-permute-start(bf16[496,128]{1,0:T(8,128)(2,1)} %get-tuple-element.20), channel_id=1, source_target_pairs={{0,24},{8,16},{16,8},{24,0},{1,25},{9,17},{17,9},{25,1},{2,26},{10... | collective-permute-start | bytes 380936 | tf_op jit(solution)/shard_map/ppermute | solution.py:488
  94.5 28.8 %collective-permute-start.6 = (bf16[496,128]{1,0:T(8,128)(2,1)}, bf16[496,128]{1,0:T(8,128)(2,1)S(1)}, u32[]{:S(2)}, u32[]{:S(2)}) collective-permute-start(bf16[496,128]{1,0:T(8,128)(2,1)} %get-tuple-element.21), channel_id=1, source_target_pairs={{0,16},{8,24},{16,0},{24,8},{1,17},{9,25},{17,1},{25,9},{2,18},{10... | collective-permute-start | bytes 380936 | tf_op jit(solution)/shard_map/ppermute | solution.py:488
  97.7 25.6 %collective-permute-start.5 = (bf16[496,128]{1,0:T(8,128)(2,1)S(1)}, bf16[496,128]{1,0:T(8,128)(2,1)S(1)}, u32[]{:S(2)}, u32[]{:S(2)}) collective-permute-start(bf16[496,128]{1,0:T(8,128)(2,1)S(1)} %get-tuple-element.22), channel_id=1, source_target_pairs={{0,8},{8,0},{16,24},{24,16},{1,9},{9,1},{17,25},{25,17},{2,10},{10... | collective-permute-start | bytes 380936 | tf_op jit(solution)/shard_map/ppermute | solution.py:488
  114.9 8.4 %copy-start.16 = (s32[3]{0:T(128)S(1)}, s32[3]{0:T(128)}, u32[]{:S(2)}) copy-start(s32[3]{0:T(128)} %copy-done.14) | copy-start | bytes 40
  115.6 53.5 %all-to-all-start.2 = ((bf16[32,96,128]{2,1,0:T(8,128)(2,1)}), bf16[32,96,128]{2,1,0:T(8,128)(2,1)S(1)}, u32[]{:S(2)}, u32[]{:S(2)}) async-start(bf16[32,96,128]{2,1,0:T(8,128)(2,1)} %after.1), calls=%async_computation.2 | async-start | bytes 1572864 | tf_op jit(solution)/shard_map/all_to_all | solution.py:490
  123.3 45.8 %copy-start.19 = (s32[12]{0:T(128)S(1)}, s32[12]{0:T(128)}, u32[]{:S(2)}) copy-start(s32[12]{0:T(128)} %fusion.10.src_ref) | copy-start | bytes 148
  124.4 48.3 %collective-permute-start.10 = (bf16[208,128]{1,0:T(8,128)(2,1)S(1)}, bf16[208,128]{1,0:T(8,128)(2,1)S(1)}, u32[]{:S(2)}, u32[]{:S(2)}) collective-permute-start(bf16[208,128]{1,0:T(8,128)(2,1)S(1)} %get-tuple-element.26), channel_id=1, source_target_pairs={{0,96},{32,64},{64,32},{96,0},{1,97},{33,65},{65,33},{97,1},{2,98}... | collective-permute-start | bytes 159752 | tf_op jit(solution)/shard_map/ppermute | solution.py:492
  130.8 41.8 %collective-permute-start.9 = (bf16[208,128]{1,0:T(8,128)(2,1)S(1)}, bf16[208,128]{1,0:T(8,128)(2,1)S(1)}, u32[]{:S(2)}, u32[]{:S(2)}) collective-permute-start(bf16[208,128]{1,0:T(8,128)(2,1)S(1)} %get-tuple-element.27), channel_id=1, source_target_pairs={{0,64},{32,96},{64,0},{96,32},{1,65},{33,97},{65,1},{97,33},{2,66}... | collective-permute-start | bytes 159752 | tf_op jit(solution)/shard_map/ppermute | solution.py:492
  139.0 33.7 %copy-start.6 = (bf16[128,128]{1,0:T(8,128)(2,1)S(1)}, bf16[128,128]{1,0:T(8,128)(2,1)}, u32[]{:S(2)}) copy-start(bf16[128,128]{1,0:T(8,128)(2,1)} %copy-done.5) | copy-start | bytes 98308
  139.0 33.7 %copy-start.12 = (bf16[16,128]{1,0:T(8,128)(2,1)S(1)}, bf16[16,128]{1,0:T(8,128)(2,1)}, u32[]{:S(2)}) copy-start(bf16[16,128]{1,0:T(8,128)(2,1)} %get-tuple-element.30.nv_ref) | copy-start | bytes 12292
  139.0 33.7 %copy-start.13 = (bf16[16,128]{1,0:T(8,128)(2,1)S(1)}, bf16[16,128]{1,0:T(8,128)(2,1)}, u32[]{:S(2)}) copy-start(bf16[16,128]{1,0:T(8,128)(2,1)} %get-tuple-element.31.nk_ref) | copy-start | bytes 12292
  139.0 33.7 %collective-permute-start.8 = (bf16[208,128]{1,0:T(8,128)(2,1)S(1)}, bf16[208,128]{1,0:T(8,128)(2,1)S(1)}, u32[]{:S(2)}, u32[]{:S(2)}) collective-permute-start(bf16[208,128]{1,0:T(8,128)(2,1)S(1)} %get-tuple-element.28), channel_id=1, source_target_pairs={{0,32},{32,0},{64,96},{96,64},{1,33},{33,1},{65,97},{97,65},{2,34}... | collective-permute-start | bytes 159752 | tf_op jit(solution)/shard_map/ppermute | solution.py:492
  169.1 5.0 %copy-start.21 = (bf16[1,2,2048,1,128]{4,2,3,1,0:T(8,128)(2,1)S(1)}, bf16[1,2,2048,1,128]{4,2,3,1,0:T(8,128)(2,1)}, u32[]{:S(2)}) copy-start(bf16[1,2,2048,1,128]{4,2,3,1,0:T(8,128)(2,1)} %param.7) | copy-start | bytes 3145732

commit v5 on v4

--- a/solution.py
+++ b/solution.py
@@ -328,7 +328,7 @@
         ],
         out_specs=pl.BlockSpec((1, CTXL), lambda i: (0, 0)),
         scratch_shapes=[pltpu.VMEM((CTXL, HD), F32)],
-        compiler_params=params(),
+        compiler_params=params(60),
         cost_estimate=pl.CostEstimate(
             flops=4 * HALF * CTXL * HD, bytes_accessed=CTXL * HD * 2, transcendentals=2 * HALF * CTXL
         ),
@@ -372,6 +372,20 @@
         compiler_params=params(),
         name="held",
     )(x, other)
+
+
+def picked_kernel(x_ref, out_ref):
+    out_ref[...] = x_ref[...]
+
+
+def picked(x):
+    return pl.pallas_call(
+        picked_kernel,
+        out_shape=jax.ShapeDtypeStruct(x.shape, x.dtype),
+        compiler_params=params(),
+        cost_estimate=pl.CostEstimate(flops=1000000000, bytes_accessed=4096, transcendentals=0),
+        name="picked",
+    )(x)
 
 
 def after_kernel(x_ref, after_ref, out_ref):
@@ -471,6 +485,7 @@
     kv_decode = lax.ppermute(kv, "grp", SWAP)
     blocks = kv_decode.reshape(2, per_dev, BLK, HD)
     q_same = lax.all_to_all(spread(q), ("zh", "zm"), 0, 0, tiled=True)
+    pick = picked(pick.reshape(1, NCTX)).reshape(NCTX)
     packed = pack(((0, 0, BLK), (1, 0, FIRST)), pick, blocks, steps[0:16])
     q_next = lax.ppermute(held(q_same, packed[0, 0:16]), "zp", SWAP)
     even, odd = jnp.where(zp == 0, q_same, q_next), jnp.where(zp == 0, q_next, q_same)

time: 182 us -> 180 us (0.989)
  the two profiles are of different devices: /device:TPU:56 before, /device:TPU:58 now
where the time goes in v5:
time: 180 us; the launch traced here: 179 us
  starting transfers between devices  73.1 us (41%)
  waiting for transfers between devices  53 us (29%)
  Pallas kernels  35.4 us (20%)
  local copies, waits for them, and re-layouts  12.1 us (7%)
  other arithmetic  4.08 us (2%)
    all_to_all x1, waiting for transfers between devices, local(): lax.all_to_all(after(rest, keys[0, 0:16]), BLOCKS, 0, 0, tiled=True)  27 us
    ppermute x3, starting transfers between devices, local(): lax.ppermute(merged[s], 'zh', [(i, i ^ s) for i in range(NZ // NQ)])  17 us
    all_to_all x1, starting transfers between devices, local(): q_same = lax.all_to_all(spread(q), ('zh', 'zm'), 0, 0, tiled=True)  14.2 us
    pallas_call x2, Pallas kernels, flash(): pl.pallas_call(functools.partial(flash_kernel, other), out_shape=(jax.Sha...  13.4 us
    all_to_all x1, starting transfers between devices, local(): lax.all_to_all(after(rest, keys[0, 0:16]), BLOCKS, 0, 0, tiled=True)  12.5 us
    ppermute x3, starting transfers between devices, local(): lax.ppermute(parts[s], ('zm', 'zp'), [(i, i ^ s) for i in range(NQ)])  10.1 us
    all_to_all x1, waiting for transfers between devices, local(): q_same = lax.all_to_all(spread(q), ('zh', 'zm'), 0, 0, tiled=True)  9.85 us
    all_to_all x1, waiting for transfers between devices, local(): keys = lax.all_to_all(packed, BLOCKS, 0, 0, tiled=True)  8.77 us
  transfers between devices with their start and end apart: 14, of which 5 were waited for; matrix products, arithmetic and copies ran while one was open for 7% of the time, Pallas kernels for 15%

profile of v5, /device:TPU:58, one launch (start us, length us, event | category | flops | bytes accessed | tf_op | source)
XLA Modules:
  0.0 178.7 jit_solution(7464786949662639848)
XLA Ops:
  0.6 0.7 copy-done.8
  1.4 0.7 spread_queries.1
  2.1 14.2 %all-to-all-start = ((bf16[8,96,128]{2,1,0:T(8,128)(2,1)}), bf16[8,96,128]{2,1,0:T(8,128)(2,1)S(1)}, u32[]{:S(2)}, u32[]{:S(2)}) async-start(bf16[8,96,128]{2,1,0:T(8,128)(2,1)} %spread_queries.1), calls=%async_computation | async-start | bytes 393216 | tf_op jit(solution)/shard_map/all_to_all | solution.py:487
  16.3 1.9 %collective-permute-start = (bf16[2,2048,128]{2,1,0:T(8,128)(2,1)}, bf16[2,2048,128]{2,1,0:T(8,128)(2,1)S(1)}, u32[]{:S(2)}, u32[]{:S(2)}) collective-permute-start(bf16[2,2048,128]{2,1,0:T(8,128)(2,1)} %bitcast.74), channel_id=1, source_target_pairs={{0,256},{256,0},{1,257},{257,1},{2,258},{258,2},{3,259},{259,3},{4... | collective-permute-start | bytes 3145736 | tf_op jit(solution)/shard_map/ppermute | solution.py:485
  18.2 0.7 dynamic-slice_reduce_fusion.1
  18.9 0.2 select_reduce_fusion
  19.1 0.7 compare_reduce_fusion
  19.8 0.1 eq.60
  19.9 0.7 slice.73
  20.6 0.1 reshape_squeeze.3
  20.7 0.1 fusion.2
  20.8 0.6 fusion.10.src_ref
  21.4 0.0 collective-permute-done.k_ref.v_ref
  21.4 3.1 %pack_blocks.2 = bf16[32,160,128]{2,1,0:T(8,128)(2,1)S(1)} custom-call(s32[32]{0:T(128)S(1)} %bitcast.72, bf16[2,16,128,128]{3,2,1,0:T(8,128)(2,1)S(1)} %bitcast.65, bf16[16,128]{1,0:T(8,128)(2,1)S(1)} %bitcast.71), custom_call_target="tpu_custom_call" | custom-call | tf_op jit(solution)/shard_map/pack_blocks/pallas_call | solution.py:353
  24.5 9.9 %all-to-all-done.x_ref = bf16[8,96,128]{2,1,0:T(8,128)(2,1)S(1)} async-done(((bf16[8,96,128]{2,1,0:T(8,128)(2,1)}), bf16[8,96,128]{2,1,0:T(8,128)(2,1)S(1)}, u32[]{:S(2)}, u32[]{:S(2)}) %all-to-all-start) | async-done | bytes 196640 | tf_op jit(solution)/shard_map/all_to_all | solution.py:487
  34.4 3.4 %collective-permute-start.1 = (bf16[8,96,128]{2,1,0:T(8,128)(2,1)S(1)}, bf16[8,96,128]{2,1,0:T(8,128)(2,1)S(1)}, u32[]{:S(2)}, u32[]{:S(2)}) collective-permute-start(bf16[8,96,128]{2,1,0:T(8,128)(2,1)S(1)} %held.1), channel_id=1, source_target_pairs={{0,8},{8,0},{1,9},{9,1},{2,10},{10,2},{3,11},{11,3},{4,12},{12,4},... | collective-permute-start | bytes 589832 | tf_op jit(solution)/shard_map/ppermute | solution.py:490
  37.9 0.1 convert_reduce_fusion.flag_ref
  38.0 5.3 %all-to-all-start.1 = ((bf16[32,160,128]{2,1,0:T(8,128)(2,1)}), bf16[32,160,128]{2,1,0:T(8,128)(2,1)S(1)}, u32[]{:S(2)}, u32[]{:S(2)}) async-start(bf16[32,160,128]{2,1,0:T(8,128)(2,1)} %copy-done.1), calls=%async_computation.1 | async-start | bytes 2621440 | tf_op jit(solution)/shard_map/all_to_all | solution.py:495
  43.3 0.6 pad_add_fusion.info_ref
  44.0 1.5 decode_partial.1.da_ref
  45.5 0.0 collective-permute-done.1
  45.5 0.1 select_bitcast_fusion.1
  45.7 2.6 %collective-permute-start.2 = (bf16[1536,128]{1,0:T(8,128)(2,1)S(1)}, bf16[1536,128]{1,0:T(8,128)(2,1)S(1)}, u32[]{:S(2)}, u32[]{:S(2)}) collective-permute-start(bf16[1536,128]{1,0:T(8,128)(2,1)S(1)} %bitcast.67), channel_id=1, source_target_pairs={{0,128},{128,0},{1,129},{129,1},{2,130},{130,2},{3,131},{131,3},{4... | collective-permute-start | bytes 1179656 | tf_op jit(solution)/shard_map/ppermute | solution.py:496
  48.3 6.4 %slab_partial.2 = (bf16[1536,128]{1,0:T(8,128)(2,1)S(1)}, f32[12,128]{1,0:T(8,128)S(1)}) custom-call(s32[3]{0:T(128)S(1)} %copy-done.11, bf16[1536,128]{1,0:T(8,128)(2,1)S(1)} %bitcast.68, bf16[2,2048,128]{2,1,0:T(8,128)(2,1)S(1)} %bitcast.76, bf16[2,2048,128]{2,1,0:T(8,128)(2,1)S(1)} %bitcast.77, f32[8,128]{1,0:T(8,128)S(1)} %slice.75.after_ref), custom_call_target="tpu_custom_call" | custom-call | flops 20000000000 | bytes 1048576 | tf_op jit(solution)/shard_map/slab_partial/pallas_call | solution.py:107
  54.7 0.0 copy-start.4
  54.7 0.0 copy-start.20
  54.8 4.7 %collective-permute-done.2.q_ref = bf16[1536,128]{1,0:T(8,128)(2,1)S(1)} collective-permute-done((bf16[1536,128]{1,0:T(8,128)(2,1)S(1)}, bf16[1536,128]{1,0:T(8,128)(2,1)S(1)}, u32[]{:S(2)}, u32[]{:S(2)}) %collective-permute-start.2) | collective-permute-done | bytes 393248 | tf_op jit(solution)/shard_map/ppermute | solution.py:496
  59.5 7.0 %slab_partial.3 = (bf16[1536,128]{1,0:T(8,128)(2,1)}, f32[12,128]{1,0:T(8,128)S(1)}) custom-call(s32[3]{0:T(128)S(1)} %copy-done.11, bf16[1536,128]{1,0:T(8,128)(2,1)S(1)} %collective-permute-done.2.q_ref, bf16[2,2048,128]{2,1,0:T(8,128)(2,1)S(1)} %bitcast.78, bf16[2,2048,128]{2,1,0:T(8,128)(2,1)S(1)} %bitcast.79, f32[8,128]{1,0:T(8,128)S(1)} %slice.59.after_ref), custom_call_target="tpu_custom_call" | custom-call | flops 20000000000 | bytes 1048576 | tf_op jit(solution)/shard_map/slab_partial/pallas_call | solution.py:107
  66.5 0.6 copy-done.6
  67.1 3.3 %collective-permute-start.3 = (bf16[1536,128]{1,0:T(8,128)(2,1)}, bf16[1536,128]{1,0:T(8,128)(2,1)}, u32[]{:S(2)}, u32[]{:S(2)}) collective-permute-start(bf16[1536,128]{1,0:T(8,128)(2,1)} %get-tuple-element.13), channel_id=1, source_target_pairs={{0,128},{128,0},{1,129},{129,1},{2,130},{130,2},{3,131},{131,3},{4... | collective-permute-start | bytes 1179656 | tf_op jit(solution)/shard_map/ppermute | solution.py:501
  70.4 0.6 fusion.5
  71.0 0.6 broadcast_in_dim.36
  71.6 5.7 %concatenate.6 = f32[64,128]{1,0:T(8,128)} concatenate(f32[12,128]{1,0:T(8,128)} %copy-done.6, f32[4,128]{1,0:T(4,128)} %broadcast_in_dim.36, f32[12,128]{1,0:T(8,128)} %copy-done.4, f32[4,128]{1,0:T(4,128)} %broadcast_in_dim.36, f32[32,128]{1,0:T(8,128)S(1)} %decode_partial.1.da_ref), dimensions={0} | concatenate | bytes 65536 | tf_op jit(solution)/shard_map/concatenate | solution.py:500
  77.3 2.7 %collective-permute-start.4 = (f32[64,128]{1,0:T(8,128)}, f32[64,128]{1,0:T(8,128)S(1)}, u32[]{:S(2)}, u32[]{:S(2)}) collective-permute-start(f32[64,128]{1,0:T(8,128)} %concatenate.6), channel_id=1, source_target_pairs={{0,128},{128,0},{1,129},{129,1},{2,130},{130,2},{3,131},{131,3},{4... | collective-permute-start | bytes 98312 | tf_op jit(solution)/shard_map/ppermute | solution.py:500
  80.0 0.9 pad_maximum_fusion.q_ref
  81.0 2.6 %collective-permute-done.4.sb_ref = f32[64,128]{1,0:T(8,128)S(1)} collective-permute-done((f32[64,128]{1,0:T(8,128)}, f32[64,128]{1,0:T(8,128)S(1)}, u32[]{:S(2)}, u32[]{:S(2)}) %collective-permute-start.4) | collective-permute-done | bytes 32800 | tf_op jit(solution)/shard_map/ppermute | solution.py:500
  83.6 0.0 collective-permute-done.3.b_ref
  83.6 1.5 pair_merge.1
  85.2 2.0 %pack_blocks.3.x_ref = bf16[32,96,128]{2,1,0:T(8,128)(2,1)S(1)} custom-call(s32[32]{0:T(128)S(1)} %bitcast.73, bf16[2,16,128,128]{3,2,1,0:T(8,128)(2,1)S(1)} %bitcast.66, bf16[16,128]{1,0:T(8,128)(2,1)S(1)} %slice_bitcast_fusion.10.after_ref), custom_call_target="tpu_custom_call" | custom-call | tf_op jit(solution)/shard_map/pack_blocks/pallas_call | solution.py:353
  87.2 0.0 copy-start
  87.2 0.9 copy-done
  88.1 3.2 %collective-permute-start.7 = (bf16[496,128]{1,0:T(8,128)(2,1)S(1)}, bf16[496,128]{1,0:T(8,128)(2,1)S(1)}, u32[]{:S(2)}, u32[]{:S(2)}) collective-permute-start(bf16[496,128]{1,0:T(8,128)(2,1)S(1)} %get-tuple-element.20), channel_id=1, source_target_pairs={{0,24},{8,16},{16,8},{24,0},{1,25},{9,17},{17,9},{25,1},{2,26},{10... | collective-permute-start | bytes 380936 | tf_op jit(solution)/shard_map/ppermute | solution.py:503
  91.4 4.7 %collective-permute-start.6 = (bf16[496,128]{1,0:T(8,128)(2,1)S(1)}, bf16[496,128]{1,0:T(8,128)(2,1)S(1)}, u32[]{:S(2)}, u32[]{:S(2)}) collective-permute-start(bf16[496,128]{1,0:T(8,128)(2,1)S(1)} %get-tuple-element.21), channel_id=1, source_target_pairs={{0,16},{8,24},{16,0},{24,8},{1,17},{9,25},{17,1},{25,9},{2,18},{10... | collective-permute-start | bytes 380936 | tf_op jit(solution)/shard_map/ppermute | solution.py:503
  96.1 2.1 %collective-permute-start.5 = (bf16[496,128]{1,0:T(8,128)(2,1)S(1)}, bf16[496,128]{1,0:T(8,128)(2,1)S(1)}, u32[]{:S(2)}, u32[]{:S(2)}) collective-permute-start(bf16[496,128]{1,0:T(8,128)(2,1)S(1)} %get-tuple-element.22), channel_id=1, source_target_pairs={{0,8},{8,0},{16,24},{24,16},{1,9},{9,1},{17,25},{25,17},{2,10},{10... | collective-permute-start | bytes 380936 | tf_op jit(solution)/shard_map/ppermute | solution.py:503
  98.2 8.8 %all-to-all-done.1.a_ref = bf16[32,160,128]{2,1,0:T(8,128)(2,1)S(1)} async-done(((bf16[32,160,128]{2,1,0:T(8,128)(2,1)}), bf16[32,160,128]{2,1,0:T(8,128)(2,1)S(1)}, u32[]{:S(2)}, u32[]{:S(2)}) %all-to-all-start.1) | async-done | bytes 1310752 | tf_op jit(solution)/shard_map/all_to_all | solution.py:495
  107.0 0.6 slice_bitcast_fusion.9.after_ref
  107.6 0.7 after.1
  108.3 12.5 %all-to-all-start.2 = ((bf16[32,96,128]{2,1,0:T(8,128)(2,1)}), bf16[32,96,128]{2,1,0:T(8,128)(2,1)S(1)}, u32[]{:S(2)}, u32[]{:S(2)}) async-start(bf16[32,96,128]{2,1,0:T(8,128)(2,1)} %after.1), calls=%async_computation.2 | async-start | bytes 1572864 | tf_op jit(solution)/shard_map/all_to_all | solution.py:505
  120.8 0.0 collective-permute-done.7.d_ref
  120.8 0.0 collective-permute-done.6.c_ref
  120.8 0.0 collective-permute-done.5.b_ref
  120.8 1.0 quad_merge.1
  121.9 6.4 %collective-permute-start.10 = (bf16[208,128]{1,0:T(8,128)(2,1)S(1)}, bf16[208,128]{1,0:T(8,128)(2,1)S(1)}, u32[]{:S(2)}, u32[]{:S(2)}) collective-permute-start(bf16[208,128]{1,0:T(8,128)(2,1)S(1)} %get-tuple-element.26), channel_id=1, source_target_pairs={{0,96},{32,64},{64,32},{96,0},{1,97},{33,65},{65,33},{97,1},{2,98}... | collective-permute-start | bytes 159752 | tf_op jit(solution)/shard_map/ppermute | solution.py:507
  128.3 8.1 %collective-permute-start.9 = (bf16[208,128]{1,0:T(8,128)(2,1)S(1)}, bf16[208,128]{1,0:T(8,128)(2,1)S(1)}, u32[]{:S(2)}, u32[]{:S(2)}) collective-permute-start(bf16[208,128]{1,0:T(8,128)(2,1)S(1)} %get-tuple-element.27), channel_id=1, source_target_pairs={{0,64},{32,96},{64,0},{96,32},{1,65},{33,97},{65,1},{97,33},{2,66}... | collective-permute-start | bytes 159752 | tf_op jit(solution)/shard_map/ppermute | solution.py:507
  136.5 0.0 copy-start.9
  136.5 2.5 %collective-permute-start.8 = (bf16[208,128]{1,0:T(8,128)(2,1)S(1)}, bf16[208,128]{1,0:T(8,128)(2,1)S(1)}, u32[]{:S(2)}, u32[]{:S(2)}) collective-permute-start(bf16[208,128]{1,0:T(8,128)(2,1)S(1)} %get-tuple-element.28), channel_id=1, source_target_pairs={{0,32},{32,0},{64,96},{96,64},{1,33},{33,1},{65,97},{97,65},{2,34}... | collective-permute-start | bytes 159752 | tf_op jit(solution)/shard_map/ppermute | solution.py:507
  139.0 27.0 %all-to-all-done.2.b_ref = bf16[32,96,128]{2,1,0:T(8,128)(2,1)S(1)} async-done(((bf16[32,96,128]{2,1,0:T(8,128)(2,1)}), bf16[32,96,128]{2,1,0:T(8,128)(2,1)S(1)}, u32[]{:S(2)}, u32[]{:S(2)}) %all-to-all-start.2) | async-done | bytes 786464 | tf_op jit(solution)/shard_map/all_to_all | solution.py:505
  166.0 2.8 %select_slots.1 = bf16[2,12,128,128]{3,2,1,0:T(8,128)(2,1)} custom-call(s32[12]{0:T(128)S(1)} %copy-done.16, bf16[32,160,128]{2,1,0:T(8,128)(2,1)S(1)} %all-to-all-done.1.a_ref, bf16[32,96,128]{2,1,0:T(8,128)(2,1)S(1)} %all-to-all-done.2.b_ref), custom_call_target="tpu_custom_call" | custom-call | tf_op jit(solution)/shard_map/select_slots/pallas_call | solution.py:423
  168.8 0.7 slice_bitcast_fusion.8.after_ref
  169.5 0.0 collective-permute-done.10.d_ref
  169.5 0.0 collective-permute-done.9.c_ref
  169.5 1.4 final_merge.1
  171.0 0.6 copy-done.18
  171.6 7.2 %heavy_columns.1 = f32[1,2048]{1,0:T(1,128)} custom-call(s32[3]{0:T(128)} %pad_add_fusion.info_ref, bf16[3072,128]{1,0:T(8,128)(2,1)} %pad_maximum_fusion.q_ref, bf16[2,2048,128]{2,1,0:T(8,128)(2,1)} %bitcast.75, f32[24,128]{1,0:T(8,128)} %copy-done.18), custom_call_target="tpu_custom_call" | custom-call | flops 1610612736 | bytes 524288 | tf_op jit(solution)/shard_map/heavy_columns/pallas_call | solution.py:319
  (49 shorter events, 0.3 us)
Async XLA Ops:
  0.6 0.7 copy-start.8
  2.1 32.3 %all-to-all-start = ((bf16[8,96,128]{2,1,0:T(8,128)(2,1)}), bf16[8,96,128]{2,1,0:T(8,128)(2,1)S(1)}, u32[]{:S(2)}, u32[]{:S(2)}) async-start(bf16[8,96,128]{2,1,0:T(8,128)(2,1)} %spread_queries.1), calls=%async_computation | async-start | bytes 393216 | tf_op jit(solution)/shard_map/all_to_all | solution.py:487
  16.3 5.2 %collective-permute-start = (bf16[2,2048,128]{2,1,0:T(8,128)(2,1)}, bf16[2,2048,128]{2,1,0:T(8,128)(2,1)S(1)}, u32[]{:S(2)}, u32[]{:S(2)}) collective-permute-start(bf16[2,2048,128]{2,1,0:T(8,128)(2,1)} %bitcast.74), channel_id=1, source_target_pairs={{0,256},{256,0},{1,257},{257,1},{2,258},{258,2},{3,259},{259,3},{4... | collective-permute-start | bytes 3145736 | tf_op jit(solution)/shard_map/ppermute | solution.py:485
  20.7 3.8 %copy-start.14 = (s32[1,32]{1,0:T(1,128)}, s32[1,32]{1,0:T(1,128)S(1)}, u32[]{:S(2)}) copy-start(s32[1,32]{1,0:T(1,128)S(1)} %picked.1) | copy-start | bytes 388
  24.5 13.3 %copy-start.1 = (bf16[32,160,128]{2,1,0:T(8,128)(2,1)}, bf16[32,160,128]{2,1,0:T(8,128)(2,1)S(1)}, u32[]{:S(2)}) copy-start(bf16[32,160,128]{2,1,0:T(8,128)(2,1)S(1)} %pack_blocks.2) | copy-start | bytes 3932164
  34.4 11.1 %collective-permute-start.1 = (bf16[8,96,128]{2,1,0:T(8,128)(2,1)S(1)}, bf16[8,96,128]{2,1,0:T(8,128)(2,1)S(1)}, u32[]{:S(2)}, u32[]{:S(2)}) collective-permute-start(bf16[8,96,128]{2,1,0:T(8,128)(2,1)S(1)} %held.1), channel_id=1, source_target_pairs={{0,8},{8,0},{1,9},{9,1},{2,10},{10,2},{3,11},{11,3},{4,12},{12,4},... | collective-permute-start | bytes 589832 | tf_op jit(solution)/shard_map/ppermute | solution.py:490
  38.0 6.0 %copy-start.19 = (bf16[1,2,1,12,128]{4,1,3,2,0:T(2,128)(2,1)S(1)}, bf16[1,2,1,12,128]{4,1,3,2,0:T(2,128)(2,1)}, u32[]{:S(2)}) copy-start(bf16[1,2,1,12,128]{4,1,3,2,0:T(2,128)(2,1)} %param.10) | copy-start | bytes 18436
  38.0 69.0 %all-to-all-start.1 = ((bf16[32,160,128]{2,1,0:T(8,128)(2,1)}), bf16[32,160,128]{2,1,0:T(8,128)(2,1)S(1)}, u32[]{:S(2)}, u32[]{:S(2)}) async-start(bf16[32,160,128]{2,1,0:T(8,128)(2,1)} %copy-done.1), calls=%async_computation.1 | async-start | bytes 2621440 | tf_op jit(solution)/shard_map/all_to_all | solution.py:495
  44.0 1.6 copy-start.2
  45.5 2.8 %copy-start.11 = (s32[3]{0:T(128)S(1)}, s32[3]{0:T(128)}, u32[]{:S(2)}) copy-start(s32[3]{0:T(128)} %pad_add_fusion.info_ref) | copy-start | bytes 40
  45.5 2.8 %copy-start.17 = (bf16[1,2,2048,1,128]{4,2,3,1,0:T(8,128)(2,1)S(1)}, bf16[1,2,2048,1,128]{4,2,3,1,0:T(8,128)(2,1)}, u32[]{:S(2)}) copy-start(bf16[1,2,2048,1,128]{4,2,3,1,0:T(8,128)(2,1)} %param.7) | copy-start | bytes 3145732
  45.7 13.8 %collective-permute-start.2 = (bf16[1536,128]{1,0:T(8,128)(2,1)S(1)}, bf16[1536,128]{1,0:T(8,128)(2,1)S(1)}, u32[]{:S(2)}, u32[]{:S(2)}) collective-permute-start(bf16[1536,128]{1,0:T(8,128)(2,1)S(1)} %bitcast.67), channel_id=1, source_target_pairs={{0,128},{128,0},{1,129},{129,1},{2,130},{130,2},{3,131},{131,3},{4... | collective-permute-start | bytes 1179656 | tf_op jit(solution)/shard_map/ppermute | solution.py:496
  54.7 11.8 %copy-start.4 = (f32[12,128]{1,0:T(8,128)}, f32[12,128]{1,0:T(8,128)S(1)}, u32[]{:S(2)}) copy-start(f32[12,128]{1,0:T(8,128)S(1)} %get-tuple-element.12.la_ref) | copy-start | bytes 18436
  54.7 15.7 %copy-start.20 = (bf16[1,2,2,1,128]{4,2,3,1,0:T(2,128)(2,1)S(1)}, bf16[1,2,2,1,128]{4,2,3,1,0:T(2,128)(2,1)}, u32[]{:S(2)}) copy-start(bf16[1,2,2,1,128]{4,2,3,1,0:T(2,128)(2,1)} %param.11) | copy-start | bytes 3076
  66.5 0.6 copy-start.6
  67.1 16.5 %collective-permute-start.3 = (bf16[1536,128]{1,0:T(8,128)(2,1)}, bf16[1536,128]{1,0:T(8,128)(2,1)}, u32[]{:S(2)}, u32[]{:S(2)}) collective-permute-start(bf16[1536,128]{1,0:T(8,128)(2,1)} %get-tuple-element.13), channel_id=1, source_target_pairs={{0,128},{128,0},{1,129},{129,1},{2,130},{130,2},{3,131},{131,3},{4... | collective-permute-start | bytes 1179656 | tf_op jit(solution)/shard_map/ppermute | solution.py:501
  77.3 6.3 %copy-start.5 = (f32[12,128]{1,0:T(8,128)S(1)}, f32[12,128]{1,0:T(8,128)}, u32[]{:S(2)}) copy-start(f32[12,128]{1,0:T(8,128)} %copy-done.4) | copy-start | bytes 18436
  77.3 6.3 %copy-start.7 = (f32[12,128]{1,0:T(8,128)S(1)}, f32[12,128]{1,0:T(8,128)}, u32[]{:S(2)}) copy-start(f32[12,128]{1,0:T(8,128)} %copy-done.6) | copy-start | bytes 18436
  77.3 6.3 %copy-start.12 = (s32[3]{0:T(128)S(1)}, s32[3]{0:T(128)}, u32[]{:S(2)}) copy-start(s32[3]{0:T(128)} %pad_add_fusion.info_ref) | copy-start | bytes 40
  77.3 7.8 %copy-start.15 = (s32[1,32]{1,0:T(1,128)S(1)}, s32[1,32]{1,0:T(1,128)}, u32[]{:S(2)}) copy-start(s32[1,32]{1,0:T(1,128)} %copy-done.14) | copy-start | bytes 388
  77.3 6.3 %collective-permute-start.4 = (f32[64,128]{1,0:T(8,128)}, f32[64,128]{1,0:T(8,128)S(1)}, u32[]{:S(2)}, u32[]{:S(2)}) collective-permute-start(f32[64,128]{1,0:T(8,128)} %concatenate.6), channel_id=1, source_target_pairs={{0,128},{128,0},{1,129},{129,1},{2,130},{130,2},{3,131},{131,3},{4... | collective-permute-start | bytes 98312 | tf_op jit(solution)/shard_map/ppermute | solution.py:500
  87.2 0.9 copy-start
  88.1 32.7 %collective-permute-start.7 = (bf16[496,128]{1,0:T(8,128)(2,1)S(1)}, bf16[496,128]{1,0:T(8,128)(2,1)S(1)}, u32[]{:S(2)}, u32[]{:S(2)}) collective-permute-start(bf16[496,128]{1,0:T(8,128)(2,1)S(1)} %get-tuple-element.20), channel_id=1, source_target_pairs={{0,24},{8,16},{16,8},{24,0},{1,25},{9,17},{17,9},{25,1},{2,26},{10... | collective-permute-start | bytes 380936 | tf_op jit(solution)/shard_map/ppermute | solution.py:503
  91.4 29.4 %collective-permute-start.6 = (bf16[496,128]{1,0:T(8,128)(2,1)S(1)}, bf16[496,128]{1,0:T(8,128)(2,1)S(1)}, u32[]{:S(2)}, u32[]{:S(2)}) collective-permute-start(bf16[496,128]{1,0:T(8,128)(2,1)S(1)} %get-tuple-element.21), channel_id=1, source_target_pairs={{0,16},{8,24},{16,0},{24,8},{1,17},{9,25},{17,1},{25,9},{2,18},{10... | collective-permute-start | bytes 380936 | tf_op jit(solution)/shard_map/ppermute | solution.py:503
  96.1 24.7 %collective-permute-start.5 = (bf16[496,128]{1,0:T(8,128)(2,1)S(1)}, bf16[496,128]{1,0:T(8,128)(2,1)S(1)}, u32[]{:S(2)}, u32[]{:S(2)}) collective-permute-start(bf16[496,128]{1,0:T(8,128)(2,1)S(1)} %get-tuple-element.22), channel_id=1, source_target_pairs={{0,8},{8,0},{16,24},{24,16},{1,9},{9,1},{17,25},{25,17},{2,10},{10... | collective-permute-start | bytes 380936 | tf_op jit(solution)/shard_map/ppermute | solution.py:503
  107.6 13.2 %copy-start.13 = (s32[3]{0:T(128)S(1)}, s32[3]{0:T(128)}, u32[]{:S(2)}) copy-start(s32[3]{0:T(128)} %pad_add_fusion.info_ref) | copy-start | bytes 40
  108.3 57.7 %all-to-all-start.2 = ((bf16[32,96,128]{2,1,0:T(8,128)(2,1)}), bf16[32,96,128]{2,1,0:T(8,128)(2,1)S(1)}, u32[]{:S(2)}, u32[]{:S(2)}) async-start(bf16[32,96,128]{2,1,0:T(8,128)(2,1)} %after.1), calls=%async_computation.2 | async-start | bytes 1572864 | tf_op jit(solution)/shard_map/all_to_all | solution.py:505
  120.8 45.1 %copy-start.16 = (s32[12]{0:T(128)S(1)}, s32[12]{0:T(128)}, u32[]{:S(2)}) copy-start(s32[12]{0:T(128)} %fusion.10.src_ref) | copy-start | bytes 148
  121.9 47.6 %collective-permute-start.10 = (bf16[208,128]{1,0:T(8,128)(2,1)S(1)}, bf16[208,128]{1,0:T(8,128)(2,1)S(1)}, u32[]{:S(2)}, u32[]{:S(2)}) collective-permute-start(bf16[208,128]{1,0:T(8,128)(2,1)S(1)} %get-tuple-element.26), channel_id=1, source_target_pairs={{0,96},{32,64},{64,32},{96,0},{1,97},{33,65},{65,33},{97,1},{2,98}... | collective-permute-start | bytes 159752 | tf_op jit(solution)/shard_map/ppermute | solution.py:507
  128.3 41.2 %collective-permute-start.9 = (bf16[208,128]{1,0:T(8,128)(2,1)S(1)}, bf16[208,128]{1,0:T(8,128)(2,1)S(1)}, u32[]{:S(2)}, u32[]{:S(2)}) collective-permute-start(bf16[208,128]{1,0:T(8,128)(2,1)S(1)} %get-tuple-element.27), channel_id=1, source_target_pairs={{0,64},{32,96},{64,0},{96,32},{1,65},{33,97},{65,1},{97,33},{2,66}... | collective-permute-start | bytes 159752 | tf_op jit(solution)/shard_map/ppermute | solution.py:507
  136.5 33.1 %copy-start.3 = (bf16[128,128]{1,0:T(8,128)(2,1)S(1)}, bf16[128,128]{1,0:T(8,128)(2,1)}, u32[]{:S(2)}) copy-start(bf16[128,128]{1,0:T(8,128)(2,1)} %copy-done.2) | copy-start | bytes 98308
  136.5 33.1 %copy-start.9 = (bf16[16,128]{1,0:T(8,128)(2,1)S(1)}, bf16[16,128]{1,0:T(8,128)(2,1)}, u32[]{:S(2)}) copy-start(bf16[16,128]{1,0:T(8,128)(2,1)} %get-tuple-element.30.nv_ref) | copy-start | bytes 12292
  136.5 33.0 %copy-start.10 = (bf16[16,128]{1,0:T(8,128)(2,1)S(1)}, bf16[16,128]{1,0:T(8,128)(2,1)}, u32[]{:S(2)}) copy-start(bf16[16,128]{1,0:T(8,128)(2,1)} %get-tuple-element.31.nk_ref) | copy-start | bytes 12292
  136.5 33.0 %collective-permute-start.8 = (bf16[208,128]{1,0:T(8,128)(2,1)S(1)}, bf16[208,128]{1,0:T(8,128)(2,1)S(1)}, u32[]{:S(2)}, u32[]{:S(2)}) collective-permute-start(bf16[208,128]{1,0:T(8,128)(2,1)S(1)} %get-tuple-element.28), channel_id=1, source_target_pairs={{0,32},{32,0},{64,96},{96,64},{1,33},{33,1},{65,97},{97,65},{2,34}... | collective-permute-start | bytes 159752 | tf_op jit(solution)/shard_map/ppermute | solution.py:507
  171.0 0.6 copy-start.18

commit v6 on v5

--- a/solution.py
+++ b/solution.py
@@ -29,7 +29,7 @@
 LR = HALF // HD
 NQ = 4
 QROWS = NZ // NQ * ROWS
-FIRST = 32
+FIRST = 16
 DECR = 6 * LR
 DSTAT = DECR + STEPR
 TAIL = 112

time: 180 us -> 180 us (level)
  the two profiles are of different devices: /device:TPU:58 before, /device:TPU:40 now
where the time goes in v6:
time: 180 us; the launch traced here: 179 us
  starting transfers between devices  74.3 us (41%)
  waiting for transfers between devices  60.5 us (34%)
  Pallas kernels  34.6 us (19%)
  local copies, waits for them, and re-layouts  5.95 us (3%)
  other arithmetic  2.97 us (2%)
    all_to_all x1, waiting for transfers between devices, local(): lax.all_to_all(after(rest, keys[0, 0:16]), BLOCKS, 0, 0, tiled=True)  33.6 us
    ppermute x3, starting transfers between devices, local(): lax.ppermute(merged[s], 'zh', [(i, i ^ s) for i in range(NZ // NQ)])  17 us
    all_to_all x1, starting transfers between devices, local(): q_same = lax.all_to_all(spread(q), ('zh', 'zm'), 0, 0, tiled=True)  14.2 us
    pallas_call x2, Pallas kernels, flash(): pl.pallas_call(functools.partial(flash_kernel, other), out_shape=(jax.Sha...  13.3 us
    all_to_all x1, starting transfers between devices, local(): lax.all_to_all(after(rest, keys[0, 0:16]), BLOCKS, 0, 0, tiled=True)  12.4 us
    ppermute x3, starting transfers between devices, local(): lax.ppermute(parts[s], ('zm', 'zp'), [(i, i ^ s) for i in range(NQ)])  10.7 us
    all_to_all x1, waiting for transfers between devices, local(): q_same = lax.all_to_all(spread(q), ('zh', 'zm'), 0, 0, tiled=True)  9.77 us
    pallas_call x1, Pallas kernels, heavy(): pl.pallas_call(heavy_kernel, out_shape=jax.ShapeDtypeStruct((1, CTXL), F3...  7.16 us
  transfers between devices with their start and end apart: 14, of which 5 were waited for; matrix products, arithmetic and copies ran while one was open for 4% of the time, Pallas kernels for 14%

profile of v6, /device:TPU:40, one launch (start us, length us, event | category | flops | bytes accessed | tf_op | source)
XLA Modules:
  0.0 179.3 jit_solution(10300467100004536576)
XLA Ops:
  0.6 0.0 copy-start.1
  0.6 0.7 copy-done.1
  1.4 0.7 spread_queries.1
  2.1 14.2 %all-to-all-start = ((bf16[8,96,128]{2,1,0:T(8,128)(2,1)}), bf16[8,96,128]{2,1,0:T(8,128)(2,1)S(1)}, u32[]{:S(2)}, u32[]{:S(2)}) async-start(bf16[8,96,128]{2,1,0:T(8,128)(2,1)} %spread_queries.1), calls=%async_computation | async-start | bytes 393216 | tf_op jit(solution)/shard_map/all_to_all | solution.py:487
  16.3 1.9 %collective-permute-start = (bf16[2,2048,128]{2,1,0:T(8,128)(2,1)}, bf16[2,2048,128]{2,1,0:T(8,128)(2,1)S(1)}, u32[]{:S(2)}, u32[]{:S(2)}) collective-permute-start(bf16[2,2048,128]{2,1,0:T(8,128)(2,1)} %bitcast.74), channel_id=1, source_target_pairs={{0,256},{256,0},{1,257},{257,1},{2,258},{258,2},{3,259},{259,3},{4... | collective-permute-start | bytes 3145736 | tf_op jit(solution)/shard_map/ppermute | solution.py:485
  18.2 0.7 dynamic-slice_reduce_fusion.1
  18.9 0.2 select_reduce_fusion
  19.1 0.7 compare_reduce_fusion
  19.9 0.1 eq.60
  19.9 0.7 slice.73
  20.6 0.1 reshape_squeeze.3
  20.7 0.7 pad.8.q_ref
  21.4 0.1 pad_add_fusion.info_ref
  21.5 0.0 copy-start.2
  21.5 0.1 convert_reduce_fusion.flag_ref
  21.6 0.1 fusion.2
  21.7 0.0 collective-permute-done.k_ref.v_ref
  21.7 2.2 %pack_blocks.2 = bf16[32,144,128]{2,1,0:T(8,128)(2,1)} custom-call(s32[32]{0:T(128)S(1)} %bitcast.72, bf16[2,16,128,128]{3,2,1,0:T(8,128)(2,1)S(1)} %bitcast.65, bf16[16,128]{1,0:T(8,128)(2,1)S(1)} %bitcast.71), custom_call_target="tpu_custom_call" | custom-call | tf_op jit(solution)/shard_map/pack_blocks/pallas_call | solution.py:353
  23.9 0.7 slice_bitcast_fusion.11.after_ref
  24.6 9.8 %all-to-all-done.x_ref = bf16[8,96,128]{2,1,0:T(8,128)(2,1)S(1)} async-done(((bf16[8,96,128]{2,1,0:T(8,128)(2,1)}), bf16[8,96,128]{2,1,0:T(8,128)(2,1)S(1)}, u32[]{:S(2)}, u32[]{:S(2)}) %all-to-all-start) | async-done | bytes 196640 | tf_op jit(solution)/shard_map/all_to_all | solution.py:487
  34.4 3.4 %collective-permute-start.1 = (bf16[8,96,128]{2,1,0:T(8,128)(2,1)S(1)}, bf16[8,96,128]{2,1,0:T(8,128)(2,1)S(1)}, u32[]{:S(2)}, u32[]{:S(2)}) collective-permute-start(bf16[8,96,128]{2,1,0:T(8,128)(2,1)S(1)} %held.1), channel_id=1, source_target_pairs={{0,8},{8,0},{1,9},{9,1},{2,10},{10,2},{3,11},{11,3},{4,12},{12,4},... | collective-permute-start | bytes 589832 | tf_op jit(solution)/shard_map/ppermute | solution.py:490
  37.9 5.2 %all-to-all-start.1 = ((bf16[32,144,128]{2,1,0:T(8,128)(2,1)}), bf16[32,144,128]{2,1,0:T(8,128)(2,1)S(1)}, u32[]{:S(2)}, u32[]{:S(2)}) async-start(bf16[32,144,128]{2,1,0:T(8,128)(2,1)} %pack_blocks.2), calls=%async_computation.1 | async-start | bytes 2359296 | tf_op jit(solution)/shard_map/all_to_all | solution.py:495
  43.1 1.5 decode_partial.1.da_ref
  44.7 0.0 collective-permute-done.1
  44.8 3.5 %collective-permute-start.2 = (bf16[1536,128]{1,0:T(8,128)(2,1)S(1)}, bf16[1536,128]{1,0:T(8,128)(2,1)S(1)}, u32[]{:S(2)}, u32[]{:S(2)}) collective-permute-start(bf16[1536,128]{1,0:T(8,128)(2,1)S(1)} %bitcast.67), channel_id=1, source_target_pairs={{0,128},{128,0},{1,129},{129,1},{2,130},{130,2},{3,131},{131,3},{4... | collective-permute-start | bytes 1179656 | tf_op jit(solution)/shard_map/ppermute | solution.py:496
  48.3 0.0 copy-done.3
  48.3 6.4 %slab_partial.2 = (bf16[1536,128]{1,0:T(8,128)(2,1)S(1)}, f32[12,128]{1,0:T(8,128)S(1)}) custom-call(s32[3]{0:T(128)S(1)} %pad_add_fusion.info_ref, bf16[1536,128]{1,0:T(8,128)(2,1)S(1)} %bitcast.68, bf16[2,2048,128]{2,1,0:T(8,128)(2,1)S(1)} %bitcast.76, bf16[2,2048,128]{2,1,0:T(8,128)(2,1)S(1)} %bitcast.77, f32[8,128]{1,0:T(8,128)S(1)} %slice.75.after_ref), custom_call_target="tpu_custom_call" | custom-call | flops 20000000000 | bytes 1048576 | tf_op jit(solution)/shard_map/slab_partial/pallas_call | solution.py:107
  54.7 0.0 copy-start.5
  54.7 4.5 %collective-permute-done.2.q_ref = bf16[1536,128]{1,0:T(8,128)(2,1)S(1)} collective-permute-done((bf16[1536,128]{1,0:T(8,128)(2,1)S(1)}, bf16[1536,128]{1,0:T(8,128)(2,1)S(1)}, u32[]{:S(2)}, u32[]{:S(2)}) %collective-permute-start.2) | collective-permute-done | bytes 393248 | tf_op jit(solution)/shard_map/ppermute | solution.py:496
  59.3 7.0 %slab_partial.3 = (bf16[1536,128]{1,0:T(8,128)(2,1)}, f32[12,128]{1,0:T(8,128)S(1)}) custom-call(s32[3]{0:T(128)S(1)} %pad_add_fusion.info_ref, bf16[1536,128]{1,0:T(8,128)(2,1)S(1)} %collective-permute-done.2.q_ref, bf16[2,2048,128]{2,1,0:T(8,128)(2,1)S(1)} %bitcast.78, bf16[2,2048,128]{2,1,0:T(8,128)(2,1)S(1)} %bitcast.79, f32[8,128]{1,0:T(8,128)S(1)} %slice.59.after_ref), custom_call_target="tpu_custom_call" | custom-call | flops 20000000000 | bytes 1048576 | tf_op jit(solution)/shard_map/slab_partial/pallas_call | solution.py:107
  66.3 2.9 %collective-permute-start.3 = (bf16[1536,128]{1,0:T(8,128)(2,1)}, bf16[1536,128]{1,0:T(8,128)(2,1)}, u32[]{:S(2)}, u32[]{:S(2)}) collective-permute-start(bf16[1536,128]{1,0:T(8,128)(2,1)} %get-tuple-element.13), channel_id=1, source_target_pairs={{0,128},{128,0},{1,129},{129,1},{2,130},{130,2},{3,131},{131,3},{4... | collective-permute-start | bytes 1179656 | tf_op jit(solution)/shard_map/ppermute | solution.py:501
  69.1 0.0 copy-done.5
  69.2 3.0 %collective-permute-start.4 = (f32[64,128]{1,0:T(8,128)S(1)}, f32[64,128]{1,0:T(8,128)S(1)}, u32[]{:S(2)}, u32[]{:S(2)}) collective-permute-start(f32[64,128]{1,0:T(8,128)S(1)} %concatenate.6), channel_id=1, source_target_pairs={{0,128},{128,0},{1,129},{129,1},{2,130},{130,2},{3,131},{131,3},{4... | collective-permute-start | bytes 98312 | tf_op jit(solution)/shard_map/ppermute | solution.py:500
  72.2 0.9 pad_maximum_fusion.q_ref
  73.1 7.1 %collective-permute-done.4.sb_ref = f32[64,128]{1,0:T(8,128)S(1)} collective-permute-done((f32[64,128]{1,0:T(8,128)S(1)}, f32[64,128]{1,0:T(8,128)S(1)}, u32[]{:S(2)}, u32[]{:S(2)}) %collective-permute-start.4) | collective-permute-done | bytes 32800 | tf_op jit(solution)/shard_map/ppermute | solution.py:500
  80.2 0.0 collective-permute-done.3.b_ref
  80.2 1.5 pair_merge.1
  81.7 2.2 %pack_blocks.3.x_ref = bf16[32,112,128]{2,1,0:T(8,128)(2,1)S(1)} custom-call(s32[32]{0:T(128)S(1)} %bitcast.73, bf16[2,16,128,128]{3,2,1,0:T(8,128)(2,1)S(1)} %bitcast.66, bf16[16,128]{1,0:T(8,128)(2,1)S(1)} %slice_bitcast_fusion.10.after_ref), custom_call_target="tpu_custom_call" | custom-call | tf_op jit(solution)/shard_map/pack_blocks/pallas_call | solution.py:353
  83.9 0.0 copy-start
  83.9 1.0 copy-done
  84.9 4.5 %collective-permute-start.7 = (bf16[496,128]{1,0:T(8,128)(2,1)S(1)}, bf16[496,128]{1,0:T(8,128)(2,1)S(1)}, u32[]{:S(2)}, u32[]{:S(2)}) collective-permute-start(bf16[496,128]{1,0:T(8,128)(2,1)S(1)} %get-tuple-element.20), channel_id=1, source_target_pairs={{0,24},{8,16},{16,8},{24,0},{1,25},{9,17},{17,9},{25,1},{2,26},{10... | collective-permute-start | bytes 380936 | tf_op jit(solution)/shard_map/ppermute | solution.py:503
  89.4 2.9 %collective-permute-start.6 = (bf16[496,128]{1,0:T(8,128)(2,1)S(1)}, bf16[496,128]{1,0:T(8,128)(2,1)S(1)}, u32[]{:S(2)}, u32[]{:S(2)}) collective-permute-start(bf16[496,128]{1,0:T(8,128)(2,1)S(1)} %get-tuple-element.21), channel_id=1, source_target_pairs={{0,16},{8,24},{16,0},{24,8},{1,17},{9,25},{17,1},{25,9},{2,18},{10... | collective-permute-start | bytes 380936 | tf_op jit(solution)/shard_map/ppermute | solution.py:503
  92.3 3.3 %collective-permute-start.5 = (bf16[496,128]{1,0:T(8,128)(2,1)S(1)}, bf16[496,128]{1,0:T(8,128)(2,1)S(1)}, u32[]{:S(2)}, u32[]{:S(2)}) collective-permute-start(bf16[496,128]{1,0:T(8,128)(2,1)S(1)} %get-tuple-element.22), channel_id=1, source_target_pairs={{0,8},{8,0},{16,24},{24,16},{1,9},{9,1},{17,25},{25,17},{2,10},{10... | collective-permute-start | bytes 380936 | tf_op jit(solution)/shard_map/ppermute | solution.py:503
  95.6 5.5 %all-to-all-done.1.a_ref = bf16[32,144,128]{2,1,0:T(8,128)(2,1)S(1)} async-done(((bf16[32,144,128]{2,1,0:T(8,128)(2,1)}), bf16[32,144,128]{2,1,0:T(8,128)(2,1)S(1)}, u32[]{:S(2)}, u32[]{:S(2)}) %all-to-all-start.1) | async-done | bytes 1179680 | tf_op jit(solution)/shard_map/all_to_all | solution.py:495
  101.1 0.6 slice_bitcast_fusion.9.after_ref
  101.7 0.7 after.1
  102.4 12.4 %all-to-all-start.2 = ((bf16[32,112,128]{2,1,0:T(8,128)(2,1)}), bf16[32,112,128]{2,1,0:T(8,128)(2,1)S(1)}, u32[]{:S(2)}, u32[]{:S(2)}) async-start(bf16[32,112,128]{2,1,0:T(8,128)(2,1)} %after.1), calls=%async_computation.2 | async-start | bytes 1835008 | tf_op jit(solution)/shard_map/all_to_all | solution.py:505
  114.9 0.0 collective-permute-done.7.d_ref
  114.9 0.0 collective-permute-done.6.c_ref
  114.9 0.0 collective-permute-done.5.b_ref
  114.9 1.0 quad_merge.1
  116.0 6.4 %collective-permute-start.10 = (bf16[208,128]{1,0:T(8,128)(2,1)S(1)}, bf16[208,128]{1,0:T(8,128)(2,1)S(1)}, u32[]{:S(2)}, u32[]{:S(2)}) collective-permute-start(bf16[208,128]{1,0:T(8,128)(2,1)S(1)} %get-tuple-element.26), channel_id=1, source_target_pairs={{0,96},{32,64},{64,32},{96,0},{1,97},{33,65},{65,33},{97,1},{2,98}... | collective-permute-start | bytes 159752 | tf_op jit(solution)/shard_map/ppermute | solution.py:507
  122.4 8.1 %collective-permute-start.9 = (bf16[208,128]{1,0:T(8,128)(2,1)S(1)}, bf16[208,128]{1,0:T(8,128)(2,1)S(1)}, u32[]{:S(2)}, u32[]{:S(2)}) collective-permute-start(bf16[208,128]{1,0:T(8,128)(2,1)S(1)} %get-tuple-element.27), channel_id=1, source_target_pairs={{0,64},{32,96},{64,0},{96,32},{1,65},{33,97},{65,1},{97,33},{2,66}... | collective-permute-start | bytes 159752 | tf_op jit(solution)/shard_map/ppermute | solution.py:507
  130.5 2.5 %collective-permute-start.8 = (bf16[208,128]{1,0:T(8,128)(2,1)S(1)}, bf16[208,128]{1,0:T(8,128)(2,1)S(1)}, u32[]{:S(2)}, u32[]{:S(2)}) collective-permute-start(bf16[208,128]{1,0:T(8,128)(2,1)S(1)} %get-tuple-element.28), channel_id=1, source_target_pairs={{0,32},{32,0},{64,96},{96,64},{1,33},{33,1},{65,97},{97,65},{2,34}... | collective-permute-start | bytes 159752 | tf_op jit(solution)/shard_map/ppermute | solution.py:507
  133.0 33.6 %all-to-all-done.2.b_ref = bf16[32,112,128]{2,1,0:T(8,128)(2,1)S(1)} async-done(((bf16[32,112,128]{2,1,0:T(8,128)(2,1)}), bf16[32,112,128]{2,1,0:T(8,128)(2,1)S(1)}, u32[]{:S(2)}, u32[]{:S(2)}) %all-to-all-start.2) | async-done | bytes 917536 | tf_op jit(solution)/shard_map/all_to_all | solution.py:505
  166.6 2.8 %select_slots.1 = bf16[2,12,128,128]{3,2,1,0:T(8,128)(2,1)} custom-call(s32[12]{0:T(128)S(1)} %fusion.10.src_ref, bf16[32,144,128]{2,1,0:T(8,128)(2,1)S(1)} %all-to-all-done.1.a_ref, bf16[32,112,128]{2,1,0:T(8,128)(2,1)S(1)} %all-to-all-done.2.b_ref), custom_call_target="tpu_custom_call" | custom-call | tf_op jit(solution)/shard_map/select_slots/pallas_call | solution.py:423
  169.4 0.7 slice_bitcast_fusion.8.after_ref
  170.1 0.0 collective-permute-done.10.d_ref
  170.1 0.0 collective-permute-done.9.c_ref
  170.1 0.0 collective-permute-done.8.b_ref
  170.1 0.0 copy-done.2
  170.1 1.4 final_merge.1
  171.6 0.6 copy-done.4
  172.2 7.2 %heavy_columns.1 = f32[1,2048]{1,0:T(1,128)} custom-call(s32[3]{0:T(128)} %copy-done.2, bf16[3072,128]{1,0:T(8,128)(2,1)} %pad_maximum_fusion.q_ref, bf16[2,2048,128]{2,1,0:T(8,128)(2,1)} %bitcast.75, f32[24,128]{1,0:T(8,128)} %copy-done.4), custom_call_target="tpu_custom_call" | custom-call | flops 1610612736 | bytes 524288 | tf_op jit(solution)/shard_map/heavy_columns/pallas_call | solution.py:319
  (19 shorter events, 0.3 us)
Async XLA Ops:
  0.6 0.7 copy-start.1
  2.1 32.3 %all-to-all-start = ((bf16[8,96,128]{2,1,0:T(8,128)(2,1)}), bf16[8,96,128]{2,1,0:T(8,128)(2,1)S(1)}, u32[]{:S(2)}, u32[]{:S(2)}) async-start(bf16[8,96,128]{2,1,0:T(8,128)(2,1)} %spread_queries.1), calls=%async_computation | async-start | bytes 393216 | tf_op jit(solution)/shard_map/all_to_all | solution.py:487
  16.3 5.5 %collective-permute-start = (bf16[2,2048,128]{2,1,0:T(8,128)(2,1)}, bf16[2,2048,128]{2,1,0:T(8,128)(2,1)S(1)}, u32[]{:S(2)}, u32[]{:S(2)}) collective-permute-start(bf16[2,2048,128]{2,1,0:T(8,128)(2,1)} %bitcast.74), channel_id=1, source_target_pairs={{0,256},{256,0},{1,257},{257,1},{2,258},{258,2},{3,259},{259,3},{4... | collective-permute-start | bytes 3145736 | tf_op jit(solution)/shard_map/ppermute | solution.py:485
  21.5 148.6 %copy-start.2 = (s32[3]{0:T(128)}, s32[3]{0:T(128)S(1)}, u32[]{:S(2)}) copy-start(s32[3]{0:T(128)S(1)} %pad_add_fusion.info_ref) | copy-start | bytes 40
  34.4 10.3 %collective-permute-start.1 = (bf16[8,96,128]{2,1,0:T(8,128)(2,1)S(1)}, bf16[8,96,128]{2,1,0:T(8,128)(2,1)S(1)}, u32[]{:S(2)}, u32[]{:S(2)}) collective-permute-start(bf16[8,96,128]{2,1,0:T(8,128)(2,1)S(1)} %held.1), channel_id=1, source_target_pairs={{0,8},{8,0},{1,9},{9,1},{2,10},{10,2},{3,11},{11,3},{4,12},{12,4},... | collective-permute-start | bytes 589832 | tf_op jit(solution)/shard_map/ppermute | solution.py:490
  37.9 63.2 %all-to-all-start.1 = ((bf16[32,144,128]{2,1,0:T(8,128)(2,1)}), bf16[32,144,128]{2,1,0:T(8,128)(2,1)S(1)}, u32[]{:S(2)}, u32[]{:S(2)}) async-start(bf16[32,144,128]{2,1,0:T(8,128)(2,1)} %pack_blocks.2), calls=%async_computation.1 | async-start | bytes 2359296 | tf_op jit(solution)/shard_map/all_to_all | solution.py:495
  44.7 3.7 %copy-start.3 = (bf16[1,2,2048,1,128]{4,2,3,1,0:T(8,128)(2,1)S(1)}, bf16[1,2,2048,1,128]{4,2,3,1,0:T(8,128)(2,1)}, u32[]{:S(2)}) copy-start(bf16[1,2,2048,1,128]{4,2,3,1,0:T(8,128)(2,1)} %param.7) | copy-start | bytes 3145732
  44.8 14.4 %collective-permute-start.2 = (bf16[1536,128]{1,0:T(8,128)(2,1)S(1)}, bf16[1536,128]{1,0:T(8,128)(2,1)S(1)}, u32[]{:S(2)}, u32[]{:S(2)}) collective-permute-start(bf16[1536,128]{1,0:T(8,128)(2,1)S(1)} %bitcast.67), channel_id=1, source_target_pairs={{0,128},{128,0},{1,129},{129,1},{2,130},{130,2},{3,131},{131,3},{4... | collective-permute-start | bytes 1179656 | tf_op jit(solution)/shard_map/ppermute | solution.py:496
  54.7 14.4 %copy-start.5 = (bf16[1,2,2,1,128]{4,2,3,1,0:T(2,128)(2,1)S(1)}, bf16[1,2,2,1,128]{4,2,3,1,0:T(2,128)(2,1)}, u32[]{:S(2)}) copy-start(bf16[1,2,2,1,128]{4,2,3,1,0:T(2,128)(2,1)} %param.11) | copy-start | bytes 3076
  66.3 13.9 %collective-permute-start.3 = (bf16[1536,128]{1,0:T(8,128)(2,1)}, bf16[1536,128]{1,0:T(8,128)(2,1)}, u32[]{:S(2)}, u32[]{:S(2)}) collective-permute-start(bf16[1536,128]{1,0:T(8,128)(2,1)} %get-tuple-element.13), channel_id=1, source_target_pairs={{0,128},{128,0},{1,129},{129,1},{2,130},{130,2},{3,131},{131,3},{4... | collective-permute-start | bytes 1179656 | tf_op jit(solution)/shard_map/ppermute | solution.py:501
  69.2 11.0 %collective-permute-start.4 = (f32[64,128]{1,0:T(8,128)S(1)}, f32[64,128]{1,0:T(8,128)S(1)}, u32[]{:S(2)}, u32[]{:S(2)}) collective-permute-start(f32[64,128]{1,0:T(8,128)S(1)} %concatenate.6), channel_id=1, source_target_pairs={{0,128},{128,0},{1,129},{129,1},{2,130},{130,2},{3,131},{131,3},{4... | collective-permute-start | bytes 98312 | tf_op jit(solution)/shard_map/ppermute | solution.py:500
  83.9 1.0 copy-start
  84.9 30.0 %collective-permute-start.7 = (bf16[496,128]{1,0:T(8,128)(2,1)S(1)}, bf16[496,128]{1,0:T(8,128)(2,1)S(1)}, u32[]{:S(2)}, u32[]{:S(2)}) collective-permute-start(bf16[496,128]{1,0:T(8,128)(2,1)S(1)} %get-tuple-element.20), channel_id=1, source_target_pairs={{0,24},{8,16},{16,8},{24,0},{1,25},{9,17},{17,9},{25,1},{2,26},{10... | collective-permute-start | bytes 380936 | tf_op jit(solution)/shard_map/ppermute | solution.py:503
  89.4 25.4 %collective-permute-start.6 = (bf16[496,128]{1,0:T(8,128)(2,1)S(1)}, bf16[496,128]{1,0:T(8,128)(2,1)S(1)}, u32[]{:S(2)}, u32[]{:S(2)}) collective-permute-start(bf16[496,128]{1,0:T(8,128)(2,1)S(1)} %get-tuple-element.21), channel_id=1, source_target_pairs={{0,16},{8,24},{16,0},{24,8},{1,17},{9,25},{17,1},{25,9},{2,18},{10... | collective-permute-start | bytes 380936 | tf_op jit(solution)/shard_map/ppermute | solution.py:503
  92.3 22.6 %collective-permute-start.5 = (bf16[496,128]{1,0:T(8,128)(2,1)S(1)}, bf16[496,128]{1,0:T(8,128)(2,1)S(1)}, u32[]{:S(2)}, u32[]{:S(2)}) collective-permute-start(bf16[496,128]{1,0:T(8,128)(2,1)S(1)} %get-tuple-element.22), channel_id=1, source_target_pairs={{0,8},{8,0},{16,24},{24,16},{1,9},{9,1},{17,25},{25,17},{2,10},{10... | collective-permute-start | bytes 380936 | tf_op jit(solution)/shard_map/ppermute | solution.py:503
  102.4 64.2 %all-to-all-start.2 = ((bf16[32,112,128]{2,1,0:T(8,128)(2,1)}), bf16[32,112,128]{2,1,0:T(8,128)(2,1)S(1)}, u32[]{:S(2)}, u32[]{:S(2)}) async-start(bf16[32,112,128]{2,1,0:T(8,128)(2,1)} %after.1), calls=%async_computation.2 | async-start | bytes 1835008 | tf_op jit(solution)/shard_map/all_to_all | solution.py:505
  116.0 54.2 %collective-permute-start.10 = (bf16[208,128]{1,0:T(8,128)(2,1)S(1)}, bf16[208,128]{1,0:T(8,128)(2,1)S(1)}, u32[]{:S(2)}, u32[]{:S(2)}) collective-permute-start(bf16[208,128]{1,0:T(8,128)(2,1)S(1)} %get-tuple-element.26), channel_id=1, source_target_pairs={{0,96},{32,64},{64,32},{96,0},{1,97},{33,65},{65,33},{97,1},{2,98}... | collective-permute-start | bytes 159752 | tf_op jit(solution)/shard_map/ppermute | solution.py:507
  122.4 47.7 %collective-permute-start.9 = (bf16[208,128]{1,0:T(8,128)(2,1)S(1)}, bf16[208,128]{1,0:T(8,128)(2,1)S(1)}, u32[]{:S(2)}, u32[]{:S(2)}) collective-permute-start(bf16[208,128]{1,0:T(8,128)(2,1)S(1)} %get-tuple-element.27), channel_id=1, source_target_pairs={{0,64},{32,96},{64,0},{96,32},{1,65},{33,97},{65,1},{97,33},{2,66}... | collective-permute-start | bytes 159752 | tf_op jit(solution)/shard_map/ppermute | solution.py:507
  130.5 39.6 %collective-permute-start.8 = (bf16[208,128]{1,0:T(8,128)(2,1)S(1)}, bf16[208,128]{1,0:T(8,128)(2,1)S(1)}, u32[]{:S(2)}, u32[]{:S(2)}) collective-permute-start(bf16[208,128]{1,0:T(8,128)(2,1)S(1)} %get-tuple-element.28), channel_id=1, source_target_pairs={{0,32},{32,0},{64,96},{96,64},{1,33},{33,1},{65,97},{97,65},{2,34}... | collective-permute-start | bytes 159752 | tf_op jit(solution)/shard_map/ppermute | solution.py:507
  171.6 0.6 copy-start.4
